TPU v7x, 32 devices: a whole 2x2x4 slice. The times are simulated.
32 devices in a mesh: dp: 4 (over y, core), pipe: 4 (over z), ctx: 2 (over x).
Axes of the slice: x: 2, y: 2, z: 4, core: 2. Of those that a mesh axis runs over, the one named last changes fastest.
Arguments:
- acts: bfloat16 [4, 4, 4, 544, 8192], P('dp', 'pipe', None, 'ctx'), may hold values from -0.25 to 0.25
- key_grads: bfloat16 [4, 4, 4, 544, 512], P('dp', 'pipe', None, 'ctx'), may hold values from -6 to 6
- weights: bfloat16 [4, 8192, 512], P('pipe', 'ctx'), may hold values from -0.25 to 0.25
- b_slot: int32 [4], P('pipe'), may hold values from 0 to 3
- cycle: int32 [8], replicated, may hold values from 0 to 7, each once
Outputs:
- passed_grad: bfloat16 [4, 4, 544, 8192], P('dp', 'pipe', 'ctx')
- weight_grad: float32 [4, 8192, 512], P('pipe', 'ctx')
Inputs may be any that keep to these rules, and one draw needn't show every extreme that they name: `cycle`: each value once.
All inputs are finite; a program needn't handle non-finite values.
Results may differ from a plain program's by a relative error of at most 0.001.
Values may be sent and summed in bfloat16 or wider, within the bound.
No kernel may reach another device: no remote copies, remote signals or barrier semaphores. Data moves between devices by JAX's collectives and lax.ppermute only.
A program may use at most 192 MiB of HBM per device.

v0:
```python
import jax
import jax.numpy as jnp
from jax import lax
from jax.sharding import PartitionSpec as P


def passed_along(value, axis, by):
    count = lax.axis_size(axis)
    pairs = [(i, i + by) for i in range(count) if 0 <= i + by < count]
    return lax.ppermute(value, axis, pairs)


def key_product(left, right):
    return lax.dot_general(
        left, right, (((1,), (1,)), ((), ())), preferred_element_type=jnp.float32
    )


def token_product(left, right):
    return lax.dot_general(
        left, right, (((0,), (0,)), ((), ())), preferred_element_type=jnp.float32
    )


def body(acts, key_grads, weights, b_slot, cycle):
    stored = acts[0, 0]
    key_store = key_grads[0, 0]
    weight_local = weights[0]
    slot_index = b_slot[0]
    micro_count = stored.shape[0]
    row_count = stored.shape[1]
    feature_total = stored.shape[2]
    key_width = key_store.shape[2]
    piece_count = cycle.shape[0]
    current = lax.dynamic_index_in_dim(key_store, slot_index, 0, keepdims=False)
    section_grad = key_product(
        current, lax.all_gather(weight_local, "ctx", axis=0, tiled=True)
    ).astype(jnp.bfloat16)
    passed_grad = passed_along(section_grad, "pipe", -1)
    position = jnp.arange(micro_count - 1, dtype=jnp.int32)
    picked = position + (position >= slot_index).astype(jnp.int32)
    chosen_acts = jnp.take(stored, picked, axis=0)
    chosen_grads = jnp.take(key_store, picked, axis=0).reshape(-1, key_width)
    ordered = jnp.take(
        chosen_acts.reshape(micro_count - 1, row_count, piece_count, feature_total // piece_count),
        cycle,
        axis=2,
    ).reshape(micro_count - 1, row_count, feature_total)
    blocked = ordered.reshape(-1, feature_total)
    owned_rows = lax.psum_scatter(
        token_product(blocked, chosen_grads), "ctx", scatter_dimension=0, tiled=True
    )
    summed = lax.psum(owned_rows, "dp")
    return (passed_grad[None, None], summed[None])


def solution(mesh):
    placed = (
        P("dp", "pipe", None, "ctx", None),
        P("dp", "pipe", None, "ctx", None),
        P("pipe", "ctx", None),
        P("pipe"),
        P(),
    )
    return jax.shard_map(
        body,
        mesh=mesh,
        in_specs=placed,
        out_specs=(P("dp", "pipe", "ctx", None), P("pipe", "ctx", None)),
        check_vma=False,
    )
```

profile of v0, /device:TPU:0, one launch (start us, length us, event | category | flops | bytes accessed | tf_op | source)
XLA Modules:
  0.0 488.8 jit_solution(3746948877405926802)
XLA Ops:
  7.2 0.0 copy-start
  7.2 0.0 all-gather.3.cloned.1.call-start
  7.2 0.7 all-gather.3.cloned.1.call-update
  7.9 0.0 reduce-scatter.2.cloned.1.call-start
  8.6 5.4 %mini-gather-slice.5 = bf16[4,272,2560]{2,1,0:T(8,128)(2,1)} slice(bf16[4,272,8192]{2,1,0:T(8,128)(2,1)} %bitcast.32), slice={[0:4], [0:272], [5632:8192]} | slice | bytes 11141120 | tf_op jit(solution)/shard_map/jit(_take)/gather | solution.py:42
  14.0 11.4 %fusion.7 = (bf16[4,272,2816]{2,1,0:T(8,128)(2,1)}, bf16[4,272,2816]{2,1,0:T(8,128)(2,1)}) fusion(bf16[4,272,8192]{2,1,0:T(8,128)(2,1)} %bitcast.33), kind=kLoop, calls=%fused_computation.26 | loop fusion | bytes 24510464 | tf_op jit(solution)/shard_map/jit(_take)/gather | solution.py:42
  25.4 6.3 %gather_fusion.2 = bf16[3,272,2816]{2,1,0:T(8,128)(2,1)} fusion(bf16[4,272,2816]{2,1,0:T(8,128)(2,1)} %get-tuple-element.2, s32[1024]{0:T(1024)S(1)} %pad_clamp_fusion.1), kind=kCustom, calls=%fused_computation.2 | custom fusion | bytes 9191436 | tf_op jit(solution)/shard_map/jit(_take)/gather | solution.py:42
  31.8 0.0 copy-start.2
  31.8 5.9 %gather_fusion.3 = bf16[3,272,2816]{2,1,0:T(8,128)(2,1)} fusion(bf16[4,272,2816]{2,1,0:T(8,128)(2,1)} %get-tuple-element.3, s32[1024]{0:T(1024)S(1)} %pad_clamp_fusion.1), kind=kCustom, calls=%fused_computation.3 | custom fusion | bytes 9191436 | tf_op jit(solution)/shard_map/jit(_take)/gather | solution.py:42
  37.6 5.5 %gather_fusion.4 = bf16[3,272,2560]{2,1,0:T(8,128)(2,1)} fusion(bf16[4,272,2560]{2,1,0:T(8,128)(2,1)} %mini-gather-slice.5, s32[1024]{0:T(1024)S(1)} %pad_clamp_fusion.1), kind=kCustom, calls=%fused_computation.4 | custom fusion | bytes 8355852 | tf_op jit(solution)/shard_map/jit(_take)/gather | solution.py:42
  43.2 0.0 copy-done.2
  43.2 6.4 %pad_maximum_fusion = bf16[3,272,8192]{2,1,0:T(8,128)(2,1)S(1)} fusion(bf16[3,272,2560]{2,1,0:T(8,128)(2,1)} %gather_fusion.4, bf16[3,272,2816]{2,1,0:T(8,128)(2,1)} %gather_fusion.3, bf16[3,272,2816]{2,1,0:T(8,128)(2,1)} %gather_fusion.2), kind=kLoop, calls=%fused_computation.6 | loop fusion | flops 40108032 | bytes 26738688
  49.6 5.7 %bitcast_select_fusion = bf16[3,272,8,1024]{3,1,0,2:T(8,128)(2,1)} fusion(bf16[3,34,8,8,1024]{4,3,2,1,0:T(8,128)(2,1)S(1)} %bitcast.30, pred[3]{0:T(512)(128)(4,1)S(1)} %compare_and_fusion), kind=kLoop, calls=%fused_computation.5 | loop fusion | flops 6684672 | bytes 26738692 | tf_op jit(solution)/shard_map/jit(_take)/select_n | solution.py:42
  55.3 11.6 %gather_fusion = bf16[8,3,272,1024]{3,2,1,0:T(8,128)(2,1)} fusion(bf16[3,272,8,1024]{3,1,0,2:T(8,128)(2,1)} %bitcast_select_fusion, s32[1024]{0:T(1024)S(1)} %pad_clamp_fusion), kind=kCustom, calls=%fused_computation | custom fusion | bytes 26738720 | tf_op jit(solution)/shard_map/jit(_take)/gather | solution.py:44
  66.9 6.8 %select_bitcast_fusion = bf16[3,272,8,1024]{3,1,0,2:T(8,128)(2,1)S(1)} fusion(bf16[8,3,272,1024]{3,2,1,0:T(8,128)(2,1)} %gather_fusion, pred[8]{0:T(512)(128)(4,1)S(1)} %compare_and_fusion.1), kind=kLoop, calls=%fused_computation.7 | loop fusion | flops 6684672 | bytes 26738696 | tf_op jit(solution)/shard_map/jit(_take)/select_n | solution.py:44
  73.6 23.3 %copy.8 = bf16[3,272,8,1024]{3,2,1,0:T(8,128)(2,1)S(1)} copy(bf16[3,272,8,1024]{3,1,0,2:T(8,128)(2,1)S(1)} %select_bitcast_fusion) | data formatting | bytes 26738688 | tf_op jit(solution)/shard_map/jit(_take)/select_n | solution.py:44
  96.9 11.6 %copy.10 = bf16[102,8,8,1024]{3,1,2,0:T(8,128)(2,1)} copy(bf16[102,8,8,1024]{3,2,1,0:T(8,128)(2,1)S(1)} %bitcast.31) | data formatting | bytes 26738688
  108.6 0.0 copy-done
  108.6 0.6 gather_fusion.1
  109.2 0.1 broadcast_select_fusion
  109.3 15.3 %fusion.8 = f32[8192,512]{1,0:T(8,128)} fusion(bf16[816,8192]{1,0:T(8,128)(2,1)} %bitcast.34, bf16[816,512]{1,0:T(8,128)(2,1)S(1)} %bitcast.36), kind=kOutput, calls=%fused_computation.27 | convolution fusion | flops 6845104128 | bytes 30982144 | tf_op jit(solution)/shard_map/dot_general | solution.py:20
  124.7 0.0 reduce-scatter.2.cloned.1.call-update
  124.7 0.2 all-reduce.2.cloned.1.call-start
  124.9 0.0 all-gather.3.cloned.1.call-done
  125.0 8.0 %convolution_convert_fusion = bf16[272,8192]{1,0:T(8,128)(2,1)} fusion(bf16[1,8192,512]{2,1,0:T(8,128)(2,1)} %all-gather.3.cloned.1.call-done, bf16[1,1,4,272,512]{4,3,2,1,0:T(8,128)(2,1)S(1)} %copy-done, s32[]{:T(128)S(6)} %select_n.60), kind=kOutput, calls=%fused_computation.8 | convolution fusion | flops 2283929600 | bytes 13123588 | tf_op jit(solution)/shard_map/dot_general | solution.py:14
  133.0 1.3 collective-permute-start
  134.2 182.8 %reduce-scatter.2.cloned.1.call-done = f32[4096,512]{1,0:T(8,128)} async-done(((f32[8192,512]{1,0:T(8,128)}), f32[4096,512]{1,0:T(8,128)}) %reduce-scatter.2.cloned.1.call-update) | async-done | bytes 8388624 | tf_op jit(solution)/shard_map/reduce_scatter | solution.py:50
  317.1 0.0 all-reduce.2.cloned.1.call-update
  317.1 0.0 collective-permute-done
  317.1 155.5 %all-reduce.2.cloned.1.call-done = f32[1,4096,512]{2,1,0:T(8,128)} async-done(((f32[1,4096,512]{2,1,0:T(8,128)}), f32[1,4096,512]{2,1,0:T(8,128)}) %all-reduce.2.cloned.1.call-update) | async-done | bytes 8388624 | tf_op jit(solution)/shard_map/psum | solution.py:53
  472.6 0.0 copy-start.1
  472.6 5.2 %copy.15 = bf16[1,1,272,8192]{3,2,1,0:T(8,128)(2,1)} copy(bf16[1,1,272,8192]{3,2,1,0:T(8,128)(2,1)} %bitcast.3) | data formatting | bytes 8912896
  477.7 1.2 copy-done.1
  478.9 3.4 copy.16
  (6 shorter events, 0.0 us)
Async XLA Ops:
  7.2 101.4 %copy-start = (bf16[1,1,4,272,512]{4,3,2,1,0:T(8,128)(2,1)S(1)}, bf16[1,1,4,272,512]{4,3,2,1,0:T(8,128)(2,1)}, u32[]{:S(2)}) copy-start(bf16[1,1,4,272,512]{4,3,2,1,0:T(8,128)(2,1)} %param.6) | copy-start | bytes 3342340
  7.2 117.8 %all-gather.3.cloned.1.call-start = ((), (), s32[]{:S(2)}) async-start(), calls=%async_computation.3 | async-start | bytes 12582912 | tf_op jit(solution)/shard_map/all_gather | solution.py:37
  7.9 309.2 %reduce-scatter.2.cloned.1.call-start = ((), (), s32[]{:S(2)}) async-start(), calls=%async_computation.1 | async-start | bytes 25165824 | tf_op jit(solution)/shard_map/reduce_scatter | solution.py:50
  31.8 11.4 %copy-start.2 = (s32[8]{0:T(128)S(1)}, s32[8]{0:T(128)}, u32[]{:S(2)}) copy-start(s32[8]{0:T(128)} %param.9) | copy-start | bytes 100
  124.7 347.9 %all-reduce.2.cloned.1.call-start = ((), (), s32[]{:S(2)}) async-start(), calls=%async_computation.2 | async-start | bytes 16777216 | tf_op jit(solution)/shard_map/psum | solution.py:53
  133.0 184.1 %collective-permute-start = (bf16[272,8192]{1,0:T(8,128)(2,1)}, bf16[272,8192]{1,0:T(8,128)(2,1)}, u32[]{:S(2)}, u32[]{:S(2)}) collective-permute-start(bf16[272,8192]{1,0:T(8,128)(2,1)} %convolution_convert_fusion), channel_id=1, source_target_pairs={{2,0},{4,2},{6,4},{3,1},{5,3},{7,5},{10,8},{12,10},{14,12},{11,9},... | collective-permute-start | bytes 13369352 | tf_op jit(solution)/shard_map/ppermute | solution.py:10
  472.6 6.3 %copy-start.1 = (f32[1,4096,512]{2,1,0:T(8,128)S(1)}, f32[1,4096,512]{2,1,0:T(8,128)}, u32[]{:S(2)}) copy-start(f32[1,4096,512]{2,1,0:T(8,128)} %all-reduce.2.cloned.1.call-done) | copy-start | bytes 25165828
Sparse Core Ops, SparseCore 0:
  9.6 106.6 all-gather.2
  124.8 192.2 reduce-scatter.1
  319.7 152.8 all-reduce.1
where the time goes:
time: 489 us
  waiting for transfers between devices  339 us (69%)
  local copies, waits for them, and re-layouts  91.4 us (19%)
  matrix products  23.3 us (5%)
  other arithmetic  19 us (4%)
  between operations  14.5 us (3%)
    reduce_scatter x1, waiting for transfers between devices, body(): lax.psum_scatter(token_product(blocked, chosen_grads), 'ctx', scatter_dim...  183 us
    psum x1, waiting for transfers between devices, body(): summed = lax.psum(owned_rows, 'dp')  155 us
    gather x5, local copies, waits for them, and re-layouts, body(): chosen_acts = jnp.take(stored, picked, axis=0)  34.5 us
    select_n x1, local copies, waits for them, and re-layouts, body(): jnp.take(chosen_acts.reshape(micro_count - 1, row_count, piece_count, fea...  23.3 us
    unnamed x9, local copies, waits for them, and re-layouts  21.4 us
    dot_general x1, matrix products, token_product(): lax.dot_general(left, right, (((0,), (0,)), ((), ())), preferred_element_...  15.3 us
    gather x1, local copies, waits for them, and re-layouts, body(): jnp.take(chosen_acts.reshape(micro_count - 1, row_count, piece_count, fea...  11.6 us
  transfers between devices with their start and end apart: 4, of which 2 were waited for; matrix products, arithmetic and copies ran while one was open for 25% of the time, Pallas kernels for 0%

commit v1 on v0

v1 whole, which is shorter than its diff:
```python
import functools

import jax
import jax.numpy as jnp
from jax import lax
from jax.experimental import pallas as pl
from jax.experimental.pallas import tpu as pltpu
from jax.sharding import PartitionSpec as P

LANES = 128
TAIL = 16
INNER = 2
TOP = 32767.0
VMEM_LIMIT = 48 << 20


def params():
    return pltpu.CompilerParams(vmem_limit_bytes=VMEM_LIMIT)


def code_shape(rows, width):
    return jax.ShapeDtypeStruct((width // LANES * rows + TAIL, LANES), jnp.int16)


def scale_of(code_ref, count):
    exponent = code_ref[count : count + TAIL, :].astype(jnp.int32)[0:1, :].astype(jnp.float32)
    return jnp.exp2(exponent) * (1.0 / (TOP * TOP))


def decoded(code_ref, start, rows, scale):
    level = code_ref[pl.ds(start, rows), :].astype(jnp.int32).astype(jnp.float32)
    return level * jnp.abs(level) * scale


def combine_kernel(*refs, n_sums, n_codes, rows, width):
    sums = refs[:n_sums]
    codes = refs[n_sums : n_sums + n_codes]
    out_ref = refs[n_sums + n_codes]
    total_ref = refs[n_sums + n_codes + 1]
    slabs = width // LANES
    step = min(rows, 128)
    scales = [scale_of(c, slabs * rows) for c in codes]

    def add(i, largest):
        r = pl.multiple_of(i * step, step)
        for j in range(slabs):
            value = sums[0][0, pl.ds(r, step), j * LANES : (j + 1) * LANES]
            for s in sums[1:]:
                value = value + s[0, pl.ds(r, step), j * LANES : (j + 1) * LANES]
            for c, scale in zip(codes, scales):
                value = value + decoded(c, pl.multiple_of(j * rows + r, step), step, scale)
            total_ref[pl.ds(r, step), j * LANES : (j + 1) * LANES] = value
            folded = jnp.abs(value).reshape(step // 8, 8, LANES)
            largest = jnp.maximum(largest, jnp.max(folded, axis=0))
        return largest

    largest = lax.fori_loop(0, rows // step, add, jnp.zeros((8, LANES), jnp.float32))
    largest = jnp.max(jnp.max(largest, axis=0, keepdims=True), axis=1, keepdims=True)
    exponent = jnp.floor(jnp.log2(jnp.maximum(largest, 1e-30))) + 2.0
    exponent = jnp.broadcast_to(exponent, (8, LANES))
    shrink = jnp.exp2(-exponent)[0:1, :]

    def encode(i, carry):
        r = pl.multiple_of(i * step, step)
        for j in range(slabs):
            value = total_ref[pl.ds(r, step), j * LANES : (j + 1) * LANES]
            root = jnp.round(jnp.sqrt(jnp.abs(value) * shrink) * TOP)
            level = jnp.where(value < 0.0, -root, root)
            place = pl.ds(pl.multiple_of(j * rows + r, step), step)
            out_ref[place, :] = level.astype(jnp.int32).astype(jnp.int16)
        return carry

    lax.fori_loop(0, rows // step, encode, 0)
    tail = jnp.concatenate([exponent] * (TAIL // 8), axis=0)
    out_ref[slabs * rows : slabs * rows + TAIL, :] = tail.astype(jnp.int32).astype(jnp.int16)


def combine(sums, codes, rows, width):
    shape = code_shape(rows, width)
    in_specs = [
        pl.BlockSpec((1, rows, width), functools.partial(lambda at, i: (at, 0, 0), at)) for _, at in sums
    ] + [pl.BlockSpec(shape.shape, lambda i: (0, 0)) for _ in codes]
    return pl.pallas_call(
        functools.partial(combine_kernel, n_sums=len(sums), n_codes=len(codes), rows=rows, width=width),
        out_shape=shape,
        grid=(1,),
        in_specs=in_specs,
        out_specs=pl.BlockSpec(shape.shape, lambda i: (0, 0)),
        scratch_shapes=[pltpu.VMEM((rows, width), jnp.float32)],
        compiler_params=params(),
        cost_estimate=pl.CostEstimate(
            flops=20 * rows * width,
            bytes_accessed=rows * width * (4 * len(sums) + 2 * len(codes) + 2),
            transcendentals=0,
        ),
    )(*[a for a, _ in sums], *codes)


def token_kernel(order, picks, *refs, count):
    left = jnp.concatenate([r[0] for r in refs[:count]], axis=0)
    right = jnp.concatenate([r[0] for r in refs[count : 2 * count]], axis=0)
    refs[2 * count][0] = lax.dot_general(
        left, right, (((0,), (0,)), ((), ())), preferred_element_type=jnp.float32
    )


def token_products(order, picks, acts, grads, block, rows):
    steps = order.shape[0]
    count = picks.shape[0]
    tokens = acts.shape[1]
    width = grads.shape[2]
    in_specs = [
        pl.BlockSpec((1, tokens, block), functools.partial(lambda m, g, o, p: (p[m], 0, o[g]), m))
        for m in range(count)
    ] + [
        pl.BlockSpec((1, tokens, width), functools.partial(lambda m, g, o, p: (p[m], 0, 0), m))
        for m in range(count)
    ]
    out = pl.pallas_call(
        functools.partial(token_kernel, count=count),
        out_shape=jax.ShapeDtypeStruct((steps, block, width), jnp.float32),
        grid_spec=pltpu.PrefetchScalarGridSpec(
            num_scalar_prefetch=2,
            grid=(steps,),
            in_specs=in_specs,
            out_specs=pl.BlockSpec((1, block, width), lambda g, o, p: (g, 0, 0)),
        ),
        compiler_params=params(),
        cost_estimate=pl.CostEstimate(
            flops=2 * steps * block * width * count * tokens,
            bytes_accessed=steps * block * (count * tokens * 2 + width * 4),
            transcendentals=0,
        ),
    )(order, picks, *([acts] * count), *([grads] * count))
    return out.reshape(steps * block // rows, rows, width)


def key_kernel(place, current_ref, *refs, count):
    out_ref = refs[-1]
    for n in range(count):

        @pl.when(pl.program_id(0) == n)
        def _():
            out_ref[...] = lax.dot_general(
                current_ref[...], refs[n][...], (((1,), (1,)), ((), ())), preferred_element_type=jnp.float32
            ).astype(out_ref.dtype)


def key_products(place, current, parts, features, held):
    tokens, width = current.shape
    rows = parts[0].shape[0]
    count = len(parts)
    in_specs = [pl.BlockSpec((tokens, width), lambda g, p: (0, 0))] + [
        pl.BlockSpec((rows, width), lambda g, p: (0, 0)) for _ in parts
    ]
    operands = [place, current, *parts]
    aliases = {}
    if held is not None:
        in_specs.append(pl.BlockSpec(memory_space=pl.ANY))
        aliases = {len(operands): 0}
        operands.append(held)
    return pl.pallas_call(
        functools.partial(key_kernel, count=count),
        out_shape=jax.ShapeDtypeStruct((tokens, features), jnp.bfloat16),
        grid_spec=pltpu.PrefetchScalarGridSpec(
            num_scalar_prefetch=1,
            grid=(count,),
            in_specs=in_specs,
            out_specs=pl.BlockSpec((tokens, rows), lambda g, p: (0, p[g])),
        ),
        input_output_aliases=aliases,
        compiler_params=params(),
        cost_estimate=pl.CostEstimate(
            flops=2 * count * rows * width * tokens,
            bytes_accessed=2 * count * rows * (width + tokens),
            transcendentals=0,
        ),
    )(*operands)


def decode_kernel(place, *refs, count, rows, width, block):
    out_ref = refs[-1]
    slabs = width // LANES
    start = pl.multiple_of(pl.program_id(1) * block, block)
    for n in range(count):

        @pl.when(pl.program_id(0) == n)
        def _():
            scale = scale_of(refs[n], slabs * rows)
            for j in range(slabs):
                out_ref[0, :, j * LANES : (j + 1) * LANES] = decoded(
                    refs[n], pl.multiple_of(j * rows + start, block), block, scale
                )


def decode(place, codes, blocks, rows, width, held):
    count = len(codes)
    block = min(rows, 512)
    shape = code_shape(rows, width).shape
    in_specs = [pl.BlockSpec(shape, lambda g, s, p: (0, 0)) for _ in codes]
    operands = [place, *codes]
    aliases = {}
    if held is not None:
        in_specs.append(pl.BlockSpec(memory_space=pl.ANY))
        aliases = {len(operands): 0}
        operands.append(held)
    return pl.pallas_call(
        functools.partial(decode_kernel, count=count, rows=rows, width=width, block=block),
        out_shape=jax.ShapeDtypeStruct((blocks, rows, width), jnp.float32),
        grid_spec=pltpu.PrefetchScalarGridSpec(
            num_scalar_prefetch=1,
            grid=(count, rows // block),
            in_specs=in_specs,
            out_specs=pl.BlockSpec((1, block, width), lambda g, s, p: (p[g], s, 0)),
        ),
        input_output_aliases=aliases,
        compiler_params=params(),
        cost_estimate=pl.CostEstimate(
            flops=4 * count * rows * width, bytes_accessed=6 * count * rows * width, transcendentals=0
        ),
    )(*operands)


def body(acts, key_grads, weights, b_slot, cycle):
    stored, grads, weight = acts[0, 0], key_grads[0, 0], weights[0]
    slot = b_slot[0]
    micro, tokens, features = stored.shape
    width = grads.shape[2]
    n_dp, n_ctx = lax.axis_size("dp"), lax.axis_size("ctx")
    n_pipe = lax.axis_size("pipe")
    outer = n_dp // INNER
    replica, section = lax.axis_index("dp"), lax.axis_index("ctx")
    me_o, me_i = replica // INNER, replica % INNER
    groups = n_dp * n_ctx
    rows = features // groups
    pieces = cycle.shape[0]

    def swap(value):
        pairs = [(d, d // INNER * INNER + (d + 1) % INNER) for d in range(n_dp)]
        return lax.ppermute(value, "dp", pairs)

    def to_outer(value, by):
        return lax.ppermute(value, "dp", [(d, (d + by * INNER) % n_dp) for d in range(n_dp)])

    def to_ctx(value, by):
        return lax.ppermute(value, "ctx", [(d, (d + by) % n_ctx) for d in range(n_ctx)])

    def to_previous(value):
        return lax.ppermute(value, "pipe", [(d, d - 1) for d in range(1, n_pipe)])

    current = to_previous(lax.dynamic_index_in_dim(grads, slot, 0, keepdims=False))
    cuts = 2
    part = weight.shape[0] // (INNER * cuts)
    sent = [
        to_previous(lax.dynamic_slice_in_dim(weight, (me_i * cuts + c) * part, part, 0)) for c in range(cuts)
    ]

    position = jnp.arange(micro - 1, dtype=jnp.int32)
    picks = position + (position >= slot).astype(jnp.int32)
    block = min(rows, features // pieces, 512)
    piece_blocks = features // pieces // block
    blocks_of = rows // block

    def order_of(wanted):
        ids = []
        for kx, ko, ki in wanted:
            owner = ((section + kx) % n_ctx) * n_dp + ((me_o + ko) % outer) * INNER + (me_i + ki) % INNER
            at = owner * blocks_of + jnp.arange(blocks_of, dtype=jnp.int32)
            ids.append(cycle[at // piece_blocks] * piece_blocks + at % piece_blocks)
        return jnp.concatenate(ids)

    def products(wanted):
        return token_products(order_of(wanted), picks, stored, grads, block, rows)

    far = [(kx, ko) for ko in range(1, outer) for kx in range(1, n_ctx)]
    near = [(0, ko) for ko in range(1, outer)]
    home = [(kx, 0) for kx in range(n_ctx)]
    terms = {}
    for wanted in (far, near, home):
        theirs = swap(products([(*w, 1) for w in wanted]))
        mine = products([(*w, 0) for w in wanted])
        for n, w in enumerate(wanted):
            terms[w] = [(mine, n), (theirs, n)]

    got = {}
    for kx, ko in far + near:
        got[kx, ko] = to_outer(combine(terms[kx, ko], [], rows, width), ko)
    crossed = []
    for kx in range(1, n_ctx):
        value = combine(terms[kx, 0], [got[kx, ko] for ko in range(1, outer)], rows, width)
        crossed.append(to_ctx(value, kx))
    own = combine(terms[0, 0], [got[0, ko] for ko in range(1, outer)] + crossed, rows, width)
    result = decode(
        jnp.stack([me_o * INNER + me_i, me_o * INNER + (me_i + 1) % INNER]), [own, swap(own)], n_dp, rows, width, None
    )
    for ko in range(1, outer):
        other = to_outer(own, ko)
        o = (me_o - ko) % outer
        place = jnp.stack([o * INNER + me_i, o * INNER + (me_i + 1) % INNER])
        result = decode(place, [other, swap(other)], n_dp, rows, width, result)

    passed = None
    for kx in range(n_ctx):
        for c in range(cuts):
            held = sent[c] if kx == 0 else to_ctx(sent[c], kx)
            source = (section - kx) % n_ctx
            place = jnp.stack(
                [(source * INNER + me_i) * cuts + c, (source * INNER + (me_i + 1) % INNER) * cuts + c]
            )
            passed = key_products(place, current, [held, swap(held)], features, passed)
    return passed[None, None], result.reshape(1, n_dp * rows, width)


def solution(mesh):
    placed = (
        P("dp", "pipe", None, "ctx", None),
        P("dp", "pipe", None, "ctx", None),
        P("pipe", "ctx", None),
        P("pipe"),
        P(),
    )
    return jax.shard_map(
        body,
        mesh=mesh,
        in_specs=placed,
        out_specs=(P("dp", "pipe", "ctx", None), P("pipe", "ctx", None)),
        check_vma=False,
    )
```

time: 489 us -> 157 us (0.32)
  waiting for transfers between devices: 339 us -> 63.3 us
  local copies, waits for them, and re-layouts: 91.4 us -> 9.87 us
  Pallas kernels: 0 us -> 66.8 us
  matrix products: 23.3 us -> 0 us
  other arithmetic: 19 us -> 0.75 us
  between operations: 14.5 us -> 1.63 us
  starting transfers between devices: 1.58 us -> 14 us
    reduce_scatter x1 -> x0, waiting for transfers between devices: 183 us -> none  [body(): lax.psum_scatter(token_product(blocked, chosen_grads), 'ctx', scatter_dim...]
    psum x1 -> x0, waiting for transfers between devices: 155 us -> none  [body(): summed = lax.psum(owned_rows, 'dp')]
    pallas_call x0 -> x16, Pallas kernels: none -> 66.8 us  [the longest x6 25.6 us: token_products(): pl.pallas_call(functools.partial(token_kernel, count=count), out_shape=ja...]
    ppermute x1 -> x18, waiting for transfers between devices: 0.01 us -> 63.3 us  [the longest x3 29.9 us: to_previous(): return lax.ppermute(value, 'pipe', [(d, d - 1) for d in range(1, n_pipe)])]
    gather x7 -> x8, local copies, waits for them, and re-layouts: 46.7 us -> 5.11 us  [order_of(): ids.append(cycle[at // piece_blocks] * piece_blocks + at % piece_blocks)]
    dot_general x2 -> x0, matrix products: 23.3 us -> none  [the longest x1 15.3 us: token_product(): lax.dot_general(left, right, (((0,), (0,)), ((), ())), preferred_element_...]
    select_n x1 -> x0, local copies, waits for them, and re-layouts: 23.3 us -> none  [body(): jnp.take(chosen_acts.reshape(micro_count - 1, row_count, piece_count, fea...]
    unnamed x9 -> x12, local copies, waits for them, and re-layouts: 21.4 us -> 3.28 us
  transfers between devices with their start and end apart: 4 -> 18, of which waited for: 2 -> 6; matrix products, arithmetic and copies ran while one was open for 25% -> 4% of each run, Pallas kernels for 0% -> 36%
where the time goes in v1:
time: 157 us; the launch traced here: 156 us
  Pallas kernels  66.8 us (43%)
  waiting for transfers between devices  63.3 us (40%)
  starting transfers between devices  14 us (9%)
  local copies, waits for them, and re-layouts  9.87 us (6%)
  between operations  1.63 us (1%)
    ppermute x3, waiting for transfers between devices, to_previous(): return lax.ppermute(value, 'pipe', [(d, d - 1) for d in range(1, n_pipe)])  29.9 us
    ppermute x3, waiting for transfers between devices, to_ctx(): lax.ppermute(value, 'ctx', [(d, (d + by) % n_ctx) for d in range(n_ctx)])  28.3 us
    pallas_call x6, Pallas kernels, token_products(): pl.pallas_call(functools.partial(token_kernel, count=count), out_shape=ja...  25.6 us
    pallas_call x4, Pallas kernels, combine(): pl.pallas_call(functools.partial(combine_kernel, n_sums=len(sums), n_code...  16.6 us
    pallas_call x4, Pallas kernels, key_products(): pl.pallas_call(functools.partial(key_kernel, count=count), out_shape=jax....  15.6 us
    pallas_call x2, Pallas kernels, decode(): pl.pallas_call(functools.partial(decode_kernel, count=count, rows=rows, w...  8.96 us
    ppermute x3, waiting for transfers between devices, to_outer(): lax.ppermute(value, 'dp', [(d, (d + by * INNER) % n_dp) for d in range(n_...  5.15 us
    gather x8, local copies, waits for them, and re-layouts, order_of(): ids.append(cycle[at // piece_blocks] * piece_blocks + at % piece_blocks)  5.11 us
  transfers between devices with their start and end apart: 18, of which 6 were waited for; matrix products, arithmetic and copies ran while one was open for 4% of the time, Pallas kernels for 36%

profile of v1, /device:TPU:0, one launch (start us, length us, event | category | flops | bytes accessed | tf_op | source)
XLA Modules:
  0.0 156.4 jit_solution(10743201418033573148)
XLA Ops:
  0.6 0.0 copy-start
  1.5 0.6 gather_fusion.3
  2.1 0.6 gather_fusion.2
  2.8 0.1 pad_add_fusion.6.order
  2.8 1.2 copy-done.2
  4.1 6.5 %shard_map.73 = f32[4,512,512]{2,1,0:T(8,128)} custom-call(s32[4]{0:T(128)S(1)} %pad_add_fusion.6.order, s32[3]{0:T(128)S(1)} %fusion.8.picks, bf16[4,272,8192]{2,1,0:T(8,128)(2,1)} %bitcast.72, bf16[4,272,8192]{2,1,0:T(8,128)(2,1)} %bitcast.73, bf16[4,272,8192]{2,1,0:T(8,128)(2,1)} %bitcast.74, bf16[4,272,512]{2,1,0:T(8,128)(2,1)S(1)} %bitcast.49, ...), custom_call_target="tpu_custom_call" | custom-call | flops 1711276032 | bytes 7536640 | tf_op jit(solution)/shard_map/pallas_call | solution.py:119
  10.6 0.5 collective-permute-start.9
  11.1 0.6 gather_fusion.6
  11.7 0.6 gather_fusion.7
  12.4 4.2 %shard_map.78 = f32[2,512,512]{2,1,0:T(8,128)} custom-call(s32[2]{0:T(128)S(1)} %get-tuple-element.11.order, s32[3]{0:T(128)S(1)} %fusion.8.picks, bf16[4,272,8192]{2,1,0:T(8,128)(2,1)} %bitcast.75, bf16[4,272,8192]{2,1,0:T(8,128)(2,1)} %bitcast.76, bf16[4,272,8192]{2,1,0:T(8,128)(2,1)} %bitcast.77, bf16[4,272,512]{2,1,0:T(8,128)(2,1)S(1)} %bitcast.52, ...), custom_call_target="tpu_custom_call" | custom-call | flops 855638016 | bytes 3768320 | tf_op jit(solution)/shard_map/pallas_call | solution.py:119
  16.6 0.1 collective-permute-start.12
  16.7 0.6 gather_fusion.4
  17.4 0.6 gather_fusion.5
  18.0 3.3 %shard_map.75 = f32[2,512,512]{2,1,0:T(8,128)S(1)} custom-call(s32[2]{0:T(128)S(1)} %get-tuple-element.9.order, s32[3]{0:T(128)S(1)} %fusion.8.picks, bf16[4,272,8192]{2,1,0:T(8,128)(2,1)} %bitcast.78, bf16[4,272,8192]{2,1,0:T(8,128)(2,1)} %bitcast.79, bf16[4,272,8192]{2,1,0:T(8,128)(2,1)} %bitcast.80, bf16[4,272,512]{2,1,0:T(8,128)(2,1)S(1)} %bitcast.55, ...), custom_call_target="tpu_custom_call" | custom-call | flops 855638016 | bytes 3768320 | tf_op jit(solution)/shard_map/pallas_call | solution.py:119
  21.3 0.5 collective-permute-start.10
  21.8 3.2 %shard_map.77 = f32[2,512,512]{2,1,0:T(8,128)S(1)} custom-call(s32[2]{0:T(128)S(1)} %get-tuple-element.10.order, s32[3]{0:T(128)S(1)} %fusion.8.picks, bf16[4,272,8192]{2,1,0:T(8,128)(2,1)} %bitcast.81, bf16[4,272,8192]{2,1,0:T(8,128)(2,1)} %bitcast.82, bf16[4,272,8192]{2,1,0:T(8,128)(2,1)} %bitcast.83, bf16[4,272,512]{2,1,0:T(8,128)(2,1)S(1)} %bitcast.58, ...), custom_call_target="tpu_custom_call" | custom-call | flops 855638016 | bytes 3768320 | tf_op jit(solution)/shard_map/pallas_call | solution.py:119
  25.0 0.0 collective-permute-done.12.refs_1_
  25.1 0.0 copy-start.5
  25.1 4.4 %shard_map.79 = s16[4112,128]{1,0:T(8,128)(2,1)} custom-call(f32[1,1024,512]{2,1,0:T(8,128)S(1)} %bitcast.70, f32[1,1024,512]{2,1,0:T(8,128)} %collective-permute-done.12.refs_1_), custom_call_target="tpu_custom_call" | custom-call | flops 10485760 | bytes 5242880 | tf_op jit(solution)/shard_map/pallas_call | solution.py:83
  29.5 2.6 %collective-permute-start.13 = (s16[4112,128]{1,0:T(8,128)(2,1)}, s16[4112,128]{1,0:T(8,128)(2,1)}, u32[]{:S(2)}, u32[]{:S(2)}) collective-permute-start(s16[4112,128]{1,0:T(8,128)(2,1)} %shard_map.79), channel_id=1, source_target_pairs={{0,16},{8,24},{16,0},{24,8},{1,17},{9,25},{17,1},{25,9},{2,18},{10... | collective-permute-start | bytes 3158024 | tf_op jit(solution)/shard_map/ppermute | solution.py:243
  32.0 1.5 dynamic-slice_bitcast_fusion
  33.5 1.3 collective-permute-start.4
  34.8 1.3 collective-permute-start.1
  36.1 0.6 gather_fusion.1
  36.8 0.6 gather_fusion
  37.4 0.1 pad_add_fusion.5.order
  37.5 5.2 %shard_map.72 = f32[4,512,512]{2,1,0:T(8,128)S(1)} custom-call(s32[4]{0:T(128)S(1)} %pad_add_fusion.5.order, s32[3]{0:T(128)S(1)} %fusion.8.picks, bf16[4,272,8192]{2,1,0:T(8,128)(2,1)} %bitcast.84, bf16[4,272,8192]{2,1,0:T(8,128)(2,1)} %bitcast.85, bf16[4,272,8192]{2,1,0:T(8,128)(2,1)} %bitcast.86, bf16[4,272,512]{2,1,0:T(8,128)(2,1)S(1)} %bitcast.61, ...), custom_call_target="tpu_custom_call" | custom-call | flops 1711276032 | bytes 7536640 | tf_op jit(solution)/shard_map/pallas_call | solution.py:119
  42.7 0.0 copy-start.4
  42.7 2.0 %copy-done.4 = f32[4,512,512]{2,1,0:T(8,128)} copy-done((f32[4,512,512]{2,1,0:T(8,128)}, f32[4,512,512]{2,1,0:T(8,128)S(1)}, u32[]{:S(2)}) %copy-start.4) | copy-done | bytes 4194328
  44.7 3.2 %shard_map.74 = f32[2,512,512]{2,1,0:T(8,128)S(1)} custom-call(s32[2]{0:T(128)S(1)} %get-tuple-element.8.order, s32[3]{0:T(128)S(1)} %fusion.8.picks, bf16[4,272,8192]{2,1,0:T(8,128)(2,1)} %bitcast.87, bf16[4,272,8192]{2,1,0:T(8,128)(2,1)} %bitcast.88, bf16[4,272,8192]{2,1,0:T(8,128)(2,1)} %bitcast.89, bf16[4,272,512]{2,1,0:T(8,128)(2,1)S(1)} %bitcast.64, ...), custom_call_target="tpu_custom_call" | custom-call | flops 855638016 | bytes 3768320 | tf_op jit(solution)/shard_map/pallas_call | solution.py:119
  48.0 0.0 collective-permute-done.10.refs_1_
  48.0 3.2 %shard_map.76 = s16[4112,128]{1,0:T(8,128)(2,1)S(1)} custom-call(f32[1,1024,512]{2,1,0:T(8,128)S(1)} %bitcast.69, f32[1,1024,512]{2,1,0:T(8,128)} %collective-permute-done.10.refs_1_), custom_call_target="tpu_custom_call" | custom-call | flops 10485760 | bytes 5242880 | tf_op jit(solution)/shard_map/pallas_call | solution.py:83
  51.2 0.1 collective-permute-start.11
  51.3 5.1 %collective-permute-done.13.refs_2_ = s16[4112,128]{1,0:T(8,128)(2,1)} collective-permute-done((s16[4112,128]{1,0:T(8,128)(2,1)}, s16[4112,128]{1,0:T(8,128)(2,1)}, u32[]{:S(2)}, u32[]{:S(2)}) %collective-permute-start.13) | collective-permute-done | bytes 1052704 | tf_op jit(solution)/shard_map/ppermute | solution.py:243
  56.4 0.0 collective-permute-done.9.refs_1_
  56.4 4.4 %shard_map.80 = s16[4112,128]{1,0:T(8,128)(2,1)S(1)} custom-call(f32[2,1024,512]{2,1,0:T(8,128)} %bitcast.67, f32[2,1024,512]{2,1,0:T(8,128)} %collective-permute-done.9.refs_1_, s16[4112,128]{1,0:T(8,128)(2,1)} %collective-permute-done.13.refs_2_), custom_call_target="tpu_custom_call" | custom-call | flops 10485760 | bytes 6291456 | tf_op jit(solution)/shard_map/pallas_call | solution.py:83
  60.8 2.0 %collective-permute-start.14 = (s16[4112,128]{1,0:T(8,128)(2,1)S(1)}, s16[4112,128]{1,0:T(8,128)(2,1)S(1)}, u32[]{:S(2)}, u32[]{:S(2)}) collective-permute-start(s16[4112,128]{1,0:T(8,128)(2,1)S(1)} %shard_map.80), channel_id=1, source_target_pairs={{0,1},{1,0},{2,3},{3,2},{4,5},{5,4},{6,7},{7,6},{8,9},{9,8},{10,11... | collective-permute-start | bytes 3158024 | tf_op jit(solution)/shard_map/ppermute | solution.py:246
  62.8 0.0 collective-permute-done.4.refs_0_
  62.8 0.4 collective-permute-start.5
  63.2 20.2 %collective-permute-done.1.refs_0_ = bf16[1024,512]{1,0:T(8,128)(2,1)} collective-permute-done((bf16[1024,512]{1,0:T(8,128)(2,1)}, bf16[1024,512]{1,0:T(8,128)(2,1)}, u32[]{:S(2)}, u32[]{:S(2)}) %collective-permute-start.1) | collective-permute-done | bytes 1048608 | tf_op jit(solution)/shard_map/ppermute | solution.py:249
  83.4 1.5 collective-permute-start.2
  84.9 2.1 %collective-permute-done.14.refs_3_ = s16[4112,128]{1,0:T(8,128)(2,1)S(1)} collective-permute-done((s16[4112,128]{1,0:T(8,128)(2,1)S(1)}, s16[4112,128]{1,0:T(8,128)(2,1)S(1)}, u32[]{:S(2)}, u32[]{:S(2)}) %collective-permute-start.14) | collective-permute-done | bytes 1052704 | tf_op jit(solution)/shard_map/ppermute | solution.py:246
  87.1 4.6 %shard_map.81.refs_0_ = s16[4112,128]{1,0:T(8,128)(2,1)S(1)} custom-call(f32[2,1024,512]{2,1,0:T(8,128)} %bitcast.68, f32[2,1024,512]{2,1,0:T(8,128)} %collective-permute-done.9.refs_1_, s16[4112,128]{1,0:T(8,128)(2,1)S(1)} %collective-permute-done.11.refs_2_, s16[4112,128]{1,0:T(8,128)(2,1)S(1)} %collective-permute-done.14.refs_3_), custom_call_target="tpu_custom_call" | custom-call | flops 10485760 | bytes 7340032 | tf_op jit(solution)/shard_map/pallas_call | solution.py:83
  91.6 2.0 %collective-permute-start.15 = (s16[4112,128]{1,0:T(8,128)(2,1)S(1)}, s16[4112,128]{1,0:T(8,128)(2,1)S(1)}, u32[]{:S(2)}, u32[]{:S(2)}) collective-permute-start(s16[4112,128]{1,0:T(8,128)(2,1)S(1)} %shard_map.81.refs_0_), channel_id=1, source_target_pairs={{0,16},{8,24},{16,0},{24,8},{1,17},{9,25},{17,1},{25,9},{2,18},{10... | collective-permute-start | bytes 3158024 | tf_op jit(solution)/shard_map/ppermute | solution.py:243
  93.7 1.3 collective-permute-start
  95.0 9.7 %collective-permute-done.current_ref = bf16[272,512]{1,0:T(8,128)(2,1)S(1)} collective-permute-done((bf16[272,512]{1,0:T(8,128)(2,1)S(1)}, bf16[272,512]{1,0:T(8,128)(2,1)S(1)}, u32[]{:S(2)}, u32[]{:S(2)}) %collective-permute-start) | collective-permute-done | bytes 278560 | tf_op jit(solution)/shard_map/ppermute | solution.py:249
  104.7 0.0 collective-permute-start.7
  104.7 5.0 %collective-permute-done.5.refs_0_ = bf16[1024,512]{1,0:T(8,128)(2,1)} collective-permute-done((bf16[1024,512]{1,0:T(8,128)(2,1)}, bf16[1024,512]{1,0:T(8,128)(2,1)}, u32[]{:S(2)}, u32[]{:S(2)}) %collective-permute-start.5) | collective-permute-done | bytes 1048608 | tf_op jit(solution)/shard_map/ppermute | solution.py:246
  109.6 0.0 collective-permute-start.6
  109.6 21.1 %collective-permute-done.2.refs_0_ = bf16[1024,512]{1,0:T(8,128)(2,1)} collective-permute-done((bf16[1024,512]{1,0:T(8,128)(2,1)}, bf16[1024,512]{1,0:T(8,128)(2,1)}, u32[]{:S(2)}, u32[]{:S(2)}) %collective-permute-start.2) | collective-permute-done | bytes 1048608 | tf_op jit(solution)/shard_map/ppermute | solution.py:246
  130.8 0.5 collective-permute-start.17
  131.3 0.0 collective-permute-done.15.refs_0_
  131.3 0.1 collective-permute-start.16
  131.4 0.1 pad_add_fusion.3.place
  131.5 0.1 pad_add_fusion.2.place
  131.5 0.1 pad_add_fusion.1.place
  131.6 0.1 pad_add_fusion.place
  131.7 0.1 pad_add_fusion.4
  131.8 3.9 %shard_map.68.refs_2_ = bf16[272,8192]{1,0:T(8,128)(2,1)} custom-call(s32[2]{0:T(128)S(1)} %pad_add_fusion.3.place, bf16[272,512]{1,0:T(8,128)(2,1)S(1)} %collective-permute-done.current_ref, bf16[1024,512]{1,0:T(8,128)(2,1)} %collective-permute-done.4.refs_0_, bf16[1024,512]{1,0:T(8,128)(2,1)} %collective-permute-done.8.refs_1_), custom_call_target="tpu_custom_call" | custom-call | flops 570425344 | bytes 3211264 | tf_op jit(solution)/shard_map/pallas_call | solution.py:162
  135.7 3.9 %shard_map.69.refs_2_ = bf16[272,8192]{1,0:T(8,128)(2,1)} custom-call(s32[2]{0:T(128)S(1)} %pad_add_fusion.2.place, bf16[272,512]{1,0:T(8,128)(2,1)S(1)} %collective-permute-done.current_ref, bf16[1024,512]{1,0:T(8,128)(2,1)} %collective-permute-done.1.refs_0_, bf16[1024,512]{1,0:T(8,128)(2,1)} %collective-permute-done.7.refs_1_, ...), custom_call_target="tpu_custom_call", output_to_operand_aliasing={{}: (4, {})} | custom-call | flops 570425344 | bytes 3211264 | tf_op jit(solution)/shard_map/pallas_call | solution.py:162
  139.6 3.9 %shard_map.70.refs_2_ = bf16[272,8192]{1,0:T(8,128)(2,1)} custom-call(s32[2]{0:T(128)S(1)} %pad_add_fusion.1.place, bf16[272,512]{1,0:T(8,128)(2,1)S(1)} %collective-permute-done.current_ref, bf16[1024,512]{1,0:T(8,128)(2,1)} %collective-permute-done.5.refs_0_, bf16[1024,512]{1,0:T(8,128)(2,1)} %collective-permute-done.6.refs_1_, ...), custom_call_target="tpu_custom_call", output_to_operand_aliasing={{}: (4, {})} | custom-call | flops 570425344 | bytes 3211264 | tf_op jit(solution)/shard_map/pallas_call | solution.py:162
  143.5 3.9 %shard_map.71 = bf16[272,8192]{1,0:T(8,128)(2,1)} custom-call(s32[2]{0:T(128)S(1)} %pad_add_fusion.place, bf16[272,512]{1,0:T(8,128)(2,1)S(1)} %collective-permute-done.current_ref, bf16[1024,512]{1,0:T(8,128)(2,1)} %collective-permute-done.2.refs_0_, bf16[1024,512]{1,0:T(8,128)(2,1)} %collective-permute-done.3.refs_1_, ...), custom_call_target="tpu_custom_call", output_to_operand_aliasing={{}: (4, {})} | custom-call | flops 570425344 | bytes 3211264 | tf_op jit(solution)/shard_map/pallas_call | solution.py:162
  147.4 4.5 %shard_map.82.refs_2_ = f32[4,1024,512]{2,1,0:T(8,128)} custom-call(s32[2]{0:T(128)S(1)} %get-tuple-element.13.place, s16[4112,128]{1,0:T(8,128)(2,1)S(1)} %shard_map.81.refs_0_, s16[4112,128]{1,0:T(8,128)(2,1)} %collective-permute-done.17.refs_1_), custom_call_target="tpu_custom_call" | custom-call | flops 4194304 | bytes 6291456 | tf_op jit(solution)/shard_map/pallas_call | solution.py:207
  151.9 4.5 %shard_map.83 = f32[4,1024,512]{2,1,0:T(8,128)} custom-call(s32[2]{0:T(128)S(1)} %get-tuple-element.12.place, s16[4112,128]{1,0:T(8,128)(2,1)S(1)} %collective-permute-done.15.refs_0_, s16[4112,128]{1,0:T(8,128)(2,1)} %collective-permute-done.16.refs_1_, f32[4,1024,512]{2,1,0:T(8,128)} %shard_map.82.refs_2_), custom_call_target="tpu_custom_call", output_to_operand_aliasing={{}: (3, {})} | custom-call | flops 4194304 | bytes 6291456 | tf_op jit(solution)/shard_map/pallas_call | solution.py:207
  (38 shorter events, 0.3 us)
Async XLA Ops:
  0.6 0.8 copy-start
  2.8 1.2 copy-start.2
  4.1 8.3 %copy-start.3 = (bf16[1,1,4,272,512]{4,3,2,1,0:T(8,128)(2,1)S(1)}, bf16[1,1,4,272,512]{4,3,2,1,0:T(8,128)(2,1)}, u32[]{:S(2)}) copy-start(bf16[1,1,4,272,512]{4,3,2,1,0:T(8,128)(2,1)} %param.6) | copy-start | bytes 3342340
  10.6 45.9 %collective-permute-start.9 = (f32[2,1024,512]{2,1,0:T(8,128)}, f32[2,1024,512]{2,1,0:T(8,128)}, u32[]{:S(2)}, u32[]{:S(2)}) collective-permute-start(f32[2,1024,512]{2,1,0:T(8,128)} %bitcast.22), channel_id=1, source_target_pairs={{0,8},{8,0},{16,24},{24,16},{1,9},{9,1},{17,25},{25,17},{2,10},{10... | collective-permute-start | bytes 12582920 | tf_op jit(solution)/shard_map/ppermute | solution.py:240
  16.6 8.4 %collective-permute-start.12 = (f32[1,1024,512]{2,1,0:T(8,128)}, f32[1,1024,512]{2,1,0:T(8,128)}, u32[]{:S(2)}, u32[]{:S(2)}) collective-permute-start(f32[1,1024,512]{2,1,0:T(8,128)} %bitcast.30), channel_id=1, source_target_pairs={{0,8},{8,0},{16,24},{24,16},{1,9},{9,1},{17,25},{25,17},{2,10},{10... | collective-permute-start | bytes 6291464 | tf_op jit(solution)/shard_map/ppermute | solution.py:240
  21.3 26.7 %collective-permute-start.10 = (f32[1,1024,512]{2,1,0:T(8,128)S(1)}, f32[1,1024,512]{2,1,0:T(8,128)}, u32[]{:S(2)}, u32[]{:S(2)}) collective-permute-start(f32[1,1024,512]{2,1,0:T(8,128)S(1)} %bitcast.71), channel_id=1, source_target_pairs={{0,8},{8,0},{16,24},{24,16},{1,9},{9,1},{17,25},{25,17},{2,10},{10... | collective-permute-start | bytes 6291464 | tf_op jit(solution)/shard_map/ppermute | solution.py:240
  25.1 7.0 %copy-start.5 = (bf16[1,4096,512]{2,1,0:T(8,128)(2,1)S(1)}, bf16[1,4096,512]{2,1,0:T(8,128)(2,1)}, u32[]{:S(2)}) copy-start(bf16[1,4096,512]{2,1,0:T(8,128)(2,1)} %param.7) | copy-start | bytes 12582916
  29.5 27.0 %collective-permute-start.13 = (s16[4112,128]{1,0:T(8,128)(2,1)}, s16[4112,128]{1,0:T(8,128)(2,1)}, u32[]{:S(2)}, u32[]{:S(2)}) collective-permute-start(s16[4112,128]{1,0:T(8,128)(2,1)} %shard_map.79), channel_id=1, source_target_pairs={{0,16},{8,24},{16,0},{24,8},{1,17},{9,25},{17,1},{25,9},{2,18},{10... | collective-permute-start | bytes 3158024 | tf_op jit(solution)/shard_map/ppermute | solution.py:243
  33.5 29.3 %collective-permute-start.4 = (bf16[1024,512]{1,0:T(8,128)(2,1)}, bf16[1024,512]{1,0:T(8,128)(2,1)}, u32[]{:S(2)}, u32[]{:S(2)}) collective-permute-start(bf16[1024,512]{1,0:T(8,128)(2,1)} %get-tuple-element.2), channel_id=1, source_target_pairs={{2,0},{4,2},{6,4},{3,1},{5,3},{7,5},{10,8},{12,10},{14,12},{11,9},... | collective-permute-start | bytes 3145736 | tf_op jit(solution)/shard_map/ppermute | solution.py:249
  34.8 48.6 %collective-permute-start.1 = (bf16[1024,512]{1,0:T(8,128)(2,1)}, bf16[1024,512]{1,0:T(8,128)(2,1)}, u32[]{:S(2)}, u32[]{:S(2)}) collective-permute-start(bf16[1024,512]{1,0:T(8,128)(2,1)} %get-tuple-element.3), channel_id=1, source_target_pairs={{2,0},{4,2},{6,4},{3,1},{5,3},{7,5},{10,8},{12,10},{14,12},{11,9},... | collective-permute-start | bytes 3145736 | tf_op jit(solution)/shard_map/ppermute | solution.py:249
  42.7 2.0 %copy-start.4 = (f32[4,512,512]{2,1,0:T(8,128)}, f32[4,512,512]{2,1,0:T(8,128)S(1)}, u32[]{:S(2)}) copy-start(f32[4,512,512]{2,1,0:T(8,128)S(1)} %shard_map.72) | copy-start | bytes 12582916
  51.2 33.7 %collective-permute-start.11 = (s16[4112,128]{1,0:T(8,128)(2,1)S(1)}, s16[4112,128]{1,0:T(8,128)(2,1)S(1)}, u32[]{:S(2)}, u32[]{:S(2)}) collective-permute-start(s16[4112,128]{1,0:T(8,128)(2,1)S(1)} %shard_map.76), channel_id=1, source_target_pairs={{0,16},{8,24},{16,0},{24,8},{1,17},{9,25},{17,1},{25,9},{2,18},{10... | collective-permute-start | bytes 3158024 | tf_op jit(solution)/shard_map/ppermute | solution.py:243
  60.8 26.2 %collective-permute-start.14 = (s16[4112,128]{1,0:T(8,128)(2,1)S(1)}, s16[4112,128]{1,0:T(8,128)(2,1)S(1)}, u32[]{:S(2)}, u32[]{:S(2)}) collective-permute-start(s16[4112,128]{1,0:T(8,128)(2,1)S(1)} %shard_map.80), channel_id=1, source_target_pairs={{0,1},{1,0},{2,3},{3,2},{4,5},{5,4},{6,7},{7,6},{8,9},{9,8},{10,11... | collective-permute-start | bytes 3158024 | tf_op jit(solution)/shard_map/ppermute | solution.py:246
  62.8 46.8 %collective-permute-start.5 = (bf16[1024,512]{1,0:T(8,128)(2,1)}, bf16[1024,512]{1,0:T(8,128)(2,1)}, u32[]{:S(2)}, u32[]{:S(2)}) collective-permute-start(bf16[1024,512]{1,0:T(8,128)(2,1)} %collective-permute-done.4.refs_0_), channel_id=1, source_target_pairs={{0,1},{1,0},{2,3},{3,2},{4,5},{5,4},{6,7},{7,6},{8,9},{9,8},{10,11... | collective-permute-start | bytes 3145736 | tf_op jit(solution)/shard_map/ppermute | solution.py:246
  83.4 47.4 %collective-permute-start.2 = (bf16[1024,512]{1,0:T(8,128)(2,1)}, bf16[1024,512]{1,0:T(8,128)(2,1)}, u32[]{:S(2)}, u32[]{:S(2)}) collective-permute-start(bf16[1024,512]{1,0:T(8,128)(2,1)} %collective-permute-done.1.refs_0_), channel_id=1, source_target_pairs={{0,1},{1,0},{2,3},{3,2},{4,5},{5,4},{6,7},{7,6},{8,9},{9,8},{10,11... | collective-permute-start | bytes 3145736 | tf_op jit(solution)/shard_map/ppermute | solution.py:246
  91.6 39.7 %collective-permute-start.15 = (s16[4112,128]{1,0:T(8,128)(2,1)S(1)}, s16[4112,128]{1,0:T(8,128)(2,1)S(1)}, u32[]{:S(2)}, u32[]{:S(2)}) collective-permute-start(s16[4112,128]{1,0:T(8,128)(2,1)S(1)} %shard_map.81.refs_0_), channel_id=1, source_target_pairs={{0,16},{8,24},{16,0},{24,8},{1,17},{9,25},{17,1},{25,9},{2,18},{10... | collective-permute-start | bytes 3158024 | tf_op jit(solution)/shard_map/ppermute | solution.py:243
  93.7 37.1 %collective-permute-start.8 = (bf16[1024,512]{1,0:T(8,128)(2,1)}, bf16[1024,512]{1,0:T(8,128)(2,1)}, u32[]{:S(2)}, u32[]{:S(2)}) collective-permute-start(bf16[1024,512]{1,0:T(8,128)(2,1)} %collective-permute-done.4.refs_0_), channel_id=1, source_target_pairs={{0,8},{8,0},{16,24},{24,16},{1,9},{9,1},{17,25},{25,17},{2,10},{10... | collective-permute-start | bytes 3145736 | tf_op jit(solution)/shard_map/ppermute | solution.py:240
  93.7 11.0 %collective-permute-start = (bf16[272,512]{1,0:T(8,128)(2,1)S(1)}, bf16[272,512]{1,0:T(8,128)(2,1)S(1)}, u32[]{:S(2)}, u32[]{:S(2)}) collective-permute-start(bf16[272,512]{1,0:T(8,128)(2,1)S(1)} %dynamic-slice_bitcast_fusion.2), channel_id=1, source_target_pairs={{2,0},{4,2},{6,4},{3,1},{5,3},{7,5},{10,8},{12,10},{14,12},{11,9},... | collective-permute-start | bytes 835592 | tf_op jit(solution)/shard_map/ppermute | solution.py:249
  104.7 31.0 %collective-permute-start.7 = (bf16[1024,512]{1,0:T(8,128)(2,1)}, bf16[1024,512]{1,0:T(8,128)(2,1)}, u32[]{:S(2)}, u32[]{:S(2)}) collective-permute-start(bf16[1024,512]{1,0:T(8,128)(2,1)} %collective-permute-done.1.refs_0_), channel_id=1, source_target_pairs={{0,8},{8,0},{16,24},{24,16},{1,9},{9,1},{17,25},{25,17},{2,10},{10... | collective-permute-start | bytes 3145736 | tf_op jit(solution)/shard_map/ppermute | solution.py:240
  109.6 29.9 %collective-permute-start.6 = (bf16[1024,512]{1,0:T(8,128)(2,1)}, bf16[1024,512]{1,0:T(8,128)(2,1)}, u32[]{:S(2)}, u32[]{:S(2)}) collective-permute-start(bf16[1024,512]{1,0:T(8,128)(2,1)} %collective-permute-done.5.refs_0_), channel_id=1, source_target_pairs={{0,8},{8,0},{16,24},{24,16},{1,9},{9,1},{17,25},{25,17},{2,10},{10... | collective-permute-start | bytes 3145736 | tf_op jit(solution)/shard_map/ppermute | solution.py:240
  130.8 12.7 %collective-permute-start.3 = (bf16[1024,512]{1,0:T(8,128)(2,1)}, bf16[1024,512]{1,0:T(8,128)(2,1)}, u32[]{:S(2)}, u32[]{:S(2)}) collective-permute-start(bf16[1024,512]{1,0:T(8,128)(2,1)} %collective-permute-done.2.refs_0_), channel_id=1, source_target_pairs={{0,8},{8,0},{16,24},{24,16},{1,9},{9,1},{17,25},{25,17},{2,10},{10... | collective-permute-start | bytes 3145736 | tf_op jit(solution)/shard_map/ppermute | solution.py:240
  130.8 16.6 %collective-permute-start.17 = (s16[4112,128]{1,0:T(8,128)(2,1)S(1)}, s16[4112,128]{1,0:T(8,128)(2,1)}, u32[]{:S(2)}, u32[]{:S(2)}) collective-permute-start(s16[4112,128]{1,0:T(8,128)(2,1)S(1)} %shard_map.81.refs_0_), channel_id=1, source_target_pairs={{0,8},{8,0},{16,24},{24,16},{1,9},{9,1},{17,25},{25,17},{2,10},{10... | collective-permute-start | bytes 3158024 | tf_op jit(solution)/shard_map/ppermute | solution.py:240
  131.3 20.6 %collective-permute-start.16 = (s16[4112,128]{1,0:T(8,128)(2,1)S(1)}, s16[4112,128]{1,0:T(8,128)(2,1)}, u32[]{:S(2)}, u32[]{:S(2)}) collective-permute-start(s16[4112,128]{1,0:T(8,128)(2,1)S(1)} %collective-permute-done.15.refs_0_), channel_id=1, source_target_pairs={{0,8},{8,0},{16,24},{24,16},{1,9},{9,1},{17,25},{25,17},{2,10},{10... | collective-permute-start | bytes 3158024 | tf_op jit(solution)/shard_map/ppermute | solution.py:240
  151.9 4.5 %copy-start.1 = (s32[8]{0:T(128)S(1)}, s32[8]{0:T(128)}, u32[]{:S(2)}) copy-start(s32[8]{0:T(128)} %param.9) | copy-start | bytes 100

commit v2 on v0

v2 whole, which is shorter than its diff:
```python
import functools
import math

import jax
import jax.numpy as jnp
from jax import lax
from jax.experimental import pallas as pl
from jax.experimental.pallas import tpu as pltpu
from jax.sharding import PartitionSpec as P

LANES = 128
TAIL = 16
MORE = 16
FAR_TAILS = 8
SIDE_TAILS = 6
DONE = jax.ShapeDtypeStruct((8, LANES), jnp.float32)
INNER = 2
TOP = 32767.0
VMEM_LIMIT = 48 << 20


def params():
    return pltpu.CompilerParams(vmem_limit_bytes=VMEM_LIMIT)


def code_shape(rows, width, tails=1):
    return jax.ShapeDtypeStruct((width // LANES * rows + TAIL * tails, LANES), jnp.int16)


def scale_of(code_ref, count):
    exponent = code_ref[count : count + TAIL, :].astype(jnp.int32)[0:1, :].astype(jnp.float32)
    return jnp.exp2(exponent) * (1.0 / (TOP * TOP))


def decoded(code_ref, start, rows, scale):
    level = code_ref[pl.ds(start, rows), :].astype(jnp.int32).astype(jnp.float32)
    return level * jnp.abs(level) * scale


def hold_kernel(*refs):
    pass


def after(value, *waits):
    return pl.pallas_call(
        hold_kernel,
        out_shape=jax.ShapeDtypeStruct(value.shape, value.dtype),
        in_specs=[pl.BlockSpec(memory_space=pl.ANY)] + [pl.BlockSpec(memory_space=pl.ANY) for _ in waits],
        out_specs=pl.BlockSpec(memory_space=pl.ANY),
        input_output_aliases={0: 0},
        compiler_params=params(),
    )(value, *waits)


def gather_total(total_ref, start, rows, whole, codes, largest):
    width = total_ref.shape[1]
    step = min(rows, 128)
    slabs = width // LANES
    scales = [scale_of(c, slabs * whole) for c in codes]

    def add(i, largest):
        r = pl.multiple_of(start + i * step, step)
        for j in range(slabs):
            slab = slice(j * LANES, (j + 1) * LANES)
            value = total_ref[pl.ds(r, step), slab]
            for c, scale in zip(codes, scales):
                value = value + decoded(c, pl.multiple_of(j * whole + r, step), step, scale)
            if codes:
                total_ref[pl.ds(r, step), slab] = value
            largest = jnp.maximum(largest, jnp.max(jnp.abs(value).reshape(step // 8, 8, LANES), axis=0))
        return largest

    return lax.fori_loop(0, rows // step, add, largest)


def encode(total_ref, largest, out_ref):
    rows, width = total_ref.shape
    step = min(rows, 128)
    slabs = width // LANES
    largest = jnp.max(jnp.max(largest, axis=0, keepdims=True), axis=1, keepdims=True)
    exponent = jnp.floor(jnp.log2(jnp.maximum(largest, 1e-30))) + 2.0
    exponent = jnp.broadcast_to(exponent, (8, LANES))
    shrink = jnp.exp2(-exponent)[0:1, :]

    def one(i, carry):
        r = pl.multiple_of(i * step, step)
        for j in range(slabs):
            value = total_ref[pl.ds(r, step), j * LANES : (j + 1) * LANES]
            root = jnp.round(jnp.sqrt(jnp.abs(value) * shrink) * TOP)
            level = jnp.where(value < 0.0, -root, root)
            place = pl.ds(pl.multiple_of(j * rows + r, step), step)
            out_ref[place, :] = level.astype(jnp.int32).astype(jnp.int16)
        return carry

    lax.fori_loop(0, rows // step, one, 0)
    tail = jnp.concatenate([exponent] * ((out_ref.shape[0] - slabs * rows) // 8), axis=0)
    out_ref[slabs * rows :, :] = tail.astype(jnp.int32).astype(jnp.int16)


def combine_kernel(kept_ref, *refs, n_codes, rows):
    out_ref, total_ref = refs[-2:]
    total_ref[...] = kept_ref[0]
    largest = gather_total(total_ref, 0, rows, rows, refs[:n_codes], jnp.zeros((8, LANES), jnp.float32))
    encode(total_ref, largest, out_ref)


def combine(kept, at, codes, *waits, tails=1):
    _, rows, width = kept.shape
    shape = code_shape(rows, width, tails)
    in_specs = (
        [pl.BlockSpec((1, rows, width), lambda i: (at, 0, 0))]
        + [pl.BlockSpec(x.shape, lambda i: (0, 0)) for x in codes]
        + [pl.BlockSpec(memory_space=pl.ANY) for _ in waits]
    )
    return pl.pallas_call(
        functools.partial(combine_kernel, n_codes=len(codes), rows=rows),
        out_shape=shape,
        grid=(1,),
        in_specs=in_specs,
        out_specs=pl.BlockSpec(shape.shape, lambda i: (0, 0)),
        scratch_shapes=[pltpu.VMEM((rows, width), jnp.float32)],
        compiler_params=params(),
    )(kept, *codes, *waits)


def token_kernel(order, picks, starts, *refs, count, groups, n_codes, n_waits, moves, n_sources, coded, rows, block):
    left = jnp.concatenate([r[0] for r in refs[:count]], axis=0)
    right = jnp.concatenate([r[0] for r in refs[count : 2 * count]], axis=0)
    refs = refs[2 * count :]
    codes, sources, outs = refs[:n_codes], refs[n_codes : n_codes + n_sources], refs[n_codes + n_sources + n_waits :]
    step = pl.program_id(1)
    ends = (pl.program_id(0) == groups - 1) & (step == rows // block - 1)
    copies = []
    n_out = groups if coded else 1
    for n, segments in enumerate(moves):
        place = 0
        for source, length in segments:
            at = pl.ds(pl.multiple_of(starts[len(copies)], TAIL), length)
            to = outs[n_out + n].at[pl.ds(place, length), :]
            copies.append((sources[source].at[at, :], to, outs[-1].at[len(copies)]))
            place += length
    if copies:

        @pl.when((pl.program_id(0) == 0) & (step == 0))
        def _():
            for c in copies:
                pltpu.make_async_copy(*c).start()

    product = lax.dot_general(left, right, (((0,), (0,)), ((), ())), preferred_element_type=jnp.float32)
    start = pl.multiple_of(step * block, block)
    scratch = outs[n_out + len(moves) :]
    total_ref = scratch[0] if coded else outs[0].at[0]
    total_ref[pl.ds(start, block), :] = product
    each = n_codes // groups
    for n in range(groups if coded or codes else 0):

        @pl.when(pl.program_id(0) == n)
        def _():
            seen = jnp.zeros((8, LANES), jnp.float32)
            if coded:
                largest_ref = scratch[1]
                seen = jnp.where(step == 0, seen, largest_ref[...])
            seen = gather_total(total_ref, start, block, rows, codes[n * each : (n + 1) * each], seen)
            if coded:
                largest_ref[...] = seen

                @pl.when(step == rows // block - 1)
                def _():
                    encode(total_ref, largest_ref[...], outs[n])

    if copies:

        @pl.when(ends)
        def _():
            for c in copies:
                pltpu.make_async_copy(*c).wait()


def token_products(
    order, first, groups, picks, acts, grads, block, rows, coded, codes, *waits, tails=1, sources=(), moves=()
):
    count = picks.shape[0]
    tokens = acts.shape[1]
    width = grads.shape[2]
    steps = rows // block
    shape = code_shape(rows, width, tails)
    in_specs = (
        [
            pl.BlockSpec(
                (1, tokens, block),
                functools.partial(lambda m, g, s, o, p, q: (p[m], 0, o[first + g * steps + s]), m),
            )
            for m in range(count)
        ]
        + [
            pl.BlockSpec((1, tokens, width), functools.partial(lambda m, g, s, o, p, q: (p[m], 0, 0), m))
            for m in range(count)
        ]
        + [pl.BlockSpec(x.shape, lambda g, s, o, p, q: (0, 0)) for x in codes]
        + [pl.BlockSpec(memory_space=pltpu.HBM) for _ in sources]
        + [pl.BlockSpec(memory_space=pl.ANY) for _ in waits]
    )
    if coded:
        out_shape = [shape] * groups
        out_specs = [pl.BlockSpec(shape.shape, lambda g, s, o, p, q: (0, 0))] * groups
        scratch = [pltpu.VMEM((rows, width), jnp.float32), pltpu.VMEM((8, LANES), jnp.float32)]
    else:
        out_shape = [jax.ShapeDtypeStruct((groups, rows, width), jnp.float32)]
        out_specs = [pl.BlockSpec((1, rows, width), lambda g, s, o, p, q: (g, 0, 0))]
        scratch = []
    starts = [jnp.asarray(at, jnp.int32) for m in moves for _, at, _ in m]
    for m in moves:
        like = sources[m[0][0]]
        out_shape.append(jax.ShapeDtypeStruct((sum(n for _, _, n in m), like.shape[1]), like.dtype))
        out_specs.append(pl.BlockSpec(out_shape[-1].shape, lambda g, s, o, p, q: (0, 0)))
    if moves:
        scratch.append(pltpu.SemaphoreType.DMA((len(starts),)))
    return pl.pallas_call(
        functools.partial(
            token_kernel,
            count=count,
            groups=groups,
            n_codes=len(codes),
            n_waits=len(waits),
            moves=[[(source, n) for source, _, n in m] for m in moves],
            n_sources=len(sources),
            coded=coded,
            rows=rows,
            block=block,
        ),
        out_shape=out_shape,
        grid_spec=pltpu.PrefetchScalarGridSpec(
            num_scalar_prefetch=3, grid=(groups, steps), in_specs=in_specs, out_specs=out_specs, scratch_shapes=scratch
        ),
        compiler_params=params(),
    )(
        order,
        picks,
        jnp.stack(starts) if starts else picks,
        *([acts] * count),
        *([grads] * count),
        *codes,
        *sources,
        *waits,
    )


def key_kernel(starts, current_ref, *refs, count, skip, rows):
    out_ref, done_ref, block_ref, sem = refs[-4:]
    step = min(rows, 512)
    copies = []
    for n in range(count):
        place = pl.multiple_of(starts[n], LANES)
        for at in range(0, rows, step):
            size = min(step, rows - at)
            block_ref[n, :, at : at + size] = lax.dot_general(
                current_ref[...],
                refs[n][skip + at : skip + at + size, :],
                (((1,), (1,)), ((), ())),
                preferred_element_type=jnp.float32,
            ).astype(out_ref.dtype)
        copies.append(pltpu.make_async_copy(block_ref.at[n], out_ref.at[:, pl.ds(place, rows)], sem.at[n]))
        copies[-1].start()
    done_ref[...] = jnp.zeros_like(done_ref)
    for c in copies:
        c.wait()


def key_products(starts, current, parts, skip, rows, features, held, *waits):
    tokens, width = current.shape
    count = len(parts)
    anywhere = pl.BlockSpec(memory_space=pltpu.HBM)
    in_specs = [pl.BlockSpec(x.shape, lambda i, p: (0, 0)) for x in (current, *parts)]
    operands = [starts, current, *parts]
    aliases = {}
    if held is not None:
        in_specs.append(anywhere)
        aliases = {len(operands): 0}
        operands.append(held)
    in_specs += [pl.BlockSpec(memory_space=pl.ANY) for _ in waits]
    operands += waits
    return pl.pallas_call(
        functools.partial(key_kernel, count=count, skip=skip, rows=rows),
        out_shape=[jax.ShapeDtypeStruct((tokens, features), jnp.bfloat16), DONE],
        grid_spec=pltpu.PrefetchScalarGridSpec(
            num_scalar_prefetch=1,
            grid=(1,),
            in_specs=in_specs,
            out_specs=[anywhere, pl.BlockSpec(DONE.shape, lambda i, p: (0, 0))],
            scratch_shapes=[pltpu.VMEM((count, tokens, rows), jnp.bfloat16), pltpu.SemaphoreType.DMA((count,))],
        ),
        input_output_aliases=aliases,
        compiler_params=params(),
    )(*operands)


def decode_kernel(place, *refs, count, rows, width):
    out_ref, done_ref, block_ref, sem = refs[-4:]
    slabs = width // LANES
    step = min(rows, 128)
    copies = []
    for n in range(count):
        scale = scale_of(refs[n], slabs * rows)

        def one(i, carry):
            r = pl.multiple_of(i * step, step)
            for j in range(slabs):
                block_ref[n, pl.ds(r, step), j * LANES : (j + 1) * LANES] = decoded(
                    refs[n], pl.multiple_of(j * rows + r, step), step, scale
                )
            return carry

        for k in range(2):
            part = rows // 2
            lax.fori_loop(k * part // step, (k + 1) * part // step, one, 0)
            at = pl.ds(k * part, part)
            copies.append(
                pltpu.make_async_copy(block_ref.at[n, at, :], out_ref.at[place[n], at, :], sem.at[2 * n + k])
            )
            copies[-1].start()
    done_ref[...] = jnp.zeros_like(done_ref)
    for c in copies:
        c.wait()


def decode(place, codes, blocks, rows, width, held, *waits):
    count = len(codes)
    anywhere = pl.BlockSpec(memory_space=pltpu.HBM)
    in_specs = [pl.BlockSpec(x.shape, lambda i, p: (0, 0)) for x in codes]
    operands = [place, *codes]
    aliases = {}
    if held is not None:
        in_specs.append(anywhere)
        aliases = {len(operands): 0}
        operands.append(held)
    in_specs += [pl.BlockSpec(memory_space=pl.ANY) for _ in waits]
    operands += waits
    return pl.pallas_call(
        functools.partial(decode_kernel, count=count, rows=rows, width=width),
        out_shape=[jax.ShapeDtypeStruct((blocks, rows, width), jnp.float32), DONE],
        grid_spec=pltpu.PrefetchScalarGridSpec(
            num_scalar_prefetch=1,
            grid=(1,),
            in_specs=in_specs,
            out_specs=[anywhere, pl.BlockSpec(DONE.shape, lambda i, p: (0, 0))],
            scratch_shapes=[
                pltpu.VMEM((count, rows, width), jnp.float32),
                pltpu.SemaphoreType.DMA((2 * count,)),
            ],
        ),
        input_output_aliases=aliases,
        compiler_params=params(),
    )(*operands)


def body(acts, key_grads, weights, b_slot, cycle):
    stored, grads, weight = acts[0, 0], key_grads[0, 0], weights[0]
    slot = b_slot[0]
    micro, tokens, features = stored.shape
    width = grads.shape[2]
    n_dp, n_ctx = lax.axis_size("dp"), lax.axis_size("ctx")
    n_pipe = lax.axis_size("pipe")
    outer = n_dp // INNER
    replica, section = lax.axis_index("dp"), lax.axis_index("ctx")
    me_o, me_i = replica // INNER, replica % INNER
    groups = n_dp * n_ctx
    rows = features // groups
    pieces = cycle.shape[0]

    def swap(value):
        pairs = [(d, d // INNER * INNER + (d + 1) % INNER) for d in range(n_dp)]
        return lax.ppermute(value, "dp", pairs)

    def to_outer(value, by):
        return lax.ppermute(value, "dp", [(d, (d + by * INNER) % n_dp) for d in range(n_dp)])

    def to_ctx(value, by):
        return lax.ppermute(value, "ctx", [(d, (d + by) % n_ctx) for d in range(n_ctx)])

    def to_previous(value):
        return lax.ppermute(value, "pipe", [(d, d - 1) for d in range(1, n_pipe)])

    half = weight.shape[0] // INNER
    part = half // 2
    late_part = max(half * 3 // 8 // LANES, 1) * LANES

    position = jnp.arange(micro - 1, dtype=jnp.int32)
    picks = position + (position >= slot).astype(jnp.int32)
    block = min(rows, features // pieces, 512)
    piece_blocks = features // pieces // block
    blocks_of = rows // block
    far = [(kx, ko) for ko in range(1, outer) for kx in range(1, n_ctx)]
    near = [(0, ko) for ko in range(1, outer)]
    side = [(kx, 0) for kx in range(1, n_ctx)]
    home = [(0, 0)]
    order, first, at = [], {}, 0
    for name, wanted, ki in (
        ("far", far, 1),
        ("far", far, 0),
        ("near side", near + side, 1),
        ("near", near, 0),
        ("side", side, 0),
        ("home", home, 1),
        ("home", home, 0),
    ):
        first[name, ki] = at
        for kx, ko in wanted:
            owner = ((section + kx) % n_ctx) * n_dp + ((me_o + ko) % outer) * INNER + (me_i + ki) % INNER
            order.append(owner * blocks_of + jnp.arange(blocks_of, dtype=jnp.int32))
            at += blocks_of
    order = jnp.concatenate(order)
    order = cycle[order // piece_blocks] * piece_blocks + order % piece_blocks

    def products(name, ki, wanted, coded, codes, *waits, **more):
        return token_products(
            order, first[name, ki], len(wanted), picks, stored, grads, block, rows, coded, codes, *waits, **more
        )

    *far_sent, own_first, own_most, own_second = products(
        "far",
        1,
        far,
        True,
        [],
        sources=(weight, grads.reshape(micro * tokens, width)),
        moves=(
            [(0, me_i * half, part), (1, slot * tokens, tokens)],
            [(0, me_i * half + late_part - MORE, half - late_part + MORE)],
            [(0, me_i * half + part - MORE, half - part + MORE)],
        ),
    )
    z_first = to_previous(own_first)
    crossed_most = [to_ctx(own_most, kx) for kx in range(1, n_ctx)]
    coded = dict(zip(far, products("far", 0, far, True, [swap(c) for c in far_sent], tails=FAR_TAILS)))
    got = {w: to_outer(coded[w], w[1]) for w in far}
    sent = products("near side", 1, near + side, True, [], *coded.values())
    theirs = [swap(c) for c in sent]
    coded = dict(zip(near, products("near", 0, near, True, theirs[: len(near)], tails=SIDE_TAILS)))
    (side_sums,) = products("side", 0, side, False, theirs[len(near) :], *coded.values())
    got.update({w: to_outer(after(coded[w], *[got[f] for f in far]), w[1]) for w in near})

    passed = passed_done = None

    def pass_on(kx, start, count, held, skip, *waits):
        nonlocal passed, passed_done
        row = ((section - kx) % n_ctx) * weight.shape[0] + start
        starts = jnp.stack([row + me_i * half, row + (me_i + 1) % INNER * half])
        passed, passed_done = key_products(starts, current, [held, swap(held)], skip, count, features, passed, *waits)

    crossed = []
    for n, (kx, _) in enumerate(side):
        value = combine(side_sums, n, [got[kx, ko] for ko in range(1, outer)], tails=SIDE_TAILS)
        crossed.append(to_ctx(value, kx))
    z_second = to_previous(after(own_second, z_first, side_sums, *crossed_most, *[got[w] for w in far]))
    home_theirs = swap(products("home", 1, home, True, [], value)[0])
    (home_sum,) = products("home", 0, home, False, [home_theirs])
    current = lax.slice_in_dim(z_first, part, part + tokens)
    next_first = lax.slice_in_dim(z_first, 0, part)
    next_late = lax.slice_in_dim(z_first, 0, late_part)
    pass_on(0, 0, part, next_first, 0, home_sum)
    z_crossed = [to_previous(after(c, z_second)) for c in crossed_most]
    own = combine(home_sum, 0, [got[0, ko] for ko in range(1, outer)] + crossed, z_second, passed_done, next_late, tails=2)
    others = {ko: to_outer(own, ko) for ko in range(1, outer)}
    late = after(next_late, own)
    late = [to_ctx(late, kx) for kx in range(1, n_ctx)]
    result, result_done = decode(
        jnp.stack([me_o * INNER + me_i, me_o * INNER + (me_i + 1) % INNER]),
        [own, swap(own)],
        n_dp,
        rows,
        width,
        None,
    )
    pass_on(0, part, half - part, after(z_second, own), MORE, result_done)
    early_done = passed_done
    for kx in range(1, n_ctx):
        pass_on(kx, late_part, half - late_part, z_crossed[kx - 1], MORE)
    most_done = passed_done
    for kx in range(1, n_ctx):
        pass_on(kx, 0, late_part, late[kx - 1], 0)
    for ko in range(1, outer):
        other = after(others[ko], early_done)
        o = (me_o - ko) % outer
        place = jnp.stack([o * INNER + me_i, o * INNER + (me_i + 1) % INNER])
        result, _ = decode(place, [other, swap(other)], n_dp, rows, width, result, most_done)
    return passed[None, None], result.reshape(1, n_dp * rows, width)


def solution(mesh):
    placed = (
        P("dp", "pipe", None, "ctx", None),
        P("dp", "pipe", None, "ctx", None),
        P("pipe", "ctx", None),
        P("pipe"),
        P(),
    )
    return jax.shard_map(
        body,
        mesh=mesh,
        in_specs=placed,
        out_specs=(P("dp", "pipe", "ctx", None), P("pipe", "ctx", None)),
        check_vma=False,
    )
```

time: 489 us -> 128 us (0.26)
  waiting for transfers between devices: 339 us -> 33.3 us
  local copies, waits for them, and re-layouts: 91.4 us -> 7.58 us
  Pallas kernels: 0 us -> 66.8 us
  matrix products: 23.3 us -> 0 us
  other arithmetic: 19 us -> 0.6 us
  starting transfers between devices: 1.58 us -> 16.3 us
  between operations: 14.5 us -> 1.79 us
    reduce_scatter x1 -> x0, waiting for transfers between devices: 183 us -> none  [body(): lax.psum_scatter(token_product(blocked, chosen_grads), 'ctx', scatter_dim...]
    psum x1 -> x0, waiting for transfers between devices: 155 us -> none  [body(): summed = lax.psum(owned_rows, 'dp')]
    pallas_call x0 -> x21, Pallas kernels: none -> 66.8 us  [the longest x7 36.9 us: token_products(): pl.pallas_call(functools.partial(token_kernel, count=count, groups=groups...]
    gather x7 -> x1, local copies, waits for them, and re-layouts: 46.7 us -> 0.66 us  [body(): order = cycle[order // piece_blocks] * piece_blocks + order % piece_blocks]
    ppermute x1 -> x19, waiting for transfers between devices: 0.01 us -> 33.3 us  [the longest x3 26.7 us: to_previous(): return lax.ppermute(value, 'pipe', [(d, d - 1) for d in range(1, n_pipe)])]
    dot_general x2 -> x0, matrix products: 23.3 us -> none  [the longest x1 15.3 us: token_product(): lax.dot_general(left, right, (((0,), (0,)), ((), ())), preferred_element_...]
    select_n x1 -> x0, local copies, waits for them, and re-layouts: 23.3 us -> none  [body(): jnp.take(chosen_acts.reshape(micro_count - 1, row_count, piece_count, fea...]
    unnamed x9 -> x16, local copies, waits for them, and re-layouts: 21.4 us -> 2.6 us
  transfers between devices with their start and end apart: 4 -> 19, of which waited for: 2 -> 6; matrix products, arithmetic and copies ran while one was open for 25% -> 4% of each run, Pallas kernels for 0% -> 46%
where the time goes in v2:
time: 128 us; the launch traced here: 126 us
  Pallas kernels  66.8 us (52%)
  waiting for transfers between devices  33.3 us (26%)
  starting transfers between devices  16.3 us (13%)
  local copies, waits for them, and re-layouts  7.58 us (6%)
  between operations  1.79 us (1%)
    pallas_call x7, Pallas kernels, token_products(): pl.pallas_call(functools.partial(token_kernel, count=count, groups=groups...  36.9 us
    ppermute x3, waiting for transfers between devices, to_previous(): return lax.ppermute(value, 'pipe', [(d, d - 1) for d in range(1, n_pipe)])  26.7 us
    pallas_call x4, Pallas kernels, key_products(): pl.pallas_call(functools.partial(key_kernel, count=count, skip=skip, rows...  14.9 us
    pallas_call x2, Pallas kernels, combine(): pl.pallas_call(functools.partial(combine_kernel, n_codes=len(codes), rows...  7.54 us
    pallas_call x2, Pallas kernels, decode(): pl.pallas_call(functools.partial(decode_kernel, count=count, rows=rows, w...  7.4 us
    ppermute x3, starting transfers between devices, to_ctx(): lax.ppermute(value, 'ctx', [(d, (d + by) % n_ctx) for d in range(n_ctx)])  4.97 us
    ppermute x3, starting transfers between devices, to_outer(): lax.ppermute(value, 'dp', [(d, (d + by * INNER) % n_dp) for d in range(n_...  4.68 us
    ppermute x3, waiting for transfers between devices, to_outer(): lax.ppermute(value, 'dp', [(d, (d + by * INNER) % n_dp) for d in range(n_...  4.43 us
  transfers between devices with their start and end apart: 19, of which 6 were waited for; matrix products, arithmetic and copies ran while one was open for 4% of the time, Pallas kernels for 46%

profile of v2, /device:TPU:0, one launch (start us, length us, event | category | flops | bytes accessed | tf_op | source)
XLA Modules:
  0.0 126.4 jit_solution(15058897102489795105)
XLA Ops:
  0.6 0.0 copy-start
  1.5 0.1 concatenate.54
  1.7 0.7 gather_fusion
  2.3 0.1 concatenate.55
  2.4 0.1 pad_add_fusion.1.starts
  2.5 1.3 copy-done.2
  3.8 5.0 %shard_map.68 = (s16[4112,128]{1,0:T(8,128)(2,1)S(1)}, bf16[1296,512]{1,0:T(8,128)(2,1)S(1)}, bf16[1296,512]{1,0:T(8,128)(2,1)S(1)}, bf16[1040,512]{1,0:T(8,128)(2,1)S(1)}) custom-call(s32[16]{0:T(128)S(1)} %fusion.order, s32[3]{0:T(128)S(1)} %fusion.1.picks.starts, s32[4]{0:T(128)S(1)} %pad_add_fusion.1.starts, bf16[4,272,8192]{2,1,0:T(8,128)(2,1)} %bitcast.65, ...), custom_call_target="tpu_custom_call" | custom-call | tf_op jit(solution)/shard_map/pallas_call | solution.py:218
  8.8 0.5 collective-permute-start.1
  9.3 1.3 %collective-permute-start = (bf16[1296,512]{1,0:T(8,128)(2,1)S(1)}, bf16[1296,512]{1,0:T(8,128)(2,1)S(1)}, u32[]{:S(2)}, u32[]{:S(2)}) collective-permute-start(bf16[1296,512]{1,0:T(8,128)(2,1)S(1)} %get-tuple-element.18), channel_id=1, source_target_pairs={{2,0},{4,2},{6,4},{3,1},{5,3},{7,5},{10,8},{12,10},{14,12},{11,9},... | collective-permute-start | bytes 3981320 | tf_op jit(solution)/shard_map/ppermute | solution.py:381
  10.6 2.6 %collective-permute-start.8 = (bf16[1296,512]{1,0:T(8,128)(2,1)S(1)}, bf16[1296,512]{1,0:T(8,128)(2,1)}, u32[]{:S(2)}, u32[]{:S(2)}) collective-permute-start(bf16[1296,512]{1,0:T(8,128)(2,1)S(1)} %get-tuple-element.23), channel_id=1, source_target_pairs={{0,1},{1,0},{2,3},{3,2},{4,5},{5,4},{6,7},{7,6},{8,9},{9,8},{10,11... | collective-permute-start | bytes 3981320 | tf_op jit(solution)/shard_map/ppermute | solution.py:378
  13.2 0.0 collective-permute-done.1.refs_6_
  13.2 5.1 %shard_map.69.refs_6_ = s16[4224,128]{1,0:T(8,128)(2,1)S(1)} custom-call(s32[16]{0:T(128)S(1)} %fusion.order, s32[3]{0:T(128)S(1)} %fusion.1.picks.starts, s32[3]{0:T(128)S(1)} %fusion.1.picks.starts, bf16[4,272,8192]{2,1,0:T(8,128)(2,1)} %bitcast.68, bf16[4,272,8192]{2,1,0:T(8,128)(2,1)} %bitcast.69, bf16[4,272,8192]{2,1,0:T(8,128)(2,1)} %bitcast.70, ...), custom_call_target="tpu_custom_call" | custom-call | tf_op jit(solution)/shard_map/pallas_call | solution.py:218
  18.3 1.6 %collective-permute-start.4 = (s16[4224,128]{1,0:T(8,128)(2,1)S(1)}, s16[4224,128]{1,0:T(8,128)(2,1)S(1)}, u32[]{:S(2)}, u32[]{:S(2)}) collective-permute-start(s16[4224,128]{1,0:T(8,128)(2,1)S(1)} %shard_map.69.refs_6_), channel_id=1, source_target_pairs={{0,16},{8,24},{16,0},{24,8},{1,17},{9,25},{17,1},{25,9},{2,18},{10... | collective-permute-start | bytes 3244040 | tf_op jit(solution)/shard_map/ppermute | solution.py:375
  19.9 8.1 %shard_map.70 = (s16[4112,128]{1,0:T(8,128)(2,1)S(1)}, s16[4112,128]{1,0:T(8,128)(2,1)S(1)}) custom-call(s32[16]{0:T(128)S(1)} %fusion.order, s32[3]{0:T(128)S(1)} %fusion.1.picks.starts, s32[3]{0:T(128)S(1)} %fusion.1.picks.starts, bf16[4,272,8192]{2,1,0:T(8,128)(2,1)} %bitcast.71, bf16[4,272,8192]{2,1,0:T(8,128)(2,1)} %bitcast.72, ...), custom_call_target="tpu_custom_call" | custom-call | tf_op jit(solution)/shard_map/pallas_call | solution.py:218
  28.0 0.1 collective-permute-start.3
  28.1 0.5 collective-permute-start.2
  28.6 2.2 %collective-permute-done.3.refs_6_ = s16[4112,128]{1,0:T(8,128)(2,1)S(1)} collective-permute-done((s16[4112,128]{1,0:T(8,128)(2,1)S(1)}, s16[4112,128]{1,0:T(8,128)(2,1)S(1)}, u32[]{:S(2)}, u32[]{:S(2)}) %collective-permute-start.3) | collective-permute-done | bytes 1052704 | tf_op jit(solution)/shard_map/ppermute | solution.py:372
  30.7 5.1 %shard_map.71.refs_7_.refs_0_ = s16[4192,128]{1,0:T(8,128)(2,1)S(1)} custom-call(s32[16]{0:T(128)S(1)} %fusion.order, s32[3]{0:T(128)S(1)} %fusion.1.picks.starts, s32[3]{0:T(128)S(1)} %fusion.1.picks.starts, bf16[4,272,8192]{2,1,0:T(8,128)(2,1)} %bitcast.74, bf16[4,272,8192]{2,1,0:T(8,128)(2,1)} %bitcast.75, bf16[4,272,8192]{2,1,0:T(8,128)(2,1)} %bitcast.76, ...), custom_call_target="tpu_custom_call" | custom-call | tf_op jit(solution)/shard_map/pallas_call | solution.py:218
  35.9 0.0 collective-permute-done.2.refs_6_
  35.9 3.7 %shard_map.72.kept_ref.refs_2_ = f32[1,1024,512]{2,1,0:T(8,128)S(1)} custom-call(s32[16]{0:T(128)S(1)} %fusion.order, s32[3]{0:T(128)S(1)} %fusion.1.picks.starts, s32[3]{0:T(128)S(1)} %fusion.1.picks.starts, bf16[4,272,8192]{2,1,0:T(8,128)(2,1)} %bitcast.77, bf16[4,272,8192]{2,1,0:T(8,128)(2,1)} %bitcast.78, bf16[4,272,8192]{2,1,0:T(8,128)(2,1)} %bitcast.79, ...), custom_call_target="tpu_custom_call" | custom-call | tf_op jit(solution)/shard_map/pallas_call | solution.py:218
  39.6 0.0 copy-start.5
  39.6 1.3 %copy-done.5 = f32[1,1024,512]{2,1,0:T(8,128)} copy-done((f32[1,1024,512]{2,1,0:T(8,128)}, f32[1,1024,512]{2,1,0:T(8,128)S(1)}, u32[]{:S(2)}) %copy-start.5) | copy-done | bytes 2097176
  40.9 2.7 %collective-permute-done.refs_1_ = bf16[1296,512]{1,0:T(8,128)(2,1)S(1)} collective-permute-done((bf16[1296,512]{1,0:T(8,128)(2,1)S(1)}, bf16[1296,512]{1,0:T(8,128)(2,1)S(1)}, u32[]{:S(2)}, u32[]{:S(2)}) %collective-permute-start) | collective-permute-done | bytes 1327136 | tf_op jit(solution)/shard_map/ppermute | solution.py:381
  43.6 0.0 collective-permute-done.8.refs_3_.refs_0_
  43.6 0.8 collective-permute-done.4.refs_0_.refs_1_.refs_4_
  44.4 1.4 %collective-permute-start.9 = (bf16[1040,512]{1,0:T(8,128)(2,1)S(1)}, bf16[1040,512]{1,0:T(8,128)(2,1)S(1)}, u32[]{:S(2)}, u32[]{:S(2)}) collective-permute-start(bf16[1040,512]{1,0:T(8,128)(2,1)S(1)} %shard_map.77), channel_id=1, source_target_pairs={{2,0},{4,2},{6,4},{3,1},{5,3},{7,5},{10,8},{12,10},{14,12},{11,9},... | collective-permute-start | bytes 3194888 | tf_op jit(solution)/shard_map/ppermute | solution.py:381
  45.8 1.6 %collective-permute-start.6 = (s16[4192,128]{1,0:T(8,128)(2,1)S(1)}, s16[4192,128]{1,0:T(8,128)(2,1)}, u32[]{:S(2)}, u32[]{:S(2)}) collective-permute-start(s16[4192,128]{1,0:T(8,128)(2,1)S(1)} %shard_map.76), channel_id=1, source_target_pairs={{0,16},{8,24},{16,0},{24,8},{1,17},{9,25},{17,1},{25,9},{2,18},{10... | collective-permute-start | bytes 3219464 | tf_op jit(solution)/shard_map/ppermute | solution.py:375
  47.4 3.0 %shard_map.73.refs_6_ = s16[4192,128]{1,0:T(8,128)(2,1)} custom-call(f32[1,1024,512]{2,1,0:T(8,128)S(1)} %copy-done.6, s16[4224,128]{1,0:T(8,128)(2,1)S(1)} %collective-permute-done.4.refs_0_.refs_1_.refs_4_), custom_call_target="tpu_custom_call" | custom-call | tf_op jit(solution)/shard_map/pallas_call | solution.py:115
  50.4 1.3 %collective-permute-start.7 = (s16[4192,128]{1,0:T(8,128)(2,1)}, s16[4192,128]{1,0:T(8,128)(2,1)}, u32[]{:S(2)}, u32[]{:S(2)}) collective-permute-start(s16[4192,128]{1,0:T(8,128)(2,1)} %shard_map.73.refs_6_), channel_id=1, source_target_pairs={{0,1},{1,0},{2,3},{3,2},{4,5},{5,4},{6,7},{7,6},{8,9},{9,8},{10,11... | collective-permute-start | bytes 3219464 | tf_op jit(solution)/shard_map/ppermute | solution.py:378
  51.7 5.7 %shard_map.74 = s16[4112,128]{1,0:T(8,128)(2,1)} custom-call(s32[16]{0:T(128)S(1)} %fusion.order, s32[3]{0:T(128)S(1)} %fusion.1.picks.starts, s32[3]{0:T(128)S(1)} %fusion.1.picks.starts, bf16[4,272,8192]{2,1,0:T(8,128)(2,1)} %bitcast.80, bf16[4,272,8192]{2,1,0:T(8,128)(2,1)} %bitcast.81, bf16[4,272,8192]{2,1,0:T(8,128)(2,1)} %bitcast.82, ...), custom_call_target="tpu_custom_call" | custom-call | tf_op jit(solution)/shard_map/pallas_call | solution.py:218
  57.4 1.1 slice.16.refs_0_
  58.5 0.5 collective-permute-start.10
  59.0 12.5 %collective-permute-done.9.refs_2_.refs_1_.refs_0_ = bf16[1040,512]{1,0:T(8,128)(2,1)S(1)} collective-permute-done((bf16[1040,512]{1,0:T(8,128)(2,1)S(1)}, bf16[1040,512]{1,0:T(8,128)(2,1)S(1)}, u32[]{:S(2)}, u32[]{:S(2)}) %collective-permute-start.9) | collective-permute-done | bytes 1064992 | tf_op jit(solution)/shard_map/ppermute | solution.py:381
  71.5 1.3 %collective-permute-start.13 = (bf16[1296,512]{1,0:T(8,128)(2,1)}, bf16[1296,512]{1,0:T(8,128)(2,1)}, u32[]{:S(2)}, u32[]{:S(2)}) collective-permute-start(bf16[1296,512]{1,0:T(8,128)(2,1)} %shard_map.81), channel_id=1, source_target_pairs={{2,0},{4,2},{6,4},{3,1},{5,3},{7,5},{10,8},{12,10},{14,12},{11,9},... | collective-permute-start | bytes 3981320 | tf_op jit(solution)/shard_map/ppermute | solution.py:381
  72.8 0.1 pad_add_fusion.2.starts
  72.9 1.0 slice.14.current_ref
  73.9 2.1 %slice.15.refs_4_.refs_0_ = bf16[768,512]{1,0:T(8,128)(2,1)} slice(bf16[1296,512]{1,0:T(8,128)(2,1)} %copy-done.7), slice={[0:768], [0:512]} | slice | bytes 1572864 | tf_op jit(solution)/shard_map/slice | solution.py:459
  75.9 4.2 %shard_map.75.refs_2_.kept_ref = f32[1,1024,512]{2,1,0:T(8,128)S(1)} custom-call(s32[16]{0:T(128)S(1)} %fusion.order, s32[3]{0:T(128)S(1)} %fusion.1.picks.starts, s32[3]{0:T(128)S(1)} %fusion.1.picks.starts, bf16[4,272,8192]{2,1,0:T(8,128)(2,1)} %bitcast.83, bf16[4,272,8192]{2,1,0:T(8,128)(2,1)} %bitcast.84, bf16[4,272,8192]{2,1,0:T(8,128)(2,1)} %bitcast.85, ...), custom_call_target="tpu_custom_call" | custom-call | tf_op jit(solution)/shard_map/pallas_call | solution.py:218
  80.1 0.0 copy-start.4
  80.1 0.0 collective-permute-done.10.refs_1_
  80.1 3.8 %shard_map.78 = (bf16[272,8192]{1,0:T(8,128)(2,1)}, f32[8,128]{1,0:T(8,128)S(1)}) custom-call(s32[2]{0:T(128)S(1)} %pad_add_fusion.2.starts, bf16[272,512]{1,0:T(8,128)(2,1)S(1)} %slice.14.current_ref, bf16[1024,512]{1,0:T(8,128)(2,1)} %slice.16.refs_0_, bf16[1024,512]{1,0:T(8,128)(2,1)} %collective-permute-done.10.refs_1_, ...), custom_call_target="tpu_custom_call" | custom-call | tf_op jit(solution)/shard_map/pallas_call | solution.py:282
  84.0 0.0 collective-permute-done.6.refs_0_
  84.0 0.0 collective-permute-done.7.refs_1_
  84.0 4.6 %shard_map.79.refs_1_.refs_0_ = s16[4128,128]{1,0:T(8,128)(2,1)S(1)} custom-call(f32[1,1024,512]{2,1,0:T(8,128)} %copy-done.4, s16[4192,128]{1,0:T(8,128)(2,1)} %collective-permute-done.6.refs_0_, s16[4192,128]{1,0:T(8,128)(2,1)} %collective-permute-done.7.refs_1_, bf16[1040,512]{1,0:T(8,128)(2,1)S(1)} %collective-permute-done.9.refs_2_.refs_1_.refs_0_, ...), custom_call_target="tpu_custom_call" | custom-call | tf_op jit(solution)/shard_map/pallas_call | solution.py:115
  88.6 0.1 collective-permute-start.15
  88.7 0.5 collective-permute-start.16
  89.2 1.5 %collective-permute-start.17 = (s16[4128,128]{1,0:T(8,128)(2,1)S(1)}, s16[4128,128]{1,0:T(8,128)(2,1)S(1)}, u32[]{:S(2)}, u32[]{:S(2)}) collective-permute-start(s16[4128,128]{1,0:T(8,128)(2,1)S(1)} %shard_map.79.refs_1_.refs_0_), channel_id=1, source_target_pairs={{0,16},{8,24},{16,0},{24,8},{1,17},{9,25},{17,1},{25,9},{2,18},{10... | collective-permute-start | bytes 3170312 | tf_op jit(solution)/shard_map/ppermute | solution.py:375
  90.7 1.0 collective-permute-start.11
  91.7 11.5 %collective-permute-done.13.refs_0_ = bf16[1296,512]{1,0:T(8,128)(2,1)} collective-permute-done((bf16[1296,512]{1,0:T(8,128)(2,1)}, bf16[1296,512]{1,0:T(8,128)(2,1)}, u32[]{:S(2)}, u32[]{:S(2)}) %collective-permute-start.13) | collective-permute-done | bytes 1327136 | tf_op jit(solution)/shard_map/ppermute | solution.py:381
  103.3 0.0 collective-permute-start.14
  103.3 0.1 pad_add_fusion.4.starts
  103.3 0.1 pad_add_fusion.5.place
  103.4 0.0 collective-permute-done.16.refs_1_
  103.4 4.0 %shard_map.83 = (f32[4,1024,512]{2,1,0:T(8,128)}, f32[8,128]{1,0:T(8,128)S(1)}) custom-call(s32[2]{0:T(128)S(1)} %pad_add_fusion.5.place, s16[4128,128]{1,0:T(8,128)(2,1)S(1)} %shard_map.79.refs_1_.refs_0_, s16[4128,128]{1,0:T(8,128)(2,1)} %collective-permute-done.16.refs_1_), custom_call_target="tpu_custom_call" | custom-call | tf_op jit(solution)/shard_map/pallas_call | solution.py:338
  107.4 3.4 %shard_map.84 = (bf16[272,8192]{1,0:T(8,128)(2,1)}, f32[8,128]{1,0:T(8,128)S(1)}) custom-call(s32[2]{0:T(128)S(1)} %pad_add_fusion.4.starts, bf16[272,512]{1,0:T(8,128)(2,1)S(1)} %slice.14.current_ref, bf16[1040,512]{1,0:T(8,128)(2,1)S(1)} %shard_map.82.refs_0_, bf16[1040,512]{1,0:T(8,128)(2,1)} %collective-permute-done.15.refs_1_, ...), custom_call_target="tpu_custom_call", output_to_operand_aliasing={{0}: (4, {})} | custom-call | tf_op jit(solution)/shard_map/pallas_call | solution.py:282
  110.8 3.6 %collective-permute-done.17.refs_0_ = s16[4128,128]{1,0:T(8,128)(2,1)S(1)} collective-permute-done((s16[4128,128]{1,0:T(8,128)(2,1)S(1)}, s16[4128,128]{1,0:T(8,128)(2,1)S(1)}, u32[]{:S(2)}, u32[]{:S(2)}) %collective-permute-start.17) | collective-permute-done | bytes 1056800 | tf_op jit(solution)/shard_map/ppermute | solution.py:375
  114.5 0.5 collective-permute-start.12
  115.0 0.1 pad_add_fusion.starts
  115.1 0.1 pad_add_fusion.3.starts
  115.1 0.1 pad_add_fusion.6.place
  115.2 4.1 %shard_map.85 = (bf16[272,8192]{1,0:T(8,128)(2,1)}, f32[8,128]{1,0:T(8,128)S(1)}) custom-call(s32[2]{0:T(128)S(1)} %pad_add_fusion.3.starts, bf16[272,512]{1,0:T(8,128)(2,1)S(1)} %slice.14.current_ref, bf16[1296,512]{1,0:T(8,128)(2,1)} %collective-permute-done.13.refs_0_, ...), custom_call_target="tpu_custom_call", output_to_operand_aliasing={{0}: (4, {})} | custom-call | tf_op jit(solution)/shard_map/pallas_call | solution.py:282
  119.3 3.7 %shard_map.86 = (bf16[272,8192]{1,0:T(8,128)(2,1)}, f32[8,128]{1,0:T(8,128)}) custom-call(s32[2]{0:T(128)S(1)} %pad_add_fusion.starts, bf16[272,512]{1,0:T(8,128)(2,1)S(1)} %slice.14.current_ref, bf16[768,512]{1,0:T(8,128)(2,1)} %collective-permute-done.11.refs_0_, ...), custom_call_target="tpu_custom_call", output_to_operand_aliasing={{0}: (4, {})} | custom-call | tf_op jit(solution)/shard_map/pallas_call | solution.py:282
  123.0 0.0 copy-start.1
  123.0 3.4 %shard_map.88 = (f32[4,1024,512]{2,1,0:T(8,128)}, f32[8,128]{1,0:T(8,128)}) custom-call(s32[2]{0:T(128)S(1)} %pad_add_fusion.6.place, s16[4128,128]{1,0:T(8,128)(2,1)S(1)} %shard_map.87.refs_0_, s16[4128,128]{1,0:T(8,128)(2,1)S(1)} %collective-permute-done.18.refs_1_, f32[4,1024,512]{2,1,0:T(8,128)} %get-tuple-element.31.refs_2_, ...), custom_call_target="tpu_custom_call", output_to_operand_aliasing={{0}: (3, {})} | custom-call | tf_op jit(solution)/shard_map/pallas_call | solution.py:338
  (36 shorter events, 0.1 us)
Async XLA Ops:
  0.6 1.0 copy-start
  2.5 1.3 copy-start.2
  3.8 9.5 %copy-start.3 = (bf16[1,1,4,272,512]{4,3,2,1,0:T(8,128)(2,1)S(1)}, bf16[1,1,4,272,512]{4,3,2,1,0:T(8,128)(2,1)}, u32[]{:S(2)}) copy-start(bf16[1,1,4,272,512]{4,3,2,1,0:T(8,128)(2,1)} %param.6) | copy-start | bytes 3342340
  8.8 4.4 %collective-permute-start.1 = (s16[4112,128]{1,0:T(8,128)(2,1)S(1)}, s16[4112,128]{1,0:T(8,128)(2,1)S(1)}, u32[]{:S(2)}, u32[]{:S(2)}) collective-permute-start(s16[4112,128]{1,0:T(8,128)(2,1)S(1)} %get-tuple-element.19), channel_id=1, source_target_pairs={{0,8},{8,0},{16,24},{24,16},{1,9},{9,1},{17,25},{25,17},{2,10},{10... | collective-permute-start | bytes 3158024 | tf_op jit(solution)/shard_map/ppermute | solution.py:372
  9.3 34.3 %collective-permute-start = (bf16[1296,512]{1,0:T(8,128)(2,1)S(1)}, bf16[1296,512]{1,0:T(8,128)(2,1)S(1)}, u32[]{:S(2)}, u32[]{:S(2)}) collective-permute-start(bf16[1296,512]{1,0:T(8,128)(2,1)S(1)} %get-tuple-element.18), channel_id=1, source_target_pairs={{2,0},{4,2},{6,4},{3,1},{5,3},{7,5},{10,8},{12,10},{14,12},{11,9},... | collective-permute-start | bytes 3981320 | tf_op jit(solution)/shard_map/ppermute | solution.py:381
  10.6 33.0 %collective-permute-start.8 = (bf16[1296,512]{1,0:T(8,128)(2,1)S(1)}, bf16[1296,512]{1,0:T(8,128)(2,1)}, u32[]{:S(2)}, u32[]{:S(2)}) collective-permute-start(bf16[1296,512]{1,0:T(8,128)(2,1)S(1)} %get-tuple-element.23), channel_id=1, source_target_pairs={{0,1},{1,0},{2,3},{3,2},{4,5},{5,4},{6,7},{7,6},{8,9},{9,8},{10,11... | collective-permute-start | bytes 3981320 | tf_op jit(solution)/shard_map/ppermute | solution.py:378
  18.3 26.0 %collective-permute-start.4 = (s16[4224,128]{1,0:T(8,128)(2,1)S(1)}, s16[4224,128]{1,0:T(8,128)(2,1)S(1)}, u32[]{:S(2)}, u32[]{:S(2)}) collective-permute-start(s16[4224,128]{1,0:T(8,128)(2,1)S(1)} %shard_map.69.refs_6_), channel_id=1, source_target_pairs={{0,16},{8,24},{16,0},{24,8},{1,17},{9,25},{17,1},{25,9},{2,18},{10... | collective-permute-start | bytes 3244040 | tf_op jit(solution)/shard_map/ppermute | solution.py:375
  28.0 2.7 %collective-permute-start.3 = (s16[4112,128]{1,0:T(8,128)(2,1)S(1)}, s16[4112,128]{1,0:T(8,128)(2,1)S(1)}, u32[]{:S(2)}, u32[]{:S(2)}) collective-permute-start(s16[4112,128]{1,0:T(8,128)(2,1)S(1)} %get-tuple-element.21), channel_id=1, source_target_pairs={{0,8},{8,0},{16,24},{24,16},{1,9},{9,1},{17,25},{25,17},{2,10},{10... | collective-permute-start | bytes 3158024 | tf_op jit(solution)/shard_map/ppermute | solution.py:372
  28.1 7.8 %collective-permute-start.2 = (s16[4112,128]{1,0:T(8,128)(2,1)S(1)}, s16[4112,128]{1,0:T(8,128)(2,1)S(1)}, u32[]{:S(2)}, u32[]{:S(2)}) collective-permute-start(s16[4112,128]{1,0:T(8,128)(2,1)S(1)} %get-tuple-element.20), channel_id=1, source_target_pairs={{0,8},{8,0},{16,24},{24,16},{1,9},{9,1},{17,25},{25,17},{2,10},{10... | collective-permute-start | bytes 3158024 | tf_op jit(solution)/shard_map/ppermute | solution.py:372
  39.6 1.3 %copy-start.5 = (f32[1,1024,512]{2,1,0:T(8,128)}, f32[1,1024,512]{2,1,0:T(8,128)S(1)}, u32[]{:S(2)}) copy-start(f32[1,1024,512]{2,1,0:T(8,128)S(1)} %shard_map.72.kept_ref.refs_2_) | copy-start | bytes 6291460
  43.6 13.8 %copy-start.7 = (bf16[1296,512]{1,0:T(8,128)(2,1)}, bf16[1296,512]{1,0:T(8,128)(2,1)S(1)}, u32[]{:S(2)}) copy-start(bf16[1296,512]{1,0:T(8,128)(2,1)S(1)} %collective-permute-done.refs_1_) | copy-start | bytes 3981316
  44.4 3.0 %copy-start.6 = (f32[1,1024,512]{2,1,0:T(8,128)S(1)}, f32[1,1024,512]{2,1,0:T(8,128)}, u32[]{:S(2)}) copy-start(f32[1,1024,512]{2,1,0:T(8,128)} %copy-done.5) | copy-start | bytes 6291460
  44.4 27.1 %collective-permute-start.9 = (bf16[1040,512]{1,0:T(8,128)(2,1)S(1)}, bf16[1040,512]{1,0:T(8,128)(2,1)S(1)}, u32[]{:S(2)}, u32[]{:S(2)}) collective-permute-start(bf16[1040,512]{1,0:T(8,128)(2,1)S(1)} %shard_map.77), channel_id=1, source_target_pairs={{2,0},{4,2},{6,4},{3,1},{5,3},{7,5},{10,8},{12,10},{14,12},{11,9},... | collective-permute-start | bytes 3194888 | tf_op jit(solution)/shard_map/ppermute | solution.py:381
  45.8 38.2 %collective-permute-start.6 = (s16[4192,128]{1,0:T(8,128)(2,1)S(1)}, s16[4192,128]{1,0:T(8,128)(2,1)}, u32[]{:S(2)}, u32[]{:S(2)}) collective-permute-start(s16[4192,128]{1,0:T(8,128)(2,1)S(1)} %shard_map.76), channel_id=1, source_target_pairs={{0,16},{8,24},{16,0},{24,8},{1,17},{9,25},{17,1},{25,9},{2,18},{10... | collective-permute-start | bytes 3219464 | tf_op jit(solution)/shard_map/ppermute | solution.py:375
  50.4 33.6 %collective-permute-start.7 = (s16[4192,128]{1,0:T(8,128)(2,1)}, s16[4192,128]{1,0:T(8,128)(2,1)}, u32[]{:S(2)}, u32[]{:S(2)}) collective-permute-start(s16[4192,128]{1,0:T(8,128)(2,1)} %shard_map.73.refs_6_), channel_id=1, source_target_pairs={{0,1},{1,0},{2,3},{3,2},{4,5},{5,4},{6,7},{7,6},{8,9},{9,8},{10,11... | collective-permute-start | bytes 3219464 | tf_op jit(solution)/shard_map/ppermute | solution.py:378
  57.4 18.5 %collective-permute-start.5 = (s16[4112,128]{1,0:T(8,128)(2,1)}, s16[4112,128]{1,0:T(8,128)(2,1)}, u32[]{:S(2)}, u32[]{:S(2)}) collective-permute-start(s16[4112,128]{1,0:T(8,128)(2,1)} %shard_map.74), channel_id=1, source_target_pairs={{0,8},{8,0},{16,24},{24,16},{1,9},{9,1},{17,25},{25,17},{2,10},{10... | collective-permute-start | bytes 3158024 | tf_op jit(solution)/shard_map/ppermute | solution.py:372
  58.5 21.6 %collective-permute-start.10 = (bf16[1024,512]{1,0:T(8,128)(2,1)}, bf16[1024,512]{1,0:T(8,128)(2,1)}, u32[]{:S(2)}, u32[]{:S(2)}) collective-permute-start(bf16[1024,512]{1,0:T(8,128)(2,1)} %slice.16.refs_0_), channel_id=1, source_target_pairs={{0,8},{8,0},{16,24},{24,16},{1,9},{9,1},{17,25},{25,17},{2,10},{10... | collective-permute-start | bytes 3145736 | tf_op jit(solution)/shard_map/ppermute | solution.py:372
  71.5 31.8 %collective-permute-start.13 = (bf16[1296,512]{1,0:T(8,128)(2,1)}, bf16[1296,512]{1,0:T(8,128)(2,1)}, u32[]{:S(2)}, u32[]{:S(2)}) collective-permute-start(bf16[1296,512]{1,0:T(8,128)(2,1)} %shard_map.81), channel_id=1, source_target_pairs={{2,0},{4,2},{6,4},{3,1},{5,3},{7,5},{10,8},{12,10},{14,12},{11,9},... | collective-permute-start | bytes 3981320 | tf_op jit(solution)/shard_map/ppermute | solution.py:381
  80.1 3.9 %copy-start.4 = (f32[1,1024,512]{2,1,0:T(8,128)}, f32[1,1024,512]{2,1,0:T(8,128)S(1)}, u32[]{:S(2)}) copy-start(f32[1,1024,512]{2,1,0:T(8,128)S(1)} %shard_map.75.refs_2_.kept_ref) | copy-start | bytes 6291460
  88.6 18.9 %collective-permute-start.15 = (bf16[1040,512]{1,0:T(8,128)(2,1)S(1)}, bf16[1040,512]{1,0:T(8,128)(2,1)}, u32[]{:S(2)}, u32[]{:S(2)}) collective-permute-start(bf16[1040,512]{1,0:T(8,128)(2,1)S(1)} %shard_map.82.refs_0_), channel_id=1, source_target_pairs={{0,8},{8,0},{16,24},{24,16},{1,9},{9,1},{17,25},{25,17},{2,10},{10... | collective-permute-start | bytes 3194888 | tf_op jit(solution)/shard_map/ppermute | solution.py:372
  88.7 14.8 %collective-permute-start.16 = (s16[4128,128]{1,0:T(8,128)(2,1)S(1)}, s16[4128,128]{1,0:T(8,128)(2,1)}, u32[]{:S(2)}, u32[]{:S(2)}) collective-permute-start(s16[4128,128]{1,0:T(8,128)(2,1)S(1)} %shard_map.79.refs_1_.refs_0_), channel_id=1, source_target_pairs={{0,8},{8,0},{16,24},{24,16},{1,9},{9,1},{17,25},{25,17},{2,10},{10... | collective-permute-start | bytes 3170312 | tf_op jit(solution)/shard_map/ppermute | solution.py:372
  89.2 25.3 %collective-permute-start.17 = (s16[4128,128]{1,0:T(8,128)(2,1)S(1)}, s16[4128,128]{1,0:T(8,128)(2,1)S(1)}, u32[]{:S(2)}, u32[]{:S(2)}) collective-permute-start(s16[4128,128]{1,0:T(8,128)(2,1)S(1)} %shard_map.79.refs_1_.refs_0_), channel_id=1, source_target_pairs={{0,16},{8,24},{16,0},{24,8},{1,17},{9,25},{17,1},{25,9},{2,18},{10... | collective-permute-start | bytes 3170312 | tf_op jit(solution)/shard_map/ppermute | solution.py:375
  90.7 23.8 %collective-permute-start.11 = (bf16[768,512]{1,0:T(8,128)(2,1)}, bf16[768,512]{1,0:T(8,128)(2,1)}, u32[]{:S(2)}, u32[]{:S(2)}) collective-permute-start(bf16[768,512]{1,0:T(8,128)(2,1)} %shard_map.80), channel_id=1, source_target_pairs={{0,1},{1,0},{2,3},{3,2},{4,5},{5,4},{6,7},{7,6},{8,9},{9,8},{10,11... | collective-permute-start | bytes 2359304 | tf_op jit(solution)/shard_map/ppermute | solution.py:378
  103.3 12.0 %collective-permute-start.14 = (bf16[1296,512]{1,0:T(8,128)(2,1)}, bf16[1296,512]{1,0:T(8,128)(2,1)}, u32[]{:S(2)}, u32[]{:S(2)}) collective-permute-start(bf16[1296,512]{1,0:T(8,128)(2,1)} %collective-permute-done.13.refs_0_), channel_id=1, source_target_pairs={{0,8},{8,0},{16,24},{24,16},{1,9},{9,1},{17,25},{25,17},{2,10},{10... | collective-permute-start | bytes 3981320 | tf_op jit(solution)/shard_map/ppermute | solution.py:372
  114.5 8.5 %collective-permute-start.18 = (s16[4128,128]{1,0:T(8,128)(2,1)S(1)}, s16[4128,128]{1,0:T(8,128)(2,1)S(1)}, u32[]{:S(2)}, u32[]{:S(2)}) collective-permute-start(s16[4128,128]{1,0:T(8,128)(2,1)S(1)} %shard_map.87.refs_0_), channel_id=1, source_target_pairs={{0,8},{8,0},{16,24},{24,16},{1,9},{9,1},{17,25},{25,17},{2,10},{10... | collective-permute-start | bytes 3170312 | tf_op jit(solution)/shard_map/ppermute | solution.py:372
  114.5 4.8 %collective-permute-start.12 = (bf16[768,512]{1,0:T(8,128)(2,1)}, bf16[768,512]{1,0:T(8,128)(2,1)S(1)}, u32[]{:S(2)}, u32[]{:S(2)}) collective-permute-start(bf16[768,512]{1,0:T(8,128)(2,1)} %collective-permute-done.11.refs_0_), channel_id=1, source_target_pairs={{0,8},{8,0},{16,24},{24,16},{1,9},{9,1},{17,25},{25,17},{2,10},{10... | collective-permute-start | bytes 2359304 | tf_op jit(solution)/shard_map/ppermute | solution.py:372
  123.0 3.4 %copy-start.1 = (s32[8]{0:T(128)S(1)}, s32[8]{0:T(128)}, u32[]{:S(2)}) copy-start(s32[8]{0:T(128)} %param.9) | copy-start | bytes 100

commit v3 on v2

--- a/solution.py
+++ b/solution.py
@@ -10,7 +10,6 @@
 
 LANES = 128
 TAIL = 16
-MORE = 16
 FAR_TAILS = 8
 SIDE_TAILS = 6
 DONE = jax.ShapeDtypeStruct((8, LANES), jnp.float32)
@@ -245,33 +244,34 @@
     )
 
 
-def key_kernel(starts, current_ref, *refs, count, skip, rows):
-    out_ref, done_ref, block_ref, sem = refs[-4:]
-    step = min(rows, 512)
+def key_kernel(starts, current_ref, *refs, segments):
+    out_ref, done_ref = refs[len(refs) - len(segments) - 3 : len(refs) - len(segments) - 1]
+    blocks, sem = refs[len(refs) - len(segments) - 1 : -1], refs[-1]
     copies = []
-    for n in range(count):
-        place = pl.multiple_of(starts[n], LANES)
+    for n, (skip, rows) in enumerate(segments):
+        step = min(rows, 512)
         for at in range(0, rows, step):
             size = min(step, rows - at)
-            block_ref[n, :, at : at + size] = lax.dot_general(
+            blocks[n][:, at : at + size] = lax.dot_general(
                 current_ref[...],
                 refs[n][skip + at : skip + at + size, :],
                 (((1,), (1,)), ((), ())),
                 preferred_element_type=jnp.float32,
             ).astype(out_ref.dtype)
-        copies.append(pltpu.make_async_copy(block_ref.at[n], out_ref.at[:, pl.ds(place, rows)], sem.at[n]))
+        place = pl.ds(pl.multiple_of(starts[n], LANES), rows)
+        copies.append(pltpu.make_async_copy(blocks[n], out_ref.at[:, place], sem.at[n]))
         copies[-1].start()
     done_ref[...] = jnp.zeros_like(done_ref)
     for c in copies:
         c.wait()
 
 
-def key_products(starts, current, parts, skip, rows, features, held, *waits):
+def key_products(current, parts, features, held, *waits):
     tokens, width = current.shape
-    count = len(parts)
+    arrays = [x for x, _, _, _ in parts]
     anywhere = pl.BlockSpec(memory_space=pltpu.HBM)
-    in_specs = [pl.BlockSpec(x.shape, lambda i, p: (0, 0)) for x in (current, *parts)]
-    operands = [starts, current, *parts]
+    in_specs = [pl.BlockSpec(x.shape, lambda i, p: (0, 0)) for x in (current, *arrays)]
+    operands = [jnp.stack([start for _, _, _, start in parts]), current, *arrays]
     aliases = {}
     if held is not None:
         in_specs.append(anywhere)
@@ -280,14 +280,15 @@
     in_specs += [pl.BlockSpec(memory_space=pl.ANY) for _ in waits]
     operands += waits
     return pl.pallas_call(
-        functools.partial(key_kernel, count=count, skip=skip, rows=rows),
+        functools.partial(key_kernel, segments=[(skip, rows) for _, skip, rows, _ in parts]),
         out_shape=[jax.ShapeDtypeStruct((tokens, features), jnp.bfloat16), DONE],
         grid_spec=pltpu.PrefetchScalarGridSpec(
             num_scalar_prefetch=1,
             grid=(1,),
             in_specs=in_specs,
             out_specs=[anywhere, pl.BlockSpec(DONE.shape, lambda i, p: (0, 0))],
-            scratch_shapes=[pltpu.VMEM((count, tokens, rows), jnp.bfloat16), pltpu.SemaphoreType.DMA((count,))],
+            scratch_shapes=[pltpu.VMEM((tokens, rows), jnp.bfloat16) for _, _, rows, _ in parts]
+            + [pltpu.SemaphoreType.DMA((len(parts),))],
         ),
         input_output_aliases=aliases,
         compiler_params=params(),
@@ -381,7 +382,6 @@
         return lax.ppermute(value, "pipe", [(d, d - 1) for d in range(1, n_pipe)])
 
     half = weight.shape[0] // INNER
-    part = half // 2
     late_part = max(half * 3 // 8 // LANES, 1) * LANES
 
     position = jnp.arange(micro - 1, dtype=jnp.int32)
@@ -416,7 +416,7 @@
             order, first[name, ki], len(wanted), picks, stored, grads, block, rows, coded, codes, *waits, **more
         )
 
-    *far_sent, own_first, own_most, own_second = products(
+    *far_sent, own_all, own_most = products(
         "far",
         1,
         far,
@@ -424,12 +424,11 @@
         [],
         sources=(weight, grads.reshape(micro * tokens, width)),
         moves=(
-            [(0, me_i * half, part), (1, slot * tokens, tokens)],
-            [(0, me_i * half + late_part - MORE, half - late_part + MORE)],
-            [(0, me_i * half + part - MORE, half - part + MORE)],
+            [(0, me_i * half, half), (1, slot * tokens, tokens)],
+            [(0, me_i * half + late_part, half - late_part)],
         ),
     )
-    z_first = to_previous(own_first)
+    z_all = to_previous(own_all)
     crossed_most = [to_ctx(own_most, kx) for kx in range(1, n_ctx)]
     coded = dict(zip(far, products("far", 0, far, True, [swap(c) for c in far_sent], tails=FAR_TAILS)))
     got = {w: to_outer(coded[w], w[1]) for w in far}
@@ -441,25 +440,32 @@
 
     passed = passed_done = None
 
-    def pass_on(kx, start, count, held, skip, *waits):
+    def pass_on(kx, start, count, held, skip, *waits, cuts=1):
         nonlocal passed, passed_done
         row = ((section - kx) % n_ctx) * weight.shape[0] + start
-        starts = jnp.stack([row + me_i * half, row + (me_i + 1) % INNER * half])
-        passed, passed_done = key_products(starts, current, [held, swap(held)], skip, count, features, passed, *waits)
+        parts = [(held, skip, count, row + me_i * half)]
+        theirs = row + (me_i + 1) % INNER * half
+        if cuts == 1:
+            parts.append((swap(held), skip, count, theirs))
+        at = 0
+        while cuts > 1 and at < count:
+            size = min(-(-count // cuts // LANES) * LANES, count - at)
+            parts.append((swap(lax.slice_in_dim(held, skip + at, skip + at + size)), 0, size, theirs + at))
+            at += size
+        passed, passed_done = key_products(current, parts, features, passed, *waits)
 
     crossed = []
     for n, (kx, _) in enumerate(side):
-        value = combine(side_sums, n, [got[kx, ko] for ko in range(1, outer)], tails=SIDE_TAILS)
+        value = combine(side_sums, n, [got[kx, ko] for ko in range(1, outer)], *crossed_most, tails=SIDE_TAILS)
         crossed.append(to_ctx(value, kx))
-    z_second = to_previous(after(own_second, z_first, side_sums, *crossed_most, *[got[w] for w in far]))
-    home_theirs = swap(products("home", 1, home, True, [], value)[0])
+    home_sent = products("home", 1, home, True, [], value)
+    home_theirs = swap(home_sent[0])
     (home_sum,) = products("home", 0, home, False, [home_theirs])
-    current = lax.slice_in_dim(z_first, part, part + tokens)
-    next_first = lax.slice_in_dim(z_first, 0, part)
-    next_late = lax.slice_in_dim(z_first, 0, late_part)
-    pass_on(0, 0, part, next_first, 0, home_sum)
-    z_crossed = [to_previous(after(c, z_second)) for c in crossed_most]
-    own = combine(home_sum, 0, [got[0, ko] for ko in range(1, outer)] + crossed, z_second, passed_done, next_late, tails=2)
+    z_crossed = [to_previous(after(c, home_sent[0])) for c in crossed_most]
+    current = lax.slice_in_dim(z_all, half, half + tokens)
+    next_late = lax.slice_in_dim(z_all, 0, late_part)
+    codes = [*[got[0, ko] for ko in range(1, outer)], *crossed]
+    own = combine(home_sum, 0, codes, current, next_late, tails=2)
     others = {ko: to_outer(own, ko) for ko in range(1, outer)}
     late = after(next_late, own)
     late = [to_ctx(late, kx) for kx in range(1, n_ctx)]
@@ -471,18 +477,19 @@
         width,
         None,
     )
-    pass_on(0, part, half - part, after(z_second, own), MORE, result_done)
+    pass_on(0, 0, half, after(z_all, own), 0, result_done, cuts=2)
     early_done = passed_done
     for kx in range(1, n_ctx):
-        pass_on(kx, late_part, half - late_part, z_crossed[kx - 1], MORE)
-    most_done = passed_done
-    for kx in range(1, n_ctx):
-        pass_on(kx, 0, late_part, late[kx - 1], 0)
+        pass_on(kx, late_part, half - late_part, after(z_crossed[kx - 1], early_done), 0, cuts=2)
+    theirs = []
     for ko in range(1, outer):
-        other = after(others[ko], early_done)
+        other = after(others[ko], passed_done, result_done, *late)
+        theirs.append(swap(other))
         o = (me_o - ko) % outer
         place = jnp.stack([o * INNER + me_i, o * INNER + (me_i + 1) % INNER])
-        result, _ = decode(place, [other, swap(other)], n_dp, rows, width, result, most_done)
+        result, _ = decode(place, [other, theirs[-1]], n_dp, rows, width, result)
+    for kx in range(1, n_ctx):
+        pass_on(kx, 0, late_part, after(late[kx - 1], *theirs), 0)
     return passed[None, None], result.reshape(1, n_dp * rows, width)
 
 

time: 128 us -> 120 us (0.938)
  Pallas kernels: 66.8 us -> 63.2 us
  starting transfers between devices: 16.3 us -> 14.1 us
  waiting for transfers between devices: 33.3 us -> 31.5 us
    ppermute x3 -> x2, waiting for transfers between devices: 26.7 us -> 17.8 us  [to_previous(): return lax.ppermute(value, 'pipe', [(d, d - 1) for d in range(1, n_pipe)])]
    ppermute x10 -> x11, waiting for transfers between devices: 2.18 us -> 7.68 us  [swap(): return lax.ppermute(value, 'dp', pairs)]
    pallas_call x4 -> x3, Pallas kernels: 14.9 us -> 11.8 us  [key_products(): pl.pallas_call(functools.partial(key_kernel, segments=[(skip, rows) for _...]
    pallas_call x2, Pallas kernels: 7.54 us -> 5.92 us  [combine(): pl.pallas_call(functools.partial(combine_kernel, n_codes=len(codes), rows...]
    ppermute x3, waiting for transfers between devices: 4.43 us -> 5.96 us  [to_outer(): lax.ppermute(value, 'dp', [(d, (d + by * INNER) % n_dp) for d in range(n_...]
    ppermute x3 -> x2, starting transfers between devices: 3.97 us -> 2.57 us  [to_previous(): return lax.ppermute(value, 'pipe', [(d, d - 1) for d in range(1, n_pipe)])]
    slice x3 -> x4, local copies, waits for them, and re-layouts: 4.14 us -> 4.72 us  [the longest x2 3.74 us: pass_on(): lax.slice_in_dim(held, skip + at, skip + at + size)]
    ppermute x10 -> x11, starting transfers between devices: 2.68 us -> 2.4 us  [swap(): return lax.ppermute(value, 'dp', pairs)]
  transfers between devices with their start and end apart: 19 -> 19, of which waited for: 6 -> 7; matrix products, arithmetic and copies ran while one was open for 4% -> 4% of each run, Pallas kernels for 46% -> 45%
where the time goes in v3:
time: 120 us; the launch traced here: 119 us
  Pallas kernels  63.2 us (53%)
  waiting for transfers between devices  31.5 us (26%)
  starting transfers between devices  14.1 us (12%)
  local copies, waits for them, and re-layouts  8.16 us (7%)
  between operations  1.79 us (1%)
    pallas_call x7, Pallas kernels, token_products(): pl.pallas_call(functools.partial(token_kernel, count=count, groups=groups...  36.9 us
    ppermute x2, waiting for transfers between devices, to_previous(): return lax.ppermute(value, 'pipe', [(d, d - 1) for d in range(1, n_pipe)])  17.8 us
    pallas_call x3, Pallas kernels, key_products(): pl.pallas_call(functools.partial(key_kernel, segments=[(skip, rows) for _...  11.8 us
    pallas_call x2, Pallas kernels, decode(): pl.pallas_call(functools.partial(decode_kernel, count=count, rows=rows, w...  8.62 us
    ppermute x11, waiting for transfers between devices, swap(): return lax.ppermute(value, 'dp', pairs)  7.68 us
    ppermute x3, waiting for transfers between devices, to_outer(): lax.ppermute(value, 'dp', [(d, (d + by * INNER) % n_dp) for d in range(n_...  5.96 us
    pallas_call x2, Pallas kernels, combine(): pl.pallas_call(functools.partial(combine_kernel, n_codes=len(codes), rows...  5.92 us
    ppermute x3, starting transfers between devices, to_outer(): lax.ppermute(value, 'dp', [(d, (d + by * INNER) % n_dp) for d in range(n_...  4.65 us
  transfers between devices with their start and end apart: 19, of which 7 were waited for; matrix products, arithmetic and copies ran while one was open for 4% of the time, Pallas kernels for 45%

profile of v3, /device:TPU:0, one launch (start us, length us, event | category | flops | bytes accessed | tf_op | source)
XLA Modules:
  0.0 119.2 jit_solution(3048439385830804786)
XLA Ops:
  0.6 0.0 copy-start
  0.9 0.1 concatenate.54
  1.7 0.7 gather_fusion
  2.3 0.1 concatenate.55
  2.4 0.1 fusion.1
  2.5 1.2 %copy-done.2 = bf16[1,1,4,272,512]{4,3,2,1,0:T(8,128)(2,1)S(1)} copy-done((bf16[1,1,4,272,512]{4,3,2,1,0:T(8,128)(2,1)S(1)}, bf16[1,1,4,272,512]{4,3,2,1,0:T(8,128)(2,1)}, u32[]{:S(2)}) %copy-start.2) | copy-done | bytes 1114136
  3.8 6.4 %shard_map.68 = (s16[4112,128]{1,0:T(8,128)(2,1)S(1)}, bf16[2320,512]{1,0:T(8,128)(2,1)}, bf16[1280,512]{1,0:T(8,128)(2,1)S(1)}) custom-call(s32[16]{0:T(128)S(1)} %fusion.order, s32[3]{0:T(128)S(1)} %get-tuple-element.48.picks.starts, s32[3]{0:T(128)S(1)} %get-tuple-element.49.starts, bf16[4,272,8192]{2,1,0:T(8,128)(2,1)} %bitcast.64, ...), custom_call_target="tpu_custom_call" | custom-call | tf_op jit(solution)/shard_map/pallas_call | solution.py:217
  10.2 0.5 collective-permute-start.1
  10.7 2.6 %collective-permute-start.5 = (bf16[1280,512]{1,0:T(8,128)(2,1)S(1)}, bf16[1280,512]{1,0:T(8,128)(2,1)}, u32[]{:S(2)}, u32[]{:S(2)}) collective-permute-start(bf16[1280,512]{1,0:T(8,128)(2,1)S(1)} %get-tuple-element.19), channel_id=1, source_target_pairs={{0,1},{1,0},{2,3},{3,2},{4,5},{5,4},{6,7},{7,6},{8,9},{9,8},{10,11... | collective-permute-start | bytes 3932168 | tf_op jit(solution)/shard_map/ppermute | solution.py:379
  13.2 1.3 %collective-permute-start = (bf16[2320,512]{1,0:T(8,128)(2,1)}, bf16[2320,512]{1,0:T(8,128)(2,1)S(1)}, u32[]{:S(2)}, u32[]{:S(2)}) collective-permute-start(bf16[2320,512]{1,0:T(8,128)(2,1)} %get-tuple-element.15), channel_id=1, source_target_pairs={{2,0},{4,2},{6,4},{3,1},{5,3},{7,5},{10,8},{12,10},{14,12},{11,9},... | collective-permute-start | bytes 7127048 | tf_op jit(solution)/shard_map/ppermute | solution.py:382
  14.5 0.0 collective-permute-done.1.refs_6_
  14.5 5.1 %shard_map.69.refs_6_ = s16[4224,128]{1,0:T(8,128)(2,1)S(1)} custom-call(s32[16]{0:T(128)S(1)} %fusion.order, s32[3]{0:T(128)S(1)} %get-tuple-element.48.picks.starts, s32[3]{0:T(128)S(1)} %get-tuple-element.48.picks.starts, bf16[4,272,8192]{2,1,0:T(8,128)(2,1)} %bitcast.67, bf16[4,272,8192]{2,1,0:T(8,128)(2,1)} %bitcast.68, bf16[4,272,8192]{2,1,0:T(8,128)(2,1)} %bitcast.69, ...), custom_call_target="tpu_custom_call" | custom-call | tf_op jit(solution)/shard_map/pallas_call | solution.py:217
  19.7 1.6 %collective-permute-start.4 = (s16[4224,128]{1,0:T(8,128)(2,1)S(1)}, s16[4224,128]{1,0:T(8,128)(2,1)S(1)}, u32[]{:S(2)}, u32[]{:S(2)}) collective-permute-start(s16[4224,128]{1,0:T(8,128)(2,1)S(1)} %shard_map.69.refs_6_), channel_id=1, source_target_pairs={{0,16},{8,24},{16,0},{24,8},{1,17},{9,25},{17,1},{25,9},{2,18},{10... | collective-permute-start | bytes 3244040 | tf_op jit(solution)/shard_map/ppermute | solution.py:376
  21.3 8.1 %shard_map.70 = (s16[4112,128]{1,0:T(8,128)(2,1)S(1)}, s16[4112,128]{1,0:T(8,128)(2,1)S(1)}) custom-call(s32[16]{0:T(128)S(1)} %fusion.order, s32[3]{0:T(128)S(1)} %get-tuple-element.48.picks.starts, s32[3]{0:T(128)S(1)} %get-tuple-element.48.picks.starts, bf16[4,272,8192]{2,1,0:T(8,128)(2,1)} %bitcast.70, bf16[4,272,8192]{2,1,0:T(8,128)(2,1)} %bitcast.71, ...), custom_call_target="tpu_custom_call" | custom-call | tf_op jit(solution)/shard_map/pallas_call | solution.py:217
  29.4 0.1 collective-permute-start.3
  29.4 0.5 collective-permute-start.2
  29.9 2.2 %collective-permute-done.3.refs_6_ = s16[4112,128]{1,0:T(8,128)(2,1)S(1)} collective-permute-done((s16[4112,128]{1,0:T(8,128)(2,1)S(1)}, s16[4112,128]{1,0:T(8,128)(2,1)S(1)}, u32[]{:S(2)}, u32[]{:S(2)}) %collective-permute-start.3) | collective-permute-done | bytes 1052704 | tf_op jit(solution)/shard_map/ppermute | solution.py:373
  32.1 5.1 %shard_map.71.refs_7_.refs_0_ = s16[4192,128]{1,0:T(8,128)(2,1)S(1)} custom-call(s32[16]{0:T(128)S(1)} %fusion.order, s32[3]{0:T(128)S(1)} %get-tuple-element.48.picks.starts, s32[3]{0:T(128)S(1)} %get-tuple-element.48.picks.starts, bf16[4,272,8192]{2,1,0:T(8,128)(2,1)} %bitcast.73, bf16[4,272,8192]{2,1,0:T(8,128)(2,1)} %bitcast.74, ...), custom_call_target="tpu_custom_call" | custom-call | tf_op jit(solution)/shard_map/pallas_call | solution.py:217
  37.2 0.0 collective-permute-done.2.refs_6_
  37.2 3.7 %shard_map.72.kept_ref = f32[1,1024,512]{2,1,0:T(8,128)S(1)} custom-call(s32[16]{0:T(128)S(1)} %fusion.order, s32[3]{0:T(128)S(1)} %get-tuple-element.48.picks.starts, s32[3]{0:T(128)S(1)} %get-tuple-element.48.picks.starts, bf16[4,272,8192]{2,1,0:T(8,128)(2,1)} %bitcast.76, bf16[4,272,8192]{2,1,0:T(8,128)(2,1)} %bitcast.77, bf16[4,272,8192]{2,1,0:T(8,128)(2,1)} %bitcast.78, ...), custom_call_target="tpu_custom_call" | custom-call | tf_op jit(solution)/shard_map/pallas_call | solution.py:217
  41.0 4.7 %collective-permute-done.4.refs_0_.refs_1_ = s16[4224,128]{1,0:T(8,128)(2,1)S(1)} collective-permute-done((s16[4224,128]{1,0:T(8,128)(2,1)S(1)}, s16[4224,128]{1,0:T(8,128)(2,1)S(1)}, u32[]{:S(2)}, u32[]{:S(2)}) %collective-permute-start.4) | collective-permute-done | bytes 1081376 | tf_op jit(solution)/shard_map/ppermute | solution.py:376
  45.7 1.5 %collective-permute-start.7 = (s16[4192,128]{1,0:T(8,128)(2,1)S(1)}, s16[4192,128]{1,0:T(8,128)(2,1)S(1)}, u32[]{:S(2)}, u32[]{:S(2)}) collective-permute-start(s16[4192,128]{1,0:T(8,128)(2,1)S(1)} %shard_map.76), channel_id=1, source_target_pairs={{0,16},{8,24},{16,0},{24,8},{1,17},{9,25},{17,1},{25,9},{2,18},{10... | collective-permute-start | bytes 3219464 | tf_op jit(solution)/shard_map/ppermute | solution.py:376
  47.2 0.0 collective-permute-done.5.refs_1_.refs_0_
  47.2 2.0 %shard_map.73.refs_6_ = s16[4192,128]{1,0:T(8,128)(2,1)S(1)} custom-call(f32[1,1024,512]{2,1,0:T(8,128)S(1)} %shard_map.72.kept_ref, s16[4224,128]{1,0:T(8,128)(2,1)S(1)} %collective-permute-done.4.refs_0_.refs_1_, bf16[1280,512]{1,0:T(8,128)(2,1)} %collective-permute-done.5.refs_1_.refs_0_), custom_call_target="tpu_custom_call" | custom-call | tf_op jit(solution)/shard_map/pallas_call | solution.py:114
  49.2 1.3 %collective-permute-start.8 = (s16[4192,128]{1,0:T(8,128)(2,1)S(1)}, s16[4192,128]{1,0:T(8,128)(2,1)S(1)}, u32[]{:S(2)}, u32[]{:S(2)}) collective-permute-start(s16[4192,128]{1,0:T(8,128)(2,1)S(1)} %shard_map.73.refs_6_), channel_id=1, source_target_pairs={{0,1},{1,0},{2,3},{3,2},{4,5},{5,4},{6,7},{7,6},{8,9},{9,8},{10,11... | collective-permute-start | bytes 3219464 | tf_op jit(solution)/shard_map/ppermute | solution.py:379
  50.5 4.7 %shard_map.74.refs_1_ = s16[4112,128]{1,0:T(8,128)(2,1)S(1)} custom-call(s32[16]{0:T(128)S(1)} %fusion.order, s32[3]{0:T(128)S(1)} %get-tuple-element.48.picks.starts, s32[3]{0:T(128)S(1)} %get-tuple-element.48.picks.starts, bf16[4,272,8192]{2,1,0:T(8,128)(2,1)} %bitcast.79, bf16[4,272,8192]{2,1,0:T(8,128)(2,1)} %bitcast.80, bf16[4,272,8192]{2,1,0:T(8,128)(2,1)} %bitcast.81, ...), custom_call_target="tpu_custom_call" | custom-call | tf_op jit(solution)/shard_map/pallas_call | solution.py:217
  55.3 0.1 collective-permute-start.6
  55.3 1.3 %collective-permute-start.11 = (bf16[1280,512]{1,0:T(8,128)(2,1)}, bf16[1280,512]{1,0:T(8,128)(2,1)}, u32[]{:S(2)}, u32[]{:S(2)}) collective-permute-start(bf16[1280,512]{1,0:T(8,128)(2,1)} %shard_map.79), channel_id=1, source_target_pairs={{2,0},{4,2},{6,4},{3,1},{5,3},{7,5},{10,8},{12,10},{14,12},{11,9},... | collective-permute-start | bytes 3932168 | tf_op jit(solution)/shard_map/ppermute | solution.py:382
  56.6 13.1 %collective-permute-done.refs_0_ = bf16[2320,512]{1,0:T(8,128)(2,1)S(1)} collective-permute-done((bf16[2320,512]{1,0:T(8,128)(2,1)}, bf16[2320,512]{1,0:T(8,128)(2,1)S(1)}, u32[]{:S(2)}, u32[]{:S(2)}) %collective-permute-start) | collective-permute-done | bytes 2375712 | tf_op jit(solution)/shard_map/ppermute | solution.py:382
  69.8 1.0 slice.27.refs_3_.refs_0_
  70.8 3.7 %shard_map.75.kept_ref = f32[1,1024,512]{2,1,0:T(8,128)S(1)} custom-call(s32[16]{0:T(128)S(1)} %fusion.order, s32[3]{0:T(128)S(1)} %get-tuple-element.48.picks.starts, s32[3]{0:T(128)S(1)} %get-tuple-element.48.picks.starts, bf16[4,272,8192]{2,1,0:T(8,128)(2,1)} %bitcast.82, bf16[4,272,8192]{2,1,0:T(8,128)(2,1)} %bitcast.83, bf16[4,272,8192]{2,1,0:T(8,128)(2,1)} %bitcast.84, ...), custom_call_target="tpu_custom_call" | custom-call | tf_op jit(solution)/shard_map/pallas_call | solution.py:217
  74.5 0.0 copy-start.4
  74.5 1.3 %copy-done.4 = f32[1,1024,512]{2,1,0:T(8,128)} copy-done((f32[1,1024,512]{2,1,0:T(8,128)}, f32[1,1024,512]{2,1,0:T(8,128)S(1)}, u32[]{:S(2)}) %copy-start.4) | copy-done | bytes 2097176
  75.8 0.0 collective-permute-done.7.refs_0_
  75.8 0.0 collective-permute-done.8.refs_1_
  75.8 4.0 %shard_map.77.refs_1_.refs_0_ = s16[4128,128]{1,0:T(8,128)(2,1)S(1)} custom-call(f32[1,1024,512]{2,1,0:T(8,128)} %copy-done.4, s16[4192,128]{1,0:T(8,128)(2,1)S(1)} %collective-permute-done.7.refs_0_, s16[4192,128]{1,0:T(8,128)(2,1)S(1)} %collective-permute-done.8.refs_1_, bf16[272,512]{1,0:T(8,128)(2,1)S(1)} %slice.26.refs_2_.current_ref, ...), custom_call_target="tpu_custom_call" | custom-call | tf_op jit(solution)/shard_map/pallas_call | solution.py:114
  79.8 0.1 collective-permute-start.14
  79.9 1.5 %fusion.12 = (bf16[1024,512]{1,0:T(8,128)(2,1)}, bf16[1024,512]{1,0:T(8,128)(2,1)}) fusion(bf16[2320,512]{1,0:T(8,128)(2,1)S(1)} %shard_map.80.refs_0_), kind=kLoop, calls=%fused_computation.37 | loop fusion | bytes 4194304 | tf_op jit(solution)/shard_map/slice | solution.py:453
  81.4 0.5 collective-permute-start.12
  81.9 0.0 collective-permute-start.13
  81.9 1.5 %collective-permute-start.10 = (s16[4128,128]{1,0:T(8,128)(2,1)S(1)}, s16[4128,128]{1,0:T(8,128)(2,1)}, u32[]{:S(2)}, u32[]{:S(2)}) collective-permute-start(s16[4128,128]{1,0:T(8,128)(2,1)S(1)} %shard_map.77.refs_1_.refs_0_), channel_id=1, source_target_pairs={{0,16},{8,24},{16,0},{24,8},{1,17},{9,25},{17,1},{25,9},{2,18},{10... | collective-permute-start | bytes 3170312 | tf_op jit(solution)/shard_map/ppermute | solution.py:376
  83.4 0.1 pad_add_fusion.4.place
  83.5 0.1 pad_add_fusion.3.starts
  83.6 0.0 collective-permute-done.14.refs_1_
  83.6 0.6 collective-permute-start.9
  84.2 4.0 %shard_map.81 = (f32[4,1024,512]{2,1,0:T(8,128)}, f32[8,128]{1,0:T(8,128)S(1)}) custom-call(s32[2]{0:T(128)S(1)} %pad_add_fusion.4.place, s16[4128,128]{1,0:T(8,128)(2,1)S(1)} %shard_map.77.refs_1_.refs_0_, s16[4128,128]{1,0:T(8,128)(2,1)} %collective-permute-done.14.refs_1_), custom_call_target="tpu_custom_call" | custom-call | tf_op jit(solution)/shard_map/pallas_call | solution.py:339
  88.2 0.0 collective-permute-done.12.refs_1_
  88.2 4.3 %shard_map.82 = (bf16[272,8192]{1,0:T(8,128)(2,1)}, f32[8,128]{1,0:T(8,128)S(1)}) custom-call(s32[3]{0:T(128)S(1)} %pad_add_fusion.3.starts, bf16[272,512]{1,0:T(8,128)(2,1)S(1)} %copy-done.6, bf16[2320,512]{1,0:T(8,128)(2,1)S(1)} %shard_map.80.refs_0_, bf16[1024,512]{1,0:T(8,128)(2,1)} %collective-permute-done.12.refs_1_, ...), custom_call_target="tpu_custom_call" | custom-call | tf_op jit(solution)/shard_map/pallas_call | solution.py:282
  92.5 4.7 %collective-permute-done.11.refs_0_ = bf16[1280,512]{1,0:T(8,128)(2,1)} collective-permute-done((bf16[1280,512]{1,0:T(8,128)(2,1)}, bf16[1280,512]{1,0:T(8,128)(2,1)}, u32[]{:S(2)}, u32[]{:S(2)}) %collective-permute-start.11) | collective-permute-done | bytes 1310752 | tf_op jit(solution)/shard_map/ppermute | solution.py:382
  97.2 2.2 %fusion.13 = (bf16[640,512]{1,0:T(8,128)(2,1)S(1)}, bf16[640,512]{1,0:T(8,128)(2,1)}) fusion(bf16[1280,512]{1,0:T(8,128)(2,1)} %shard_map.83.refs_0_), kind=kLoop, calls=%fused_computation.38 | loop fusion | bytes 2621440 | tf_op jit(solution)/shard_map/slice | solution.py:453
  99.4 0.0 collective-permute-start.15
  99.4 0.5 collective-permute-start.16
  100.0 0.1 pad_add_fusion.2.starts
  100.0 2.6 %collective-permute-done.15.refs_1_ = bf16[640,512]{1,0:T(8,128)(2,1)S(1)} collective-permute-done((bf16[640,512]{1,0:T(8,128)(2,1)}, bf16[640,512]{1,0:T(8,128)(2,1)S(1)}, u32[]{:S(2)}, u32[]{:S(2)}) %collective-permute-start.15) | collective-permute-done | bytes 655392 | tf_op jit(solution)/shard_map/ppermute | solution.py:373
  102.7 0.0 collective-permute-done.16.refs_2_
  102.7 3.8 %shard_map.84 = (bf16[272,8192]{1,0:T(8,128)(2,1)}, f32[8,128]{1,0:T(8,128)S(1)}) custom-call(s32[3]{0:T(128)S(1)} %pad_add_fusion.2.starts, bf16[272,512]{1,0:T(8,128)(2,1)S(1)} %copy-done.7, bf16[1280,512]{1,0:T(8,128)(2,1)} %shard_map.83.refs_0_, bf16[640,512]{1,0:T(8,128)(2,1)S(1)} %collective-permute-done.15.refs_1_, ...), custom_call_target="tpu_custom_call", output_to_operand_aliasing={{0}: (5, {})} | custom-call | tf_op jit(solution)/shard_map/pallas_call | solution.py:282
  106.5 1.2 %collective-permute-done.10.refs_0_ = s16[4128,128]{1,0:T(8,128)(2,1)} collective-permute-done((s16[4128,128]{1,0:T(8,128)(2,1)S(1)}, s16[4128,128]{1,0:T(8,128)(2,1)}, u32[]{:S(2)}, u32[]{:S(2)}) %collective-permute-start.10) | collective-permute-done | bytes 1056800 | tf_op jit(solution)/shard_map/ppermute | solution.py:376
  107.7 2.9 %collective-permute-done.17.refs_1_ = s16[4128,128]{1,0:T(8,128)(2,1)S(1)} collective-permute-done((s16[4128,128]{1,0:T(8,128)(2,1)}, s16[4128,128]{1,0:T(8,128)(2,1)S(1)}, u32[]{:S(2)}, u32[]{:S(2)}) %collective-permute-start.17) | collective-permute-done | bytes 1056800 | tf_op jit(solution)/shard_map/ppermute | solution.py:373
  110.6 0.1 collective-permute-start.18
  110.7 0.1 pad_add_fusion.starts
  110.8 0.1 pad_add_fusion.5.place
  110.9 4.6 %shard_map.88 = (f32[4,1024,512]{2,1,0:T(8,128)}, f32[8,128]{1,0:T(8,128)}) custom-call(s32[2]{0:T(128)S(1)} %pad_add_fusion.5.place, s16[4128,128]{1,0:T(8,128)(2,1)} %shard_map.85.refs_0_, s16[4128,128]{1,0:T(8,128)(2,1)S(1)} %collective-permute-done.17.refs_1_, f32[4,1024,512]{2,1,0:T(8,128)} %get-tuple-element.26.refs_2_), custom_call_target="tpu_custom_call", output_to_operand_aliasing={{0}: (3, {})} | custom-call | tf_op jit(solution)/shard_map/pallas_call | solution.py:339
  115.5 0.0 copy-start.1
  115.5 3.7 %shard_map.87 = (bf16[272,8192]{1,0:T(8,128)(2,1)}, f32[8,128]{1,0:T(8,128)}) custom-call(s32[2]{0:T(128)S(1)} %pad_add_fusion.starts, bf16[272,512]{1,0:T(8,128)(2,1)S(1)} %copy-done.7, bf16[768,512]{1,0:T(8,128)(2,1)} %shard_map.86.refs_0_, bf16[768,512]{1,0:T(8,128)(2,1)S(1)} %collective-permute-done.18.refs_1_, ...), custom_call_target="tpu_custom_call", output_to_operand_aliasing={{0}: (4, {})} | custom-call | tf_op jit(solution)/shard_map/pallas_call | solution.py:282
  (35 shorter events, 0.1 us)
Async XLA Ops:
  0.6 1.0 copy-start
  2.5 1.2 %copy-start.2 = (bf16[1,1,4,272,512]{4,3,2,1,0:T(8,128)(2,1)S(1)}, bf16[1,1,4,272,512]{4,3,2,1,0:T(8,128)(2,1)}, u32[]{:S(2)}) copy-start(bf16[1,1,4,272,512]{4,3,2,1,0:T(8,128)(2,1)} %param.6) | copy-start | bytes 3342340
  3.8 10.8 %copy-start.3 = (bf16[1,1,4,272,512]{4,3,2,1,0:T(8,128)(2,1)S(1)}, bf16[1,1,4,272,512]{4,3,2,1,0:T(8,128)(2,1)}, u32[]{:S(2)}) copy-start(bf16[1,1,4,272,512]{4,3,2,1,0:T(8,128)(2,1)} %param.6) | copy-start | bytes 3342340
  10.2 4.4 %collective-permute-start.1 = (s16[4112,128]{1,0:T(8,128)(2,1)S(1)}, s16[4112,128]{1,0:T(8,128)(2,1)S(1)}, u32[]{:S(2)}, u32[]{:S(2)}) collective-permute-start(s16[4112,128]{1,0:T(8,128)(2,1)S(1)} %get-tuple-element.16), channel_id=1, source_target_pairs={{0,8},{8,0},{16,24},{24,16},{1,9},{9,1},{17,25},{25,17},{2,10},{10... | collective-permute-start | bytes 3158024 | tf_op jit(solution)/shard_map/ppermute | solution.py:373
  10.7 36.5 %collective-permute-start.5 = (bf16[1280,512]{1,0:T(8,128)(2,1)S(1)}, bf16[1280,512]{1,0:T(8,128)(2,1)}, u32[]{:S(2)}, u32[]{:S(2)}) collective-permute-start(bf16[1280,512]{1,0:T(8,128)(2,1)S(1)} %get-tuple-element.19), channel_id=1, source_target_pairs={{0,1},{1,0},{2,3},{3,2},{4,5},{5,4},{6,7},{7,6},{8,9},{9,8},{10,11... | collective-permute-start | bytes 3932168 | tf_op jit(solution)/shard_map/ppermute | solution.py:379
  13.2 56.5 %collective-permute-start = (bf16[2320,512]{1,0:T(8,128)(2,1)}, bf16[2320,512]{1,0:T(8,128)(2,1)S(1)}, u32[]{:S(2)}, u32[]{:S(2)}) collective-permute-start(bf16[2320,512]{1,0:T(8,128)(2,1)} %get-tuple-element.15), channel_id=1, source_target_pairs={{2,0},{4,2},{6,4},{3,1},{5,3},{7,5},{10,8},{12,10},{14,12},{11,9},... | collective-permute-start | bytes 7127048 | tf_op jit(solution)/shard_map/ppermute | solution.py:382
  19.7 26.0 %collective-permute-start.4 = (s16[4224,128]{1,0:T(8,128)(2,1)S(1)}, s16[4224,128]{1,0:T(8,128)(2,1)S(1)}, u32[]{:S(2)}, u32[]{:S(2)}) collective-permute-start(s16[4224,128]{1,0:T(8,128)(2,1)S(1)} %shard_map.69.refs_6_), channel_id=1, source_target_pairs={{0,16},{8,24},{16,0},{24,8},{1,17},{9,25},{17,1},{25,9},{2,18},{10... | collective-permute-start | bytes 3244040 | tf_op jit(solution)/shard_map/ppermute | solution.py:376
  29.4 2.7 %collective-permute-start.3 = (s16[4112,128]{1,0:T(8,128)(2,1)S(1)}, s16[4112,128]{1,0:T(8,128)(2,1)S(1)}, u32[]{:S(2)}, u32[]{:S(2)}) collective-permute-start(s16[4112,128]{1,0:T(8,128)(2,1)S(1)} %get-tuple-element.18), channel_id=1, source_target_pairs={{0,8},{8,0},{16,24},{24,16},{1,9},{9,1},{17,25},{25,17},{2,10},{10... | collective-permute-start | bytes 3158024 | tf_op jit(solution)/shard_map/ppermute | solution.py:373
  29.4 7.8 %collective-permute-start.2 = (s16[4112,128]{1,0:T(8,128)(2,1)S(1)}, s16[4112,128]{1,0:T(8,128)(2,1)S(1)}, u32[]{:S(2)}, u32[]{:S(2)}) collective-permute-start(s16[4112,128]{1,0:T(8,128)(2,1)S(1)} %get-tuple-element.17), channel_id=1, source_target_pairs={{0,8},{8,0},{16,24},{24,16},{1,9},{9,1},{17,25},{25,17},{2,10},{10... | collective-permute-start | bytes 3158024 | tf_op jit(solution)/shard_map/ppermute | solution.py:373
  45.7 30.1 %collective-permute-start.7 = (s16[4192,128]{1,0:T(8,128)(2,1)S(1)}, s16[4192,128]{1,0:T(8,128)(2,1)S(1)}, u32[]{:S(2)}, u32[]{:S(2)}) collective-permute-start(s16[4192,128]{1,0:T(8,128)(2,1)S(1)} %shard_map.76), channel_id=1, source_target_pairs={{0,16},{8,24},{16,0},{24,8},{1,17},{9,25},{17,1},{25,9},{2,18},{10... | collective-permute-start | bytes 3219464 | tf_op jit(solution)/shard_map/ppermute | solution.py:376
  49.2 26.6 %collective-permute-start.8 = (s16[4192,128]{1,0:T(8,128)(2,1)S(1)}, s16[4192,128]{1,0:T(8,128)(2,1)S(1)}, u32[]{:S(2)}, u32[]{:S(2)}) collective-permute-start(s16[4192,128]{1,0:T(8,128)(2,1)S(1)} %shard_map.73.refs_6_), channel_id=1, source_target_pairs={{0,1},{1,0},{2,3},{3,2},{4,5},{5,4},{6,7},{7,6},{8,9},{9,8},{10,11... | collective-permute-start | bytes 3219464 | tf_op jit(solution)/shard_map/ppermute | solution.py:379
  55.3 15.5 %collective-permute-start.6 = (s16[4112,128]{1,0:T(8,128)(2,1)S(1)}, s16[4112,128]{1,0:T(8,128)(2,1)S(1)}, u32[]{:S(2)}, u32[]{:S(2)}) collective-permute-start(s16[4112,128]{1,0:T(8,128)(2,1)S(1)} %shard_map.74.refs_1_), channel_id=1, source_target_pairs={{0,8},{8,0},{16,24},{24,16},{1,9},{9,1},{17,25},{25,17},{2,10},{10... | collective-permute-start | bytes 3158024 | tf_op jit(solution)/shard_map/ppermute | solution.py:373
  55.3 41.9 %collective-permute-start.11 = (bf16[1280,512]{1,0:T(8,128)(2,1)}, bf16[1280,512]{1,0:T(8,128)(2,1)}, u32[]{:S(2)}, u32[]{:S(2)}) collective-permute-start(bf16[1280,512]{1,0:T(8,128)(2,1)} %shard_map.79), channel_id=1, source_target_pairs={{2,0},{4,2},{6,4},{3,1},{5,3},{7,5},{10,8},{12,10},{14,12},{11,9},... | collective-permute-start | bytes 3932168 | tf_op jit(solution)/shard_map/ppermute | solution.py:382
  69.8 6.0 %copy-start.5 = (bf16[272,512]{1,0:T(8,128)(2,1)}, bf16[272,512]{1,0:T(8,128)(2,1)S(1)}, u32[]{:S(2)}) copy-start(bf16[272,512]{1,0:T(8,128)(2,1)S(1)} %slice.26.refs_2_.current_ref) | copy-start | bytes 835588
  74.5 1.3 %copy-start.4 = (f32[1,1024,512]{2,1,0:T(8,128)}, f32[1,1024,512]{2,1,0:T(8,128)S(1)}, u32[]{:S(2)}) copy-start(f32[1,1024,512]{2,1,0:T(8,128)S(1)} %shard_map.75.kept_ref) | copy-start | bytes 6291460
  79.8 3.8 %collective-permute-start.14 = (s16[4128,128]{1,0:T(8,128)(2,1)S(1)}, s16[4128,128]{1,0:T(8,128)(2,1)}, u32[]{:S(2)}, u32[]{:S(2)}) collective-permute-start(s16[4128,128]{1,0:T(8,128)(2,1)S(1)} %shard_map.77.refs_1_.refs_0_), channel_id=1, source_target_pairs={{0,8},{8,0},{16,24},{24,16},{1,9},{9,1},{17,25},{25,17},{2,10},{10... | collective-permute-start | bytes 3170312 | tf_op jit(solution)/shard_map/ppermute | solution.py:373
  81.4 6.8 %collective-permute-start.12 = (bf16[1024,512]{1,0:T(8,128)(2,1)}, bf16[1024,512]{1,0:T(8,128)(2,1)}, u32[]{:S(2)}, u32[]{:S(2)}) collective-permute-start(bf16[1024,512]{1,0:T(8,128)(2,1)} %get-tuple-element.29), channel_id=1, source_target_pairs={{0,8},{8,0},{16,24},{24,16},{1,9},{9,1},{17,25},{25,17},{2,10},{10... | collective-permute-start | bytes 3145736 | tf_op jit(solution)/shard_map/ppermute | solution.py:373
  81.9 6.3 %collective-permute-start.13 = (bf16[1024,512]{1,0:T(8,128)(2,1)}, bf16[1024,512]{1,0:T(8,128)(2,1)}, u32[]{:S(2)}, u32[]{:S(2)}) collective-permute-start(bf16[1024,512]{1,0:T(8,128)(2,1)} %get-tuple-element.28), channel_id=1, source_target_pairs={{0,8},{8,0},{16,24},{24,16},{1,9},{9,1},{17,25},{25,17},{2,10},{10... | collective-permute-start | bytes 3145736 | tf_op jit(solution)/shard_map/ppermute | solution.py:373
  81.9 25.8 %collective-permute-start.10 = (s16[4128,128]{1,0:T(8,128)(2,1)S(1)}, s16[4128,128]{1,0:T(8,128)(2,1)}, u32[]{:S(2)}, u32[]{:S(2)}) collective-permute-start(s16[4128,128]{1,0:T(8,128)(2,1)S(1)} %shard_map.77.refs_1_.refs_0_), channel_id=1, source_target_pairs={{0,16},{8,24},{16,0},{24,8},{1,17},{9,25},{17,1},{25,9},{2,18},{10... | collective-permute-start | bytes 3170312 | tf_op jit(solution)/shard_map/ppermute | solution.py:376
  83.6 4.6 %copy-start.6 = (bf16[272,512]{1,0:T(8,128)(2,1)S(1)}, bf16[272,512]{1,0:T(8,128)(2,1)}, u32[]{:S(2)}) copy-start(bf16[272,512]{1,0:T(8,128)(2,1)} %copy-done.5) | copy-start | bytes 835588
  83.6 22.9 %collective-permute-start.9 = (bf16[768,512]{1,0:T(8,128)(2,1)}, bf16[768,512]{1,0:T(8,128)(2,1)}, u32[]{:S(2)}, u32[]{:S(2)}) collective-permute-start(bf16[768,512]{1,0:T(8,128)(2,1)} %shard_map.78), channel_id=1, source_target_pairs={{0,1},{1,0},{2,3},{3,2},{4,5},{5,4},{6,7},{7,6},{8,9},{9,8},{10,11... | collective-permute-start | bytes 2359304 | tf_op jit(solution)/shard_map/ppermute | solution.py:379
  97.2 5.5 %copy-start.7 = (bf16[272,512]{1,0:T(8,128)(2,1)S(1)}, bf16[272,512]{1,0:T(8,128)(2,1)}, u32[]{:S(2)}) copy-start(bf16[272,512]{1,0:T(8,128)(2,1)} %copy-done.5) | copy-start | bytes 835588
  99.4 3.2 %collective-permute-start.15 = (bf16[640,512]{1,0:T(8,128)(2,1)}, bf16[640,512]{1,0:T(8,128)(2,1)S(1)}, u32[]{:S(2)}, u32[]{:S(2)}) collective-permute-start(bf16[640,512]{1,0:T(8,128)(2,1)} %get-tuple-element.31), channel_id=1, source_target_pairs={{0,8},{8,0},{16,24},{24,16},{1,9},{9,1},{17,25},{25,17},{2,10},{10... | collective-permute-start | bytes 1966088 | tf_op jit(solution)/shard_map/ppermute | solution.py:373
  99.4 3.2 %collective-permute-start.16 = (bf16[640,512]{1,0:T(8,128)(2,1)S(1)}, bf16[640,512]{1,0:T(8,128)(2,1)S(1)}, u32[]{:S(2)}, u32[]{:S(2)}) collective-permute-start(bf16[640,512]{1,0:T(8,128)(2,1)S(1)} %get-tuple-element.30), channel_id=1, source_target_pairs={{0,8},{8,0},{16,24},{24,16},{1,9},{9,1},{17,25},{25,17},{2,10},{10... | collective-permute-start | bytes 1966088 | tf_op jit(solution)/shard_map/ppermute | solution.py:373
  107.7 2.9 %collective-permute-start.17 = (s16[4128,128]{1,0:T(8,128)(2,1)}, s16[4128,128]{1,0:T(8,128)(2,1)S(1)}, u32[]{:S(2)}, u32[]{:S(2)}) collective-permute-start(s16[4128,128]{1,0:T(8,128)(2,1)} %shard_map.85.refs_0_), channel_id=1, source_target_pairs={{0,8},{8,0},{16,24},{24,16},{1,9},{9,1},{17,25},{25,17},{2,10},{10... | collective-permute-start | bytes 3170312 | tf_op jit(solution)/shard_map/ppermute | solution.py:373
  110.6 4.9 %collective-permute-start.18 = (bf16[768,512]{1,0:T(8,128)(2,1)}, bf16[768,512]{1,0:T(8,128)(2,1)S(1)}, u32[]{:S(2)}, u32[]{:S(2)}) collective-permute-start(bf16[768,512]{1,0:T(8,128)(2,1)} %shard_map.86.refs_0_), channel_id=1, source_target_pairs={{0,8},{8,0},{16,24},{24,16},{1,9},{9,1},{17,25},{25,17},{2,10},{10... | collective-permute-start | bytes 2359304 | tf_op jit(solution)/shard_map/ppermute | solution.py:373
  115.5 3.7 %copy-start.1 = (s32[8]{0:T(128)S(1)}, s32[8]{0:T(128)}, u32[]{:S(2)}) copy-start(s32[8]{0:T(128)} %param.9) | copy-start | bytes 100

commit v4 on v3

v4 whole, which is shorter than its diff:
```python
import functools
import math

import jax
import jax.numpy as jnp
from jax import lax
from jax.experimental import pallas as pl
from jax.experimental.pallas import tpu as pltpu
from jax.sharding import PartitionSpec as P

LANES = 128
TAIL = 16
MORE = 16
FAR_TAILS = 3
SIDE_TAILS = 6
DONE = jax.ShapeDtypeStruct((8, LANES), jnp.float32)
INNER = 2
TOP = 32767.0
VMEM_LIMIT = 26 << 20
TOKEN_VMEM_LIMIT = 48 << 20
FIRST_VMEM_LIMIT = 48 << 20


def params(limit=VMEM_LIMIT):
    return pltpu.CompilerParams(vmem_limit_bytes=limit)


def code_shape(rows, width, tails=1):
    return jax.ShapeDtypeStruct((width // LANES * rows + TAIL * tails, LANES), jnp.int16)


def scale_of(code_ref, count):
    exponent = code_ref[count : count + TAIL, :].astype(jnp.int32)[0:1, :].astype(jnp.float32)
    return jnp.exp2(exponent) * (1.0 / (TOP * TOP))


def decoded(code_ref, start, rows, scale):
    level = code_ref[pl.ds(start, rows), :].astype(jnp.int32).astype(jnp.float32)
    return level * jnp.abs(level) * scale


def hold_kernel(*refs):
    pass


def after(value, *waits):
    return pl.pallas_call(
        hold_kernel,
        out_shape=jax.ShapeDtypeStruct(value.shape, value.dtype),
        in_specs=[pl.BlockSpec(memory_space=pl.ANY)] + [pl.BlockSpec(memory_space=pl.ANY) for _ in waits],
        out_specs=pl.BlockSpec(memory_space=pl.ANY),
        input_output_aliases={0: 0},
        compiler_params=params(),
    )(value, *waits)


def split_kernel(value_ref, *refs, cuts):
    outs, buffers, sem = refs[: len(cuts)], refs[len(cuts) : -1], refs[-1]
    coming = [
        pltpu.make_async_copy(value_ref.at[pl.ds(at, rows), :], buffers[n], sem.at[n])
        for n, (at, rows) in enumerate(cuts)
    ]
    leaving = [
        pltpu.make_async_copy(buffers[n], outs[n], sem.at[len(cuts) + n]) for n in range(len(cuts))
    ]
    for c in coming:
        c.start()
    for c, d in zip(coming, leaving):
        c.wait()
        d.start()
    for d in leaving:
        d.wait()


def split(value, *cuts):
    shapes = [jax.ShapeDtypeStruct((rows, value.shape[1]), value.dtype) for _, rows in cuts]
    return pl.pallas_call(
        functools.partial(split_kernel, cuts=cuts),
        out_shape=shapes,
        in_specs=[pl.BlockSpec(memory_space=pl.ANY)],
        out_specs=[pl.BlockSpec(memory_space=pl.ANY)] * len(cuts),
        scratch_shapes=[pltpu.VMEM(x.shape, x.dtype) for x in shapes]
        + [pltpu.SemaphoreType.DMA((2 * len(cuts),))],
        compiler_params=params(),
    )(value)


def gather_total(total_ref, start, rows, whole, codes, largest):
    width = total_ref.shape[1]
    step = min(rows, 128)
    slabs = width // LANES
    scales = [scale_of(c, slabs * whole) for c in codes]

    def add(i, largest):
        r = pl.multiple_of(start + i * step, step)
        for j in range(slabs):
            slab = slice(j * LANES, (j + 1) * LANES)
            value = total_ref[pl.ds(r, step), slab]
            for c, scale in zip(codes, scales):
                value = value + decoded(c, pl.multiple_of(j * whole + r, step), step, scale)
            if codes:
                total_ref[pl.ds(r, step), slab] = value
            largest = jnp.maximum(largest, jnp.max(jnp.abs(value).reshape(step // 8, 8, LANES), axis=0))
        return largest

    return lax.fori_loop(0, rows // step, add, largest)


def encode(total_ref, largest, out_ref):
    rows, width = total_ref.shape
    step = min(rows, 128)
    slabs = width // LANES
    largest = jnp.max(jnp.max(largest, axis=0, keepdims=True), axis=1, keepdims=True)
    exponent = jnp.floor(jnp.log2(jnp.maximum(largest, 1e-30))) + 2.0
    exponent = jnp.broadcast_to(exponent, (8, LANES))
    shrink = jnp.exp2(-exponent)[0:1, :]

    def one(i, carry):
        r = pl.multiple_of(i * step, step)
        for j in range(slabs):
            value = total_ref[pl.ds(r, step), j * LANES : (j + 1) * LANES]
            root = jnp.round(jnp.sqrt(jnp.abs(value) * shrink) * TOP)
            level = jnp.where(value < 0.0, -root, root)
            place = pl.ds(pl.multiple_of(j * rows + r, step), step)
            out_ref[place, :] = level.astype(jnp.int32).astype(jnp.int16)
        return carry

    lax.fori_loop(0, rows // step, one, 0)
    tail = jnp.concatenate([exponent] * ((out_ref.shape[0] - slabs * rows) // 8), axis=0)
    out_ref[slabs * rows :, :] = tail.astype(jnp.int32).astype(jnp.int16)


def combine_kernel(kept_ref, *refs, n_codes, rows):
    out_ref, total_ref = refs[-2:]
    total_ref[...] = kept_ref[0]
    largest = gather_total(total_ref, 0, rows, rows, refs[:n_codes], jnp.zeros((8, LANES), jnp.float32))
    encode(total_ref, largest, out_ref)


def combine(kept, codes, *waits, tails=1):
    _, rows, width = kept.shape
    shape = code_shape(rows, width, tails)
    in_specs = (
        [pl.BlockSpec((1, rows, width), lambda i: (0, 0, 0))]
        + [pl.BlockSpec(x.shape, lambda i: (0, 0)) for x in codes]
        + [pl.BlockSpec(memory_space=pl.ANY) for _ in waits]
    )
    return pl.pallas_call(
        functools.partial(combine_kernel, n_codes=len(codes), rows=rows),
        out_shape=shape,
        grid=(1,),
        in_specs=in_specs,
        out_specs=pl.BlockSpec(shape.shape, lambda i: (0, 0)),
        scratch_shapes=[pltpu.VMEM((rows, width), jnp.float32)],
        compiler_params=params(),
    )(kept, *codes, *waits)


def token_kernel(where, slot, cycle, acts_ref, grads_ref, *refs, owners, sizes, n_codes, n_sources, n_waits, coded, moves, rows, block):
    codes, sources, refs = refs[:n_codes], refs[n_codes : n_codes + n_sources], refs[n_codes + n_sources + n_waits :]
    groups = len(owners)
    outs, moved, refs = refs[:groups], refs[groups : groups + len(moves)], refs[groups + len(moves) :]
    left_ref, right_ref, total_refs, code_refs, sem = refs[:5]
    moving_refs = refs[5:]
    count, tokens = acts_ref.shape[0] - 1, grads_ref.shape[1]
    steps = rows // block
    n_ctx, outer, piece = sizes
    copies = []

    def copy(source, target):
        copies.append(pltpu.make_async_copy(source, target, sem.at[len(copies)]))
        copies[-1].start()
        return copies[-1]

    def pick(m):
        return m + (m >= slot[0]).astype(jnp.int32)

    def first_column(k):
        kx, ko, ki = owners[k // steps]
        ctx = lax.rem(where[0] + kx, n_ctx)
        replica = lax.rem(where[1] + ko, outer) * INNER + lax.rem(where[2] + ki, INNER)
        at = (ctx * (outer * INNER) + replica) * rows + k % steps * block
        return pl.multiple_of(cycle[at // piece] * piece + lax.rem(at, piece), block)

    ready = []
    for k in range(groups * steps):
        ready.append([])
        columns = pl.ds(first_column(k), block)
        for m in range(count):
            place = pl.ds(m * tokens, tokens)
            if k == 0:
                ready[0].append(copy(grads_ref.at[pick(m)], right_ref.at[place, :]))
            ready[k].append(copy(acts_ref.at[pick(m), :, columns], left_ref.at[k, place, :]))
    moving = []
    for buffer_ref, segments in zip(moving_refs, moves):
        place = 0
        for source, start, length in segments:
            there = pl.ds(pl.multiple_of(start(where, slot), TAIL), length)
            moving.append(copy(sources[source].at[there, :], buffer_ref.at[pl.ds(place, length), :]))
            place += length

    each = n_codes // groups
    leaving = []
    for n in range(groups):
        total_ref = total_refs.at[n]
        largest = jnp.zeros((8, LANES), jnp.float32)
        for b in range(steps):
            k = n * steps + b
            for c in ready[k]:
                c.wait()
            part = pl.ds(b * block, block)
            total_ref[part, :] = lax.dot_general(
                left_ref[k], right_ref[...], (((0,), (0,)), ((), ())), preferred_element_type=jnp.float32
            )
            if coded[n] or codes:
                largest = gather_total(total_ref, b * block, block, rows, codes[n * each : (n + 1) * each], largest)
            if not coded[n]:
                leaving.append(copy(total_ref.at[part, :], outs[n].at[0, part, :]))
        if coded[n]:
            encode(total_ref, largest, code_refs.at[n])
            leaving.append(copy(code_refs.at[n], outs[n]))
        if n == 0:
            for c in moving:
                c.wait()
            leaving += [copy(buffer_ref, out_ref) for buffer_ref, out_ref in zip(moving_refs, moved)]
    for c in leaving:
        c.wait()


def token_products(
    where, slot, cycle, sizes, owners, coded, acts, grads, block, rows, codes, *waits, tails=1, sources=(), moves=(), limit
):
    count = acts.shape[0] - 1
    tokens = acts.shape[1]
    width = grads.shape[2]
    groups = len(owners)
    blocks = groups * (rows // block)
    shape = code_shape(rows, width, tails)

    stays = pl.BlockSpec(memory_space=pltpu.HBM)
    in_specs = (
        [stays, stays]
        + [pl.BlockSpec(x.shape, lambda i, *_: (0, 0)) for x in codes]
        + [stays for _ in sources]
        + [pl.BlockSpec(memory_space=pl.ANY) for _ in waits]
    )
    out_shape = [shape if c else jax.ShapeDtypeStruct((1, rows, width), jnp.float32) for c in coded]
    for m in moves:
        like = sources[m[0][0]]
        out_shape.append(jax.ShapeDtypeStruct((sum(n for _, _, n in m), like.shape[1]), like.dtype))
    n_copies = count * (blocks + 1) + sum(len(m) + 1 for m in moves) + blocks
    scratch = [
        pltpu.VMEM((blocks, count * tokens, block), acts.dtype),
        pltpu.VMEM((count * tokens, width), grads.dtype),
        pltpu.VMEM((groups, rows, width), jnp.float32),
        pltpu.VMEM((groups if any(coded) else 1, *(shape.shape if any(coded) else (TAIL, LANES))), jnp.int16),
        pltpu.SemaphoreType.DMA((n_copies,)),
    ] + [pltpu.VMEM(x.shape, x.dtype) for x in out_shape[groups:]]
    return pl.pallas_call(
        functools.partial(
            token_kernel,
            owners=owners,
            sizes=sizes,
            n_codes=len(codes),
            n_sources=len(sources),
            n_waits=len(waits),
            coded=coded,
            moves=moves,
            rows=rows,
            block=block,
        ),
        out_shape=out_shape,
        grid_spec=pltpu.PrefetchScalarGridSpec(
            num_scalar_prefetch=3,
            grid=(1,),
            in_specs=in_specs,
            out_specs=[pl.BlockSpec(memory_space=pl.ANY) for _ in out_shape],
            scratch_shapes=scratch,
        ),
        compiler_params=params(limit),
    )(where, slot, cycle, acts, grads, *codes, *sources, *waits)


def key_kernel(starts, current_ref, *refs, segments):
    out_ref, done_ref = refs[len(refs) - len(segments) - 3 : len(refs) - len(segments) - 1]
    blocks, sem = refs[len(refs) - len(segments) - 1 : -1], refs[-1]
    copies = []
    for n, (skip, rows) in enumerate(segments):
        step = min(rows, 512)
        for at in range(0, rows, step):
            size = min(step, rows - at)
            blocks[n][:, at : at + size] = lax.dot_general(
                current_ref[...],
                refs[n][skip + at : skip + at + size, :],
                (((1,), (1,)), ((), ())),
                preferred_element_type=jnp.float32,
            ).astype(out_ref.dtype)
        place = pl.ds(pl.multiple_of(starts[n], LANES), rows)
        copies.append(pltpu.make_async_copy(blocks[n], out_ref.at[:, place], sem.at[n]))
        copies[-1].start()
    done_ref[...] = jnp.zeros_like(done_ref)
    for c in copies:
        c.wait()


def key_products(current, parts, features, held, *waits):
    tokens, width = current.shape
    arrays = [x for x, _, _, _ in parts]
    anywhere = pl.BlockSpec(memory_space=pltpu.HBM)
    in_specs = [pl.BlockSpec(x.shape, lambda i, p: (0, 0)) for x in (current, *arrays)]
    operands = [jnp.stack([start for _, _, _, start in parts]), current, *arrays]
    aliases = {}
    if held is not None:
        in_specs.append(anywhere)
        aliases = {len(operands): 0}
        operands.append(held)
    in_specs += [pl.BlockSpec(memory_space=pl.ANY) for _ in waits]
    operands += waits
    return pl.pallas_call(
        functools.partial(key_kernel, segments=[(skip, rows) for _, skip, rows, _ in parts]),
        out_shape=[jax.ShapeDtypeStruct((tokens, features), jnp.bfloat16), DONE],
        grid_spec=pltpu.PrefetchScalarGridSpec(
            num_scalar_prefetch=1,
            grid=(1,),
            in_specs=in_specs,
            out_specs=[anywhere, pl.BlockSpec(DONE.shape, lambda i, p: (0, 0))],
            scratch_shapes=[pltpu.VMEM((tokens, rows), jnp.bfloat16) for _, _, rows, _ in parts]
            + [pltpu.SemaphoreType.DMA((len(parts),))],
        ),
        input_output_aliases=aliases,
        compiler_params=params(),
    )(*operands)


def decode_kernel(place, *refs, count, rows, width):
    out_ref, done_ref, code_refs, block_ref, sem = refs[-5:]
    slabs = width // LANES
    step = min(rows, 128)
    coming = [pltpu.make_async_copy(refs[n], code_refs.at[n], sem.at[n]) for n in range(count)]
    for c in coming:
        c.start()
    copies = []
    for n in range(count):
        coming[n].wait()
        scale = scale_of(code_refs.at[n], slabs * rows)

        def one(i, carry):
            r = pl.multiple_of(i * step, step)
            for j in range(slabs):
                block_ref[n, pl.ds(r, step), j * LANES : (j + 1) * LANES] = decoded(
                    code_refs.at[n], pl.multiple_of(j * rows + r, step), step, scale
                )
            return carry

        for k in range(2):
            part = rows // 2
            lax.fori_loop(k * part // step, (k + 1) * part // step, one, 0)
            at = pl.ds(k * part, part)
            copies.append(
                pltpu.make_async_copy(
                    block_ref.at[n, at, :], out_ref.at[place[n], at, :], sem.at[count + 2 * n + k]
                )
            )
            copies[-1].start()
    done_ref[...] = jnp.zeros_like(done_ref)
    for c in copies:
        c.wait()


def decode(place, codes, blocks, rows, width, held, *waits):
    count = len(codes)
    anywhere = pl.BlockSpec(memory_space=pltpu.HBM)
    in_specs = [pl.BlockSpec(memory_space=pl.ANY) for _ in codes]
    operands = [place, *codes]
    aliases = {}
    if held is not None:
        in_specs.append(anywhere)
        aliases = {len(operands): 0}
        operands.append(held)
    in_specs += [pl.BlockSpec(memory_space=pl.ANY) for _ in waits]
    operands += waits
    return pl.pallas_call(
        functools.partial(decode_kernel, count=count, rows=rows, width=width),
        out_shape=[jax.ShapeDtypeStruct((blocks, rows, width), jnp.float32), DONE],
        grid_spec=pltpu.PrefetchScalarGridSpec(
            num_scalar_prefetch=1,
            grid=(1,),
            in_specs=in_specs,
            out_specs=[anywhere, pl.BlockSpec(DONE.shape, lambda i, p: (0, 0))],
            scratch_shapes=[
                pltpu.VMEM((count, *codes[0].shape), jnp.int16),
                pltpu.VMEM((count, rows, width), jnp.float32),
                pltpu.SemaphoreType.DMA((3 * count,)),
            ],
        ),
        input_output_aliases=aliases,
        compiler_params=params(),
    )(*operands)


def body(acts, key_grads, weights, b_slot, cycle):
    stored, grads, weight = acts[0, 0], key_grads[0, 0], weights[0]
    micro, tokens, features = stored.shape
    width = grads.shape[2]
    n_dp, n_ctx = lax.axis_size("dp"), lax.axis_size("ctx")
    n_pipe = lax.axis_size("pipe")
    outer = n_dp // INNER
    replica, section = lax.axis_index("dp"), lax.axis_index("ctx")
    me_o, me_i = replica // INNER, replica % INNER
    groups = n_dp * n_ctx
    rows = features // groups
    pieces = cycle.shape[0]

    def swap(value):
        pairs = [(d, d // INNER * INNER + (d + 1) % INNER) for d in range(n_dp)]
        return lax.ppermute(value, "dp", pairs)

    def to_outer(value, by):
        return lax.ppermute(value, "dp", [(d, (d + by * INNER) % n_dp) for d in range(n_dp)])

    def to_ctx(value, by):
        return lax.ppermute(value, "ctx", [(d, (d + by) % n_ctx) for d in range(n_ctx)])

    def to_previous(value):
        return lax.ppermute(value, "pipe", [(d, d - 1) for d in range(1, n_pipe)])

    half = weight.shape[0] // INNER
    late_part = max(half * 3 // 8 // LANES, 1) * LANES

    block = min(rows, features // pieces, 512)
    far = [(kx, ko) for ko in range(1, outer) for kx in range(1, n_ctx)]
    near = [(0, ko) for ko in range(1, outer)]
    side = [(kx, 0) for kx in range(1, n_ctx)]
    home = [(0, 0)]
    where = jnp.stack([section, me_o, me_i]).astype(jnp.int32)
    sizes = (n_ctx, outer, features // pieces)

    def sent_by(wanted):
        return [(kx, ko, 1) for kx, ko in wanted]

    def kept_by(wanted):
        return [(kx, ko, 0) for kx, ko in wanted]

    def products(owners, coded, codes, *waits, limit=TOKEN_VMEM_LIMIT, **more):
        flags = coded if isinstance(coded, list) else [coded] * len(owners)
        return token_products(
            where, b_slot, cycle, sizes, owners, flags, stored, grads, block, rows, codes, *waits, limit=limit, **more
        )

    *far_out, own_all, own_most = products(
        sent_by(far) + kept_by(far),
        [True] * len(far) + [False] * len(far),
        [],
        sources=(weight, grads.reshape(micro * tokens, width)),
        moves=(
            [(0, lambda w, b: w[2] * half, half), (1, lambda w, b: b[0] * tokens, tokens)],
            [(0, lambda w, b: w[2] * half + late_part, half - late_part)],
        ),
        limit=FIRST_VMEM_LIMIT,
    )
    z_all = to_previous(own_all)
    crossed_most = [to_ctx(own_most, kx) for kx in range(1, n_ctx)]
    far_theirs = [swap(c) for c in far_out[: len(far)]]
    coded = {
        w: combine(kept, [theirs], tails=FAR_TAILS) for w, kept, theirs in zip(far, far_out[len(far) :], far_theirs)
    }
    got = {w: to_outer(coded[w], w[1]) for w in far}
    sent = products(sent_by(near + side), True, [], *coded.values())
    theirs = [swap(c) for c in sent]
    coded = dict(zip(near, products(kept_by(near), True, theirs[: len(near)], tails=SIDE_TAILS)))
    side_sums = products(kept_by(side), False, theirs[len(near) :], *coded.values())

    passed = passed_done = None

    def pass_on(kx, start, pieces, *waits):
        nonlocal passed, passed_done
        parts = []
        for piece, rows in pieces:
            row = ((section - kx) % n_ctx) * weight.shape[0] + start
            parts.append((piece, 0, rows, row + me_i * half))
            parts.append((swap(piece), 0, rows, row + (me_i + 1) % INNER * half))
            start = start + rows
        passed, passed_done = key_products(current, parts, features, passed, *waits)
        return [x for x, _, _, _ in parts[1::2]]

    values = [
        combine(total, [got[kx, ko] for ko in range(1, outer)], tails=SIDE_TAILS + 1)
        for (kx, _), total in zip(side, side_sums)
    ]
    crossed = [to_ctx(v, kx) for (kx, _), v in zip(side, values)]
    got.update({w: to_outer(after(coded[w], *values), w[1]) for w in near})
    home_sent = products(sent_by(home), True, [], *values, *crossed_most)
    home_theirs = swap(home_sent[0])
    (home_kept,) = products(kept_by(home), False, [], home_sent[0])
    z_crossed = [to_previous(after(c, home_kept)) for c in crossed_most]
    z_first, z_second, late, current = split(
        z_all,
        (0, half // 2 + MORE),
        (half // 2, half - half // 2 + MORE),
        (0, late_part),
        (half, tokens),
    )
    z_pieces = [(z_first, half // 2), (z_second, half - half // 2)]
    codes = [home_theirs, *[got[0, ko] for ko in range(1, outer)], *crossed]
    own = combine(home_kept, codes, current, tails=2)
    others = {ko: to_outer(own, ko) for ko in range(1, outer)}
    late = [to_ctx(late, kx) for kx in range(1, n_ctx)]
    pass_on(0, 0, z_pieces)
    result, result_done = decode(
        jnp.stack([me_o * INNER + me_i, me_o * INNER + (me_i + 1) % INNER]),
        [own, swap(own)],
        n_dp,
        rows,
        width,
        None,
        passed_done,
    )
    most = half - late_part
    first = min(-(-most * 11 // 16 // LANES) * LANES, most - LANES)
    for kx in range(1, n_ctx):
        held = after(z_crossed[kx - 1], result_done)
        pieces = split(held, (0, first), (first, most - first))
        pass_on(kx, late_part, [(pieces[0], first), (pieces[1], most - first)])
    crossed_done = passed_done
    late_theirs = []
    for kx in range(1, n_ctx):
        late_theirs += pass_on(kx, 0, [(late[kx - 1], late_part)])
    for ko in range(1, outer):
        other = after(others[ko], crossed_done, *late_theirs)
        o = (me_o - ko) % outer
        place = jnp.stack([o * INNER + me_i, o * INNER + (me_i + 1) % INNER])
        result, _ = decode(place, [other, swap(other)], n_dp, rows, width, result, passed_done)
    return passed[None, None], result.reshape(1, n_dp * rows, width)


def solution(mesh):
    placed = (
        P("dp", "pipe", None, "ctx", None),
        P("dp", "pipe", None, "ctx", None),
        P("pipe", "ctx", None),
        P("pipe"),
        P(),
    )
    return jax.shard_map(
        body,
        mesh=mesh,
        in_specs=placed,
        out_specs=(P("dp", "pipe", "ctx", None), P("pipe", "ctx", None)),
        check_vma=False,
    )
```

time: 120 us -> 113 us (0.942)
  local copies, waits for them, and re-layouts: 8.16 us -> 1.9 us
  waiting for transfers between devices: 31.5 us -> 27.8 us
  Pallas kernels: 63.2 us -> 64.9 us
  starting transfers between devices: 14.1 us -> 15.7 us
    slice x4 -> x0, local copies, waits for them, and re-layouts: 4.72 us -> none  [the longest x2 3.74 us: pass_on(): lax.slice_in_dim(held, skip + at, skip + at + size)]
    pallas_call x2 -> x3, Pallas kernels: 5.92 us -> 8.98 us  [combine(): pl.pallas_call(functools.partial(combine_kernel, n_codes=len(codes), rows...]
    ppermute x11, waiting for transfers between devices: 7.68 us -> 5.1 us  [swap(): return lax.ppermute(value, 'dp', pairs)]
    ppermute x3, waiting for transfers between devices: 5.96 us -> 4.09 us  [to_outer(): lax.ppermute(value, 'dp', [(d, (d + by * INNER) % n_dp) for d in range(n_...]
    ppermute x3, starting transfers between devices: 4.44 us -> 5.72 us  [to_ctx(): lax.ppermute(value, 'ctx', [(d, (d + by) % n_ctx) for d in range(n_ctx)])]
    pallas_call x7 -> x8, Pallas kernels: 36.9 us -> 35.7 us  [the longest x6 32.4 us: token_products(): pl.pallas_call(functools.partial(token_kernel, owners=owners, sizes=sizes...]
    unnamed x16 -> x4, local copies, waits for them, and re-layouts: 2.6 us -> 1.9 us
  transfers between devices with their start and end apart: 19 -> 19, of which waited for: 7 -> 5; matrix products, arithmetic and copies ran while one was open for 4% -> 0% of each run, Pallas kernels for 45% -> 47%
where the time goes in v4:
time: 113 us; the launch traced here: 112 us
  Pallas kernels  64.9 us (57%)
  waiting for transfers between devices  27.8 us (25%)
  starting transfers between devices  15.7 us (14%)
  local copies, waits for them, and re-layouts  1.9 us (2%)
  between operations  1.7 us (2%)
    pallas_call x6, Pallas kernels, token_products(): pl.pallas_call(functools.partial(token_kernel, owners=owners, sizes=sizes...  32.4 us
    ppermute x2, waiting for transfers between devices, to_previous(): return lax.ppermute(value, 'pipe', [(d, d - 1) for d in range(1, n_pipe)])  18.6 us
    pallas_call x3, Pallas kernels, key_products(): pl.pallas_call(functools.partial(key_kernel, segments=[(skip, rows) for _...  11.5 us
    pallas_call x3, Pallas kernels, combine(): pl.pallas_call(functools.partial(combine_kernel, n_codes=len(codes), rows...  8.98 us
    pallas_call x2, Pallas kernels, decode(): pl.pallas_call(functools.partial(decode_kernel, count=count, rows=rows, w...  8.66 us
    ppermute x3, starting transfers between devices, to_ctx(): lax.ppermute(value, 'ctx', [(d, (d + by) % n_ctx) for d in range(n_ctx)])  5.72 us
    ppermute x11, waiting for transfers between devices, swap(): return lax.ppermute(value, 'dp', pairs)  5.1 us
    ppermute x3, starting transfers between devices, to_outer(): lax.ppermute(value, 'dp', [(d, (d + by * INNER) % n_dp) for d in range(n_...  4.6 us
  transfers between devices with their start and end apart: 19, of which 5 were waited for; matrix products, arithmetic and copies ran while one was open for 0% of the time, Pallas kernels for 47%

profile of v4, /device:TPU:0, one launch (start us, length us, event | category | flops | bytes accessed | tf_op | source)
XLA Modules:
  0.0 112.5 jit_solution(17089320128912345296)
XLA Ops:
  1.3 0.1 pad_add_fusion.1.where
  1.4 0.0 copy-start
  1.4 1.2 %copy-done = bf16[1,1,4,272,512]{4,3,2,1,0:T(8,128)(2,1)S(1)} copy-done((bf16[1,1,4,272,512]{4,3,2,1,0:T(8,128)(2,1)S(1)}, bf16[1,1,4,272,512]{4,3,2,1,0:T(8,128)(2,1)}, u32[]{:S(2)}) %copy-start) | copy-done | bytes 1114136
  2.6 0.0 copy-start.1
  2.6 0.7 copy-done.1
  3.3 6.8 %shard_map.68 = (s16[4112,128]{1,0:T(8,128)(2,1)S(1)}, f32[1,1024,512]{2,1,0:T(8,128)S(1)}, bf16[2320,512]{1,0:T(8,128)(2,1)}, bf16[1280,512]{1,0:T(8,128)(2,1)}) custom-call(s32[3]{0:T(128)S(1)} %pad_add_fusion.1.where, s32[1]{0:T(128)S(6)} %copy.21.slot, s32[8]{0:T(128)S(1)} %copy-done.1, bf16[4,272,8192]{2,1,0:T(8,128)(2,1)} %bitcast.30, ...), custom_call_target="tpu_custom_call" | custom-call | tf_op jit(solution)/shard_map/pallas_call | solution.py:259
  10.1 0.5 collective-permute-start.4
  10.6 1.3 %collective-permute-start = (bf16[2320,512]{1,0:T(8,128)(2,1)}, bf16[2320,512]{1,0:T(8,128)(2,1)S(1)}, u32[]{:S(2)}, u32[]{:S(2)}) collective-permute-start(bf16[2320,512]{1,0:T(8,128)(2,1)} %get-tuple-element.23), channel_id=1, source_target_pairs={{2,0},{4,2},{6,4},{3,1},{5,3},{7,5},{10,8},{12,10},{14,12},{11,9},... | collective-permute-start | bytes 7127048 | tf_op jit(solution)/shard_map/ppermute | solution.py:425
  11.9 2.6 %collective-permute-start.3 = (bf16[1280,512]{1,0:T(8,128)(2,1)}, bf16[1280,512]{1,0:T(8,128)(2,1)S(1)}, u32[]{:S(2)}, u32[]{:S(2)}) collective-permute-start(bf16[1280,512]{1,0:T(8,128)(2,1)} %get-tuple-element.26), channel_id=1, source_target_pairs={{0,1},{1,0},{2,3},{3,2},{4,5},{5,4},{6,7},{7,6},{8,9},{9,8},{10,11... | collective-permute-start | bytes 3932168 | tf_op jit(solution)/shard_map/ppermute | solution.py:422
  14.5 0.0 collective-permute-done.4.refs_0_
  14.5 2.0 %shard_map.70.refs_0_ = s16[4144,128]{1,0:T(8,128)(2,1)S(1)} custom-call(f32[1,1024,512]{2,1,0:T(8,128)S(1)} %get-tuple-element.27.kept_ref, s16[4112,128]{1,0:T(8,128)(2,1)S(1)} %collective-permute-done.4.refs_0_), custom_call_target="tpu_custom_call" | custom-call | tf_op jit(solution)/shard_map/pallas_call | solution.py:148
  16.5 1.6 %collective-permute-start.7 = (s16[4144,128]{1,0:T(8,128)(2,1)S(1)}, s16[4144,128]{1,0:T(8,128)(2,1)S(1)}, u32[]{:S(2)}, u32[]{:S(2)}) collective-permute-start(s16[4144,128]{1,0:T(8,128)(2,1)S(1)} %shard_map.70.refs_0_), channel_id=1, source_target_pairs={{0,16},{8,24},{16,0},{24,8},{1,17},{9,25},{17,1},{25,9},{2,18},{10... | collective-permute-start | bytes 3182600 | tf_op jit(solution)/shard_map/ppermute | solution.py:419
  18.1 8.0 %shard_map.71 = (s16[4112,128]{1,0:T(8,128)(2,1)S(1)}, s16[4112,128]{1,0:T(8,128)(2,1)S(1)}) custom-call(s32[3]{0:T(128)S(1)} %pad_add_fusion.1.where, s32[1]{0:T(128)S(6)} %copy.21.slot, s32[8]{0:T(128)S(1)} %copy-done.1, bf16[4,272,8192]{2,1,0:T(8,128)(2,1)} %bitcast.31, bf16[4,272,512]{2,1,0:T(8,128)(2,1)S(1)} %bitcast.25, ...), custom_call_target="tpu_custom_call" | custom-call | tf_op jit(solution)/shard_map/pallas_call | solution.py:259
  26.0 0.1 collective-permute-start.6
  26.1 0.5 collective-permute-start.5
  26.6 2.2 %collective-permute-done.6.refs_0_ = s16[4112,128]{1,0:T(8,128)(2,1)S(1)} collective-permute-done((s16[4112,128]{1,0:T(8,128)(2,1)S(1)}, s16[4112,128]{1,0:T(8,128)(2,1)S(1)}, u32[]{:S(2)}, u32[]{:S(2)}) %collective-permute-start.6) | collective-permute-done | bytes 1052704 | tf_op jit(solution)/shard_map/ppermute | solution.py:416
  28.8 5.3 %shard_map.72.refs_1_.refs_0_ = s16[4192,128]{1,0:T(8,128)(2,1)S(1)} custom-call(s32[3]{0:T(128)S(1)} %pad_add_fusion.1.where, s32[1]{0:T(128)S(6)} %copy.21.slot, s32[8]{0:T(128)S(1)} %copy-done.1, bf16[4,272,8192]{2,1,0:T(8,128)(2,1)} %bitcast.32, bf16[4,272,512]{2,1,0:T(8,128)(2,1)S(1)} %bitcast.26, s16[4112,128]{1,0:T(8,128)(2,1)S(1)} %collective-permute-done.6.refs_0_), custom_call_target="tpu_custom_call" | custom-call | tf_op jit(solution)/shard_map/pallas_call | solution.py:259
  34.0 0.0 collective-permute-done.5.refs_0_
  34.1 3.9 %shard_map.73.kept_ref = f32[1,1024,512]{2,1,0:T(8,128)S(1)} custom-call(s32[3]{0:T(128)S(1)} %pad_add_fusion.1.where, s32[1]{0:T(128)S(6)} %copy.21.slot, s32[8]{0:T(128)S(1)} %copy-done.1, bf16[4,272,8192]{2,1,0:T(8,128)(2,1)} %bitcast.33, bf16[4,272,512]{2,1,0:T(8,128)(2,1)S(1)} %bitcast.27, s16[4112,128]{1,0:T(8,128)(2,1)S(1)} %collective-permute-done.5.refs_0_, ...), custom_call_target="tpu_custom_call" | custom-call | tf_op jit(solution)/shard_map/pallas_call | solution.py:259
  38.0 4.1 %collective-permute-done.7.refs_0_ = s16[4144,128]{1,0:T(8,128)(2,1)S(1)} collective-permute-done((s16[4144,128]{1,0:T(8,128)(2,1)S(1)}, s16[4144,128]{1,0:T(8,128)(2,1)S(1)}, u32[]{:S(2)}, u32[]{:S(2)}) %collective-permute-start.7) | collective-permute-done | bytes 1060896 | tf_op jit(solution)/shard_map/ppermute | solution.py:419
  42.1 2.0 %shard_map.74.refs_0_.refs_1_ = s16[4208,128]{1,0:T(8,128)(2,1)S(1)} custom-call(f32[1,1024,512]{2,1,0:T(8,128)S(1)} %shard_map.73.kept_ref, s16[4144,128]{1,0:T(8,128)(2,1)S(1)} %collective-permute-done.7.refs_0_), custom_call_target="tpu_custom_call" | custom-call | tf_op jit(solution)/shard_map/pallas_call | solution.py:148
  44.1 1.3 %collective-permute-start.11 = (s16[4208,128]{1,0:T(8,128)(2,1)S(1)}, s16[4208,128]{1,0:T(8,128)(2,1)S(1)}, u32[]{:S(2)}, u32[]{:S(2)}) collective-permute-start(s16[4208,128]{1,0:T(8,128)(2,1)S(1)} %shard_map.74.refs_0_.refs_1_), channel_id=1, source_target_pairs={{0,1},{1,0},{2,3},{3,2},{4,5},{5,4},{6,7},{7,6},{8,9},{9,8},{10,11... | collective-permute-start | bytes 3231752 | tf_op jit(solution)/shard_map/ppermute | solution.py:422
  45.3 1.5 %collective-permute-start.10 = (s16[4192,128]{1,0:T(8,128)(2,1)S(1)}, s16[4192,128]{1,0:T(8,128)(2,1)}, u32[]{:S(2)}, u32[]{:S(2)}) collective-permute-start(s16[4192,128]{1,0:T(8,128)(2,1)S(1)} %shard_map.78), channel_id=1, source_target_pairs={{0,16},{8,24},{16,0},{24,8},{1,17},{9,25},{17,1},{25,9},{2,18},{10... | collective-permute-start | bytes 3219464 | tf_op jit(solution)/shard_map/ppermute | solution.py:419
  46.9 0.0 collective-permute-done.3.refs_1_.refs_0_
  46.9 4.9 %shard_map.75.refs_0_ = s16[4112,128]{1,0:T(8,128)(2,1)S(1)} custom-call(s32[3]{0:T(128)S(1)} %pad_add_fusion.1.where, s32[1]{0:T(128)S(6)} %copy.21.slot, s32[8]{0:T(128)S(1)} %copy-done.1, bf16[4,272,8192]{2,1,0:T(8,128)(2,1)} %bitcast.34, bf16[4,272,512]{2,1,0:T(8,128)(2,1)S(1)} %bitcast.28, s16[4208,128]{1,0:T(8,128)(2,1)S(1)} %shard_map.74.refs_0_.refs_1_, ...), custom_call_target="tpu_custom_call" | custom-call | tf_op jit(solution)/shard_map/pallas_call | solution.py:259
  51.7 0.1 collective-permute-start.9
  51.8 3.5 %shard_map.76.refs_1_.kept_ref = f32[1,1024,512]{2,1,0:T(8,128)S(1)} custom-call(s32[3]{0:T(128)S(1)} %pad_add_fusion.1.where, s32[1]{0:T(128)S(6)} %copy.21.slot, s32[8]{0:T(128)S(1)} %copy-done.1, bf16[4,272,8192]{2,1,0:T(8,128)(2,1)} %bitcast.35, bf16[4,272,512]{2,1,0:T(8,128)(2,1)S(1)} %bitcast.29, s16[4112,128]{1,0:T(8,128)(2,1)S(1)} %shard_map.75.refs_0_), custom_call_target="tpu_custom_call" | custom-call | tf_op jit(solution)/shard_map/pallas_call | solution.py:259
  55.3 1.5 %collective-permute-start.8 = (bf16[1280,512]{1,0:T(8,128)(2,1)S(1)}, bf16[1280,512]{1,0:T(8,128)(2,1)S(1)}, u32[]{:S(2)}, u32[]{:S(2)}) collective-permute-start(bf16[1280,512]{1,0:T(8,128)(2,1)S(1)} %shard_map.77), channel_id=1, source_target_pairs={{2,0},{4,2},{6,4},{3,1},{5,3},{7,5},{10,8},{12,10},{14,12},{11,9},... | collective-permute-start | bytes 3932168 | tf_op jit(solution)/shard_map/ppermute | solution.py:425
  56.8 11.0 %collective-permute-done.value_ref = bf16[2320,512]{1,0:T(8,128)(2,1)S(1)} collective-permute-done((bf16[2320,512]{1,0:T(8,128)(2,1)}, bf16[2320,512]{1,0:T(8,128)(2,1)S(1)}, u32[]{:S(2)}, u32[]{:S(2)}) %collective-permute-start) | collective-permute-done | bytes 2375712 | tf_op jit(solution)/shard_map/ppermute | solution.py:425
  67.8 2.0 %shard_map.69 = (bf16[1040,512]{1,0:T(8,128)(2,1)}, bf16[1040,512]{1,0:T(8,128)(2,1)}, bf16[768,512]{1,0:T(8,128)(2,1)}, bf16[272,512]{1,0:T(8,128)(2,1)S(1)}) custom-call(bf16[2320,512]{1,0:T(8,128)(2,1)S(1)} %collective-permute-done.value_ref), custom_call_target="tpu_custom_call" | custom-call | tf_op jit(solution)/shard_map/pallas_call | solution.py:77
  69.7 0.1 collective-permute-start.13
  69.8 0.0 collective-permute-done.9.refs_0_
  69.8 0.5 collective-permute-start.14
  70.3 0.0 collective-permute-done.10.refs_1_
  70.3 0.0 collective-permute-done.11.refs_2_
  70.3 5.0 %shard_map.79.refs_0_ = s16[4128,128]{1,0:T(8,128)(2,1)} custom-call(f32[1,1024,512]{2,1,0:T(8,128)S(1)} %shard_map.76.refs_1_.kept_ref, s16[4112,128]{1,0:T(8,128)(2,1)S(1)} %collective-permute-done.9.refs_0_, s16[4192,128]{1,0:T(8,128)(2,1)} %collective-permute-done.10.refs_1_, s16[4208,128]{1,0:T(8,128)(2,1)S(1)} %collective-permute-done.11.refs_2_, ...), custom_call_target="tpu_custom_call" | custom-call | tf_op jit(solution)/shard_map/pallas_call | solution.py:148
  75.4 0.1 collective-permute-start.12
  75.5 1.9 %collective-permute-start.1 = (bf16[768,512]{1,0:T(8,128)(2,1)}, bf16[768,512]{1,0:T(8,128)(2,1)}, u32[]{:S(2)}, u32[]{:S(2)}) collective-permute-start(bf16[768,512]{1,0:T(8,128)(2,1)} %get-tuple-element.25), channel_id=1, source_target_pairs={{0,1},{1,0},{2,3},{3,2},{4,5},{5,4},{6,7},{7,6},{8,9},{9,8},{10,11... | collective-permute-start | bytes 2359304 | tf_op jit(solution)/shard_map/ppermute | solution.py:422
  77.3 0.0 collective-permute-done.13.refs_1_
  77.3 1.5 %collective-permute-start.17 = (s16[4128,128]{1,0:T(8,128)(2,1)}, s16[4128,128]{1,0:T(8,128)(2,1)}, u32[]{:S(2)}, u32[]{:S(2)}) collective-permute-start(s16[4128,128]{1,0:T(8,128)(2,1)} %shard_map.79.refs_0_), channel_id=1, source_target_pairs={{0,16},{8,24},{16,0},{24,8},{1,17},{9,25},{17,1},{25,9},{2,18},{10... | collective-permute-start | bytes 3170312 | tf_op jit(solution)/shard_map/ppermute | solution.py:419
  78.8 0.1 pad_add_fusion.3.place
  78.9 0.1 pad_add_fusion.4.starts
  79.0 0.0 collective-permute-done.14.refs_3_
  79.0 4.9 %shard_map.80 = (bf16[272,8192]{1,0:T(8,128)(2,1)}, f32[8,128]{1,0:T(8,128)S(1)}) custom-call(s32[4]{0:T(128)S(1)} %pad_add_fusion.4.starts, bf16[272,512]{1,0:T(8,128)(2,1)S(1)} %get-tuple-element.24.refs_3_.current_ref, bf16[1040,512]{1,0:T(8,128)(2,1)} %get-tuple-element.31.refs_0_, bf16[1040,512]{1,0:T(8,128)(2,1)} %collective-permute-done.13.refs_1_, ...), custom_call_target="tpu_custom_call" | custom-call | tf_op jit(solution)/shard_map/pallas_call | solution.py:319
  83.9 0.0 collective-permute-done.12.refs_1_
  83.9 4.0 %shard_map.81 = (f32[4,1024,512]{2,1,0:T(8,128)}, f32[8,128]{1,0:T(8,128)S(1)}) custom-call(s32[2]{0:T(128)S(1)} %pad_add_fusion.3.place, s16[4128,128]{1,0:T(8,128)(2,1)} %shard_map.79.refs_0_, s16[4128,128]{1,0:T(8,128)(2,1)} %collective-permute-done.12.refs_1_, f32[8,128]{1,0:T(8,128)S(1)} %get-tuple-element.33.refs_2_), custom_call_target="tpu_custom_call" | custom-call | tf_op jit(solution)/shard_map/pallas_call | solution.py:382
  88.0 7.7 %collective-permute-done.8.refs_0_ = bf16[1280,512]{1,0:T(8,128)(2,1)S(1)} collective-permute-done((bf16[1280,512]{1,0:T(8,128)(2,1)S(1)}, bf16[1280,512]{1,0:T(8,128)(2,1)S(1)}, u32[]{:S(2)}, u32[]{:S(2)}) %collective-permute-start.8) | collective-permute-done | bytes 1310752 | tf_op jit(solution)/shard_map/ppermute | solution.py:425
  95.7 1.4 %shard_map.83 = (bf16[896,512]{1,0:T(8,128)(2,1)}, bf16[384,512]{1,0:T(8,128)(2,1)S(1)}) custom-call(bf16[1280,512]{1,0:T(8,128)(2,1)S(1)} %shard_map.82.value_ref), custom_call_target="tpu_custom_call" | custom-call | tf_op jit(solution)/shard_map/pallas_call | solution.py:77
  97.0 0.1 collective-permute-start.15
  97.1 0.0 collective-permute-done.1.refs_0_
  97.1 0.5 collective-permute-start.2
  97.6 0.1 collective-permute-start.16
  97.7 0.1 pad_add_fusion.2.starts
  97.8 2.9 %collective-permute-done.16.refs_3_ = bf16[384,512]{1,0:T(8,128)(2,1)S(1)} collective-permute-done((bf16[384,512]{1,0:T(8,128)(2,1)S(1)}, bf16[384,512]{1,0:T(8,128)(2,1)S(1)}, u32[]{:S(2)}, u32[]{:S(2)}) %collective-permute-start.16) | collective-permute-done | bytes 393248 | tf_op jit(solution)/shard_map/ppermute | solution.py:416
  100.7 0.0 collective-permute-done.15.refs_1_
  100.7 3.5 %shard_map.84 = (bf16[272,8192]{1,0:T(8,128)(2,1)}, f32[8,128]{1,0:T(8,128)S(1)}) custom-call(s32[4]{0:T(128)S(1)} %pad_add_fusion.2.starts, bf16[272,512]{1,0:T(8,128)(2,1)S(1)} %get-tuple-element.24.refs_3_.current_ref, bf16[896,512]{1,0:T(8,128)(2,1)} %get-tuple-element.35.refs_0_, ...), custom_call_target="tpu_custom_call", output_to_operand_aliasing={{0}: (6, {})} | custom-call | tf_op jit(solution)/shard_map/pallas_call | solution.py:319
  104.2 0.0 collective-permute-done.2.refs_1_.refs_2_
  104.2 0.0 collective-permute-done.17.refs_0_
  104.2 0.2 collective-permute-start.18
  104.4 0.1 pad_add_fusion.starts
  104.5 0.1 pad_add_fusion.5.place
  104.6 3.1 %shard_map.85 = (bf16[272,8192]{1,0:T(8,128)(2,1)}, f32[8,128]{1,0:T(8,128)S(1)}) custom-call(s32[2]{0:T(128)S(1)} %pad_add_fusion.starts, bf16[272,512]{1,0:T(8,128)(2,1)S(1)} %get-tuple-element.24.refs_3_.current_ref, bf16[768,512]{1,0:T(8,128)(2,1)} %collective-permute-done.1.refs_0_, ...), custom_call_target="tpu_custom_call", output_to_operand_aliasing={{0}: (4, {})} | custom-call | tf_op jit(solution)/shard_map/pallas_call | solution.py:319
  107.7 0.0 collective-permute-done.18.refs_1_
  107.7 4.6 %shard_map.87 = (f32[4,1024,512]{2,1,0:T(8,128)}, f32[8,128]{1,0:T(8,128)}) custom-call(s32[2]{0:T(128)S(1)} %pad_add_fusion.5.place, s16[4128,128]{1,0:T(8,128)(2,1)} %shard_map.86.refs_0_, s16[4128,128]{1,0:T(8,128)(2,1)S(1)} %collective-permute-done.18.refs_1_, f32[4,1024,512]{2,1,0:T(8,128)} %get-tuple-element.41.refs_2_, ...), custom_call_target="tpu_custom_call", output_to_operand_aliasing={{0}: (3, {})} | custom-call | tf_op jit(solution)/shard_map/pallas_call | solution.py:382
  (4 shorter events, 0.0 us)
Async XLA Ops:
  1.4 1.2 %copy-start = (bf16[1,1,4,272,512]{4,3,2,1,0:T(8,128)(2,1)S(1)}, bf16[1,1,4,272,512]{4,3,2,1,0:T(8,128)(2,1)}, u32[]{:S(2)}) copy-start(bf16[1,1,4,272,512]{4,3,2,1,0:T(8,128)(2,1)} %param.6) | copy-start | bytes 3342340
  2.6 0.7 copy-start.1
  10.1 4.4 %collective-permute-start.4 = (s16[4112,128]{1,0:T(8,128)(2,1)S(1)}, s16[4112,128]{1,0:T(8,128)(2,1)S(1)}, u32[]{:S(2)}, u32[]{:S(2)}) collective-permute-start(s16[4112,128]{1,0:T(8,128)(2,1)S(1)} %get-tuple-element.28), channel_id=1, source_target_pairs={{0,8},{8,0},{16,24},{24,16},{1,9},{9,1},{17,25},{25,17},{2,10},{10... | collective-permute-start | bytes 3158024 | tf_op jit(solution)/shard_map/ppermute | solution.py:416
  10.6 57.1 %collective-permute-start = (bf16[2320,512]{1,0:T(8,128)(2,1)}, bf16[2320,512]{1,0:T(8,128)(2,1)S(1)}, u32[]{:S(2)}, u32[]{:S(2)}) collective-permute-start(bf16[2320,512]{1,0:T(8,128)(2,1)} %get-tuple-element.23), channel_id=1, source_target_pairs={{2,0},{4,2},{6,4},{3,1},{5,3},{7,5},{10,8},{12,10},{14,12},{11,9},... | collective-permute-start | bytes 7127048 | tf_op jit(solution)/shard_map/ppermute | solution.py:425
  11.9 34.9 %collective-permute-start.3 = (bf16[1280,512]{1,0:T(8,128)(2,1)}, bf16[1280,512]{1,0:T(8,128)(2,1)S(1)}, u32[]{:S(2)}, u32[]{:S(2)}) collective-permute-start(bf16[1280,512]{1,0:T(8,128)(2,1)} %get-tuple-element.26), channel_id=1, source_target_pairs={{0,1},{1,0},{2,3},{3,2},{4,5},{5,4},{6,7},{7,6},{8,9},{9,8},{10,11... | collective-permute-start | bytes 3932168 | tf_op jit(solution)/shard_map/ppermute | solution.py:422
  16.5 25.6 %collective-permute-start.7 = (s16[4144,128]{1,0:T(8,128)(2,1)S(1)}, s16[4144,128]{1,0:T(8,128)(2,1)S(1)}, u32[]{:S(2)}, u32[]{:S(2)}) collective-permute-start(s16[4144,128]{1,0:T(8,128)(2,1)S(1)} %shard_map.70.refs_0_), channel_id=1, source_target_pairs={{0,16},{8,24},{16,0},{24,8},{1,17},{9,25},{17,1},{25,9},{2,18},{10... | collective-permute-start | bytes 3182600 | tf_op jit(solution)/shard_map/ppermute | solution.py:419
  26.0 2.7 %collective-permute-start.6 = (s16[4112,128]{1,0:T(8,128)(2,1)S(1)}, s16[4112,128]{1,0:T(8,128)(2,1)S(1)}, u32[]{:S(2)}, u32[]{:S(2)}) collective-permute-start(s16[4112,128]{1,0:T(8,128)(2,1)S(1)} %get-tuple-element.30), channel_id=1, source_target_pairs={{0,8},{8,0},{16,24},{24,16},{1,9},{9,1},{17,25},{25,17},{2,10},{10... | collective-permute-start | bytes 3158024 | tf_op jit(solution)/shard_map/ppermute | solution.py:416
  26.1 7.9 %collective-permute-start.5 = (s16[4112,128]{1,0:T(8,128)(2,1)S(1)}, s16[4112,128]{1,0:T(8,128)(2,1)S(1)}, u32[]{:S(2)}, u32[]{:S(2)}) collective-permute-start(s16[4112,128]{1,0:T(8,128)(2,1)S(1)} %get-tuple-element.29), channel_id=1, source_target_pairs={{0,8},{8,0},{16,24},{24,16},{1,9},{9,1},{17,25},{25,17},{2,10},{10... | collective-permute-start | bytes 3158024 | tf_op jit(solution)/shard_map/ppermute | solution.py:416
  44.1 26.3 %collective-permute-start.11 = (s16[4208,128]{1,0:T(8,128)(2,1)S(1)}, s16[4208,128]{1,0:T(8,128)(2,1)S(1)}, u32[]{:S(2)}, u32[]{:S(2)}) collective-permute-start(s16[4208,128]{1,0:T(8,128)(2,1)S(1)} %shard_map.74.refs_0_.refs_1_), channel_id=1, source_target_pairs={{0,1},{1,0},{2,3},{3,2},{4,5},{5,4},{6,7},{7,6},{8,9},{9,8},{10,11... | collective-permute-start | bytes 3231752 | tf_op jit(solution)/shard_map/ppermute | solution.py:422
  45.3 25.0 %collective-permute-start.10 = (s16[4192,128]{1,0:T(8,128)(2,1)S(1)}, s16[4192,128]{1,0:T(8,128)(2,1)}, u32[]{:S(2)}, u32[]{:S(2)}) collective-permute-start(s16[4192,128]{1,0:T(8,128)(2,1)S(1)} %shard_map.78), channel_id=1, source_target_pairs={{0,16},{8,24},{16,0},{24,8},{1,17},{9,25},{17,1},{25,9},{2,18},{10... | collective-permute-start | bytes 3219464 | tf_op jit(solution)/shard_map/ppermute | solution.py:419
  51.7 18.1 %collective-permute-start.9 = (s16[4112,128]{1,0:T(8,128)(2,1)S(1)}, s16[4112,128]{1,0:T(8,128)(2,1)S(1)}, u32[]{:S(2)}, u32[]{:S(2)}) collective-permute-start(s16[4112,128]{1,0:T(8,128)(2,1)S(1)} %shard_map.75.refs_0_), channel_id=1, source_target_pairs={{0,8},{8,0},{16,24},{24,16},{1,9},{9,1},{17,25},{25,17},{2,10},{10... | collective-permute-start | bytes 3158024 | tf_op jit(solution)/shard_map/ppermute | solution.py:416
  55.3 40.3 %collective-permute-start.8 = (bf16[1280,512]{1,0:T(8,128)(2,1)S(1)}, bf16[1280,512]{1,0:T(8,128)(2,1)S(1)}, u32[]{:S(2)}, u32[]{:S(2)}) collective-permute-start(bf16[1280,512]{1,0:T(8,128)(2,1)S(1)} %shard_map.77), channel_id=1, source_target_pairs={{2,0},{4,2},{6,4},{3,1},{5,3},{7,5},{10,8},{12,10},{14,12},{11,9},... | collective-permute-start | bytes 3932168 | tf_op jit(solution)/shard_map/ppermute | solution.py:425
  69.7 7.6 %collective-permute-start.13 = (bf16[1040,512]{1,0:T(8,128)(2,1)}, bf16[1040,512]{1,0:T(8,128)(2,1)}, u32[]{:S(2)}, u32[]{:S(2)}) collective-permute-start(bf16[1040,512]{1,0:T(8,128)(2,1)} %get-tuple-element.31.refs_0_), channel_id=1, source_target_pairs={{0,8},{8,0},{16,24},{24,16},{1,9},{9,1},{17,25},{25,17},{2,10},{10... | collective-permute-start | bytes 3194888 | tf_op jit(solution)/shard_map/ppermute | solution.py:416
  69.8 9.2 %collective-permute-start.14 = (bf16[1040,512]{1,0:T(8,128)(2,1)}, bf16[1040,512]{1,0:T(8,128)(2,1)}, u32[]{:S(2)}, u32[]{:S(2)}) collective-permute-start(bf16[1040,512]{1,0:T(8,128)(2,1)} %get-tuple-element.32.refs_2_), channel_id=1, source_target_pairs={{0,8},{8,0},{16,24},{24,16},{1,9},{9,1},{17,25},{25,17},{2,10},{10... | collective-permute-start | bytes 3194888 | tf_op jit(solution)/shard_map/ppermute | solution.py:416
  75.4 8.6 %collective-permute-start.12 = (s16[4128,128]{1,0:T(8,128)(2,1)}, s16[4128,128]{1,0:T(8,128)(2,1)}, u32[]{:S(2)}, u32[]{:S(2)}) collective-permute-start(s16[4128,128]{1,0:T(8,128)(2,1)} %shard_map.79.refs_0_), channel_id=1, source_target_pairs={{0,8},{8,0},{16,24},{24,16},{1,9},{9,1},{17,25},{25,17},{2,10},{10... | collective-permute-start | bytes 3170312 | tf_op jit(solution)/shard_map/ppermute | solution.py:416
  75.5 21.7 %collective-permute-start.1 = (bf16[768,512]{1,0:T(8,128)(2,1)}, bf16[768,512]{1,0:T(8,128)(2,1)}, u32[]{:S(2)}, u32[]{:S(2)}) collective-permute-start(bf16[768,512]{1,0:T(8,128)(2,1)} %get-tuple-element.25), channel_id=1, source_target_pairs={{0,1},{1,0},{2,3},{3,2},{4,5},{5,4},{6,7},{7,6},{8,9},{9,8},{10,11... | collective-permute-start | bytes 2359304 | tf_op jit(solution)/shard_map/ppermute | solution.py:422
  77.3 26.9 %collective-permute-start.17 = (s16[4128,128]{1,0:T(8,128)(2,1)}, s16[4128,128]{1,0:T(8,128)(2,1)}, u32[]{:S(2)}, u32[]{:S(2)}) collective-permute-start(s16[4128,128]{1,0:T(8,128)(2,1)} %shard_map.79.refs_0_), channel_id=1, source_target_pairs={{0,16},{8,24},{16,0},{24,8},{1,17},{9,25},{17,1},{25,9},{2,18},{10... | collective-permute-start | bytes 3170312 | tf_op jit(solution)/shard_map/ppermute | solution.py:419
  97.0 3.7 %collective-permute-start.15 = (bf16[896,512]{1,0:T(8,128)(2,1)}, bf16[896,512]{1,0:T(8,128)(2,1)S(1)}, u32[]{:S(2)}, u32[]{:S(2)}) collective-permute-start(bf16[896,512]{1,0:T(8,128)(2,1)} %get-tuple-element.35.refs_0_), channel_id=1, source_target_pairs={{0,8},{8,0},{16,24},{24,16},{1,9},{9,1},{17,25},{25,17},{2,10},{10... | collective-permute-start | bytes 2752520 | tf_op jit(solution)/shard_map/ppermute | solution.py:416
  97.1 7.1 %collective-permute-start.2 = (bf16[768,512]{1,0:T(8,128)(2,1)}, bf16[768,512]{1,0:T(8,128)(2,1)S(1)}, u32[]{:S(2)}, u32[]{:S(2)}) collective-permute-start(bf16[768,512]{1,0:T(8,128)(2,1)} %collective-permute-done.1.refs_0_), channel_id=1, source_target_pairs={{0,8},{8,0},{16,24},{24,16},{1,9},{9,1},{17,25},{25,17},{2,10},{10... | collective-permute-start | bytes 2359304 | tf_op jit(solution)/shard_map/ppermute | solution.py:416
  97.6 3.1 %collective-permute-start.16 = (bf16[384,512]{1,0:T(8,128)(2,1)S(1)}, bf16[384,512]{1,0:T(8,128)(2,1)S(1)}, u32[]{:S(2)}, u32[]{:S(2)}) collective-permute-start(bf16[384,512]{1,0:T(8,128)(2,1)S(1)} %get-tuple-element.36.refs_2_), channel_id=1, source_target_pairs={{0,8},{8,0},{16,24},{24,16},{1,9},{9,1},{17,25},{25,17},{2,10},{10... | collective-permute-start | bytes 1179656 | tf_op jit(solution)/shard_map/ppermute | solution.py:416
  104.2 3.4 %collective-permute-start.18 = (s16[4128,128]{1,0:T(8,128)(2,1)}, s16[4128,128]{1,0:T(8,128)(2,1)S(1)}, u32[]{:S(2)}, u32[]{:S(2)}) collective-permute-start(s16[4128,128]{1,0:T(8,128)(2,1)} %shard_map.86.refs_0_), channel_id=1, source_target_pairs={{0,8},{8,0},{16,24},{24,16},{1,9},{9,1},{17,25},{25,17},{2,10},{10... | collective-permute-start | bytes 3170312 | tf_op jit(solution)/shard_map/ppermute | solution.py:416

commit v5 on v4

--- a/solution.py
+++ b/solution.py
@@ -10,15 +10,18 @@
 
 LANES = 128
 TAIL = 16
-MORE = 16
+CHUNKS = 2
+MORE = 32
+PAD = 160
+LATE_PAD = 48
 FAR_TAILS = 3
-SIDE_TAILS = 6
+SIDE_TAILS = 16
 DONE = jax.ShapeDtypeStruct((8, LANES), jnp.float32)
 INNER = 2
 TOP = 32767.0
 VMEM_LIMIT = 26 << 20
-TOKEN_VMEM_LIMIT = 48 << 20
-FIRST_VMEM_LIMIT = 48 << 20
+TOKEN_VMEM_LIMIT = 47 << 20
+FIRST_VMEM_LIMIT = 47 << 20
 
 
 def params(limit=VMEM_LIMIT):
@@ -97,7 +100,7 @@
             slab = slice(j * LANES, (j + 1) * LANES)
             value = total_ref[pl.ds(r, step), slab]
             for c, scale in zip(codes, scales):
-                value = value + decoded(c, pl.multiple_of(j * whole + r, step), step, scale)
+                value = value + decoded(c, pl.multiple_of(r * slabs + j * step, step), step, scale)
             if codes:
                 total_ref[pl.ds(r, step), slab] = value
             largest = jnp.maximum(largest, jnp.max(jnp.abs(value).reshape(step // 8, 8, LANES), axis=0))
@@ -121,7 +124,7 @@
             value = total_ref[pl.ds(r, step), j * LANES : (j + 1) * LANES]
             root = jnp.round(jnp.sqrt(jnp.abs(value) * shrink) * TOP)
             level = jnp.where(value < 0.0, -root, root)
-            place = pl.ds(pl.multiple_of(j * rows + r, step), step)
+            place = pl.ds(pl.multiple_of(r * slabs + j * step, step), step)
             out_ref[place, :] = level.astype(jnp.int32).astype(jnp.int16)
         return carry
 
@@ -156,7 +159,23 @@
     )(kept, *codes, *waits)
 
 
-def token_kernel(where, slot, cycle, acts_ref, grads_ref, *refs, owners, sizes, n_codes, n_sources, n_waits, coded, moves, rows, block):
+def token_kernel(
+    where,
+    slot,
+    cycle,
+    acts_ref,
+    grads_ref,
+    *refs,
+    owners,
+    sizes,
+    n_codes,
+    n_sources,
+    n_waits,
+    coded,
+    moves,
+    rows,
+    block,
+):
     codes, sources, refs = refs[:n_codes], refs[n_codes : n_codes + n_sources], refs[n_codes + n_sources + n_waits :]
     groups = len(owners)
     outs, moved, refs = refs[:groups], refs[groups : groups + len(moves)], refs[groups + len(moves) :]
@@ -336,34 +355,41 @@
     out_ref, done_ref, code_refs, block_ref, sem = refs[-5:]
     slabs = width // LANES
     step = min(rows, 128)
-    coming = [pltpu.make_async_copy(refs[n], code_refs.at[n], sem.at[n]) for n in range(count)]
-    for c in coming:
-        c.start()
+    part = rows // CHUNKS
     copies = []
+
+    def copy(source, target):
+        copies.append(pltpu.make_async_copy(source, target, sem.at[len(copies)]))
+        copies[-1].start()
+        return copies[-1]
+
+    coming = []
     for n in range(count):
-        coming[n].wait()
+        tail = pl.ds(slabs * rows, TAIL)
+        coming.append([copy(refs[n].at[tail, :], code_refs.at[n, tail, :])])
+        for k in range(CHUNKS):
+            at = pl.ds(k * part * slabs, part * slabs)
+            coming[n].append(copy(refs[n].at[at, :], code_refs.at[n, at, :]))
+    leaving = []
+    for n in range(count):
+        coming[n][0].wait()
         scale = scale_of(code_refs.at[n], slabs * rows)
 
         def one(i, carry):
             r = pl.multiple_of(i * step, step)
             for j in range(slabs):
                 block_ref[n, pl.ds(r, step), j * LANES : (j + 1) * LANES] = decoded(
-                    code_refs.at[n], pl.multiple_of(j * rows + r, step), step, scale
+                    code_refs.at[n], pl.multiple_of(r * slabs + j * step, step), step, scale
                 )
             return carry
 
-        for k in range(2):
-            part = rows // 2
+        for k in range(CHUNKS):
+            coming[n][1 + k].wait()
             lax.fori_loop(k * part // step, (k + 1) * part // step, one, 0)
             at = pl.ds(k * part, part)
-            copies.append(
-                pltpu.make_async_copy(
-                    block_ref.at[n, at, :], out_ref.at[place[n], at, :], sem.at[count + 2 * n + k]
-                )
-            )
-            copies[-1].start()
+            leaving.append(copy(block_ref.at[n, at, :], out_ref.at[place[n], at, :]))
     done_ref[...] = jnp.zeros_like(done_ref)
-    for c in copies:
+    for c in leaving:
         c.wait()
 
 
@@ -390,7 +416,7 @@
             scratch_shapes=[
                 pltpu.VMEM((count, *codes[0].shape), jnp.int16),
                 pltpu.VMEM((count, rows, width), jnp.float32),
-                pltpu.SemaphoreType.DMA((3 * count,)),
+                pltpu.SemaphoreType.DMA(((2 * CHUNKS + 1) * count,)),
             ],
         ),
         input_output_aliases=aliases,
@@ -425,7 +451,7 @@
         return lax.ppermute(value, "pipe", [(d, d - 1) for d in range(1, n_pipe)])
 
     half = weight.shape[0] // INNER
-    late_part = max(half * 3 // 8 // LANES, 1) * LANES
+    late_part = half // 2 // LANES * LANES
 
     block = min(rows, features // pieces, 512)
     far = [(kx, ko) for ko in range(1, outer) for kx in range(1, n_ctx)]
@@ -454,7 +480,7 @@
         sources=(weight, grads.reshape(micro * tokens, width)),
         moves=(
             [(0, lambda w, b: w[2] * half, half), (1, lambda w, b: b[0] * tokens, tokens)],
-            [(0, lambda w, b: w[2] * half + late_part, half - late_part)],
+            [(0, lambda w, b: w[2] * half + late_part - PAD, half - late_part + PAD)],
         ),
         limit=FIRST_VMEM_LIMIT,
     )
@@ -467,12 +493,13 @@
     got = {w: to_outer(coded[w], w[1]) for w in far}
     sent = products(sent_by(near + side), True, [], *coded.values())
     theirs = [swap(c) for c in sent]
-    coded = dict(zip(near, products(kept_by(near), True, theirs[: len(near)], tails=SIDE_TAILS)))
+    coded = dict(zip(near, products(kept_by(near), True, theirs[: len(near)], tails=SIDE_TAILS - 6)))
     side_sums = products(kept_by(side), False, theirs[len(near) :], *coded.values())
 
     passed = passed_done = None
-
-    def pass_on(kx, start, pieces, *waits):
+    own_dones = []
+
+    def pass_on(kx, start, pieces, *waits, apart=False):
         nonlocal passed, passed_done
         parts = []
         for piece, rows in pieces:
@@ -480,7 +507,9 @@
             parts.append((piece, 0, rows, row + me_i * half))
             parts.append((swap(piece), 0, rows, row + (me_i + 1) % INNER * half))
             start = start + rows
-        passed, passed_done = key_products(current, parts, features, passed, *waits)
+        for some in (parts[0::2], parts[1::2]) if apart else (parts,):
+            passed, passed_done = key_products(current, some, features, passed, *waits)
+            own_dones.append(passed_done)
         return [x for x, _, _, _ in parts[1::2]]
 
     values = [
@@ -497,12 +526,12 @@
         z_all,
         (0, half // 2 + MORE),
         (half // 2, half - half // 2 + MORE),
-        (0, late_part),
+        (0, late_part + LATE_PAD),
         (half, tokens),
     )
     z_pieces = [(z_first, half // 2), (z_second, half - half // 2)]
     codes = [home_theirs, *[got[0, ko] for ko in range(1, outer)], *crossed]
-    own = combine(home_kept, codes, current, tails=2)
+    own = combine(home_kept, codes, current, tails=4)
     others = {ko: to_outer(own, ko) for ko in range(1, outer)}
     late = [to_ctx(late, kx) for kx in range(1, n_ctx)]
     pass_on(0, 0, z_pieces)
@@ -516,15 +545,14 @@
         passed_done,
     )
     most = half - late_part
-    first = min(-(-most * 11 // 16 // LANES) * LANES, most - LANES)
     for kx in range(1, n_ctx):
         held = after(z_crossed[kx - 1], result_done)
-        pieces = split(held, (0, first), (first, most - first))
-        pass_on(kx, late_part, [(pieces[0], first), (pieces[1], most - first)])
+        pass_on(kx, late_part, [(split(held, (PAD, most))[0], most)], apart=True)
     crossed_done = passed_done
+    late = [after(x, own_dones[-2]) for x in late]
     late_theirs = []
     for kx in range(1, n_ctx):
-        late_theirs += pass_on(kx, 0, [(late[kx - 1], late_part)])
+        late_theirs += pass_on(kx, 0, [(split(late[kx - 1], (0, late_part))[0], late_part)])
     for ko in range(1, outer):
         other = after(others[ko], crossed_done, *late_theirs)
         o = (me_o - ko) % outer

time: 113 us -> 110 us (0.973)
  waiting for transfers between devices: 27.8 us -> 26.3 us
    ppermute x11 -> x10, waiting for transfers between devices: 5.1 us -> 2.75 us  [swap(): return lax.ppermute(value, 'dp', pairs)]
    ppermute x3, waiting for transfers between devices: 4.09 us -> 5.83 us  [to_outer(): lax.ppermute(value, 'dp', [(d, (d + by * INNER) % n_dp) for d in range(n_...]
    pallas_call x3, Pallas kernels: 8.98 us -> 7.72 us  [combine(): pl.pallas_call(functools.partial(combine_kernel, n_codes=len(codes), rows...]
    pallas_call x2 -> x3, Pallas kernels: 3.33 us -> 4.59 us  [split(): pl.pallas_call(functools.partial(split_kernel, cuts=cuts), out_shape=shap...]
    pallas_call x3 -> x4, Pallas kernels: 11.5 us -> 10.9 us  [key_products(): pl.pallas_call(functools.partial(key_kernel, segments=[(skip, rows) for _...]
    ppermute x11 -> x10, starting transfers between devices: 2.66 us -> 2.38 us  [swap(): return lax.ppermute(value, 'dp', pairs)]
  transfers between devices with their start and end apart: 19 -> 18, of which waited for: 5 -> 6; matrix products, arithmetic and copies ran while one was open for 0% -> 0% of each run, Pallas kernels for 47% -> 48%
where the time goes in v5:
time: 110 us
  Pallas kernels  64.1 us (58%)
  waiting for transfers between devices  26.3 us (24%)
  starting transfers between devices  15.5 us (14%)
  local copies, waits for them, and re-layouts  1.9 us (2%)
  between operations  1.69 us (2%)
    pallas_call x6, Pallas kernels, token_products(): pl.pallas_call(functools.partial(token_kernel, owners=owners, sizes=sizes...  32.5 us
    ppermute x2, waiting for transfers between devices, to_previous(): return lax.ppermute(value, 'pipe', [(d, d - 1) for d in range(1, n_pipe)])  17.7 us
    pallas_call x4, Pallas kernels, key_products(): pl.pallas_call(functools.partial(key_kernel, segments=[(skip, rows) for _...  10.9 us
    pallas_call x2, Pallas kernels, decode(): pl.pallas_call(functools.partial(decode_kernel, count=count, rows=rows, w...  8.34 us
    pallas_call x3, Pallas kernels, combine(): pl.pallas_call(functools.partial(combine_kernel, n_codes=len(codes), rows...  7.72 us
    ppermute x3, waiting for transfers between devices, to_outer(): lax.ppermute(value, 'dp', [(d, (d + by * INNER) % n_dp) for d in range(n_...  5.83 us
    ppermute x3, starting transfers between devices, to_ctx(): lax.ppermute(value, 'ctx', [(d, (d + by) % n_ctx) for d in range(n_ctx)])  5.79 us
    ppermute x3, starting transfers between devices, to_outer(): lax.ppermute(value, 'dp', [(d, (d + by * INNER) % n_dp) for d in range(n_...  4.6 us
  transfers between devices with their start and end apart: 18, of which 6 were waited for; matrix products, arithmetic and copies ran while one was open for 0% of the time, Pallas kernels for 48%

profile of v5, /device:TPU:0, one launch (start us, length us, event | category | flops | bytes accessed | tf_op | source)
XLA Modules:
  0.0 109.9 jit_solution(546571235182291819)
XLA Ops:
  1.3 0.1 pad_add_fusion.1.where
  1.4 0.0 copy-start
  1.4 1.2 %copy-done = bf16[1,1,4,272,512]{4,3,2,1,0:T(8,128)(2,1)S(1)} copy-done((bf16[1,1,4,272,512]{4,3,2,1,0:T(8,128)(2,1)S(1)}, bf16[1,1,4,272,512]{4,3,2,1,0:T(8,128)(2,1)}, u32[]{:S(2)}) %copy-start) | copy-done | bytes 1114136
  2.6 0.0 copy-start.1
  2.6 0.7 copy-done.1
  3.3 7.0 %shard_map.68 = (s16[4112,128]{1,0:T(8,128)(2,1)S(1)}, f32[1,1024,512]{2,1,0:T(8,128)S(1)}, bf16[2320,512]{1,0:T(8,128)(2,1)}, bf16[1184,512]{1,0:T(8,128)(2,1)S(1)}) custom-call(s32[3]{0:T(128)S(1)} %pad_add_fusion.1.where, s32[1]{0:T(128)S(6)} %copy.25.slot, s32[8]{0:T(128)S(1)} %copy-done.1, bf16[4,272,8192]{2,1,0:T(8,128)(2,1)} %bitcast.28, ...), custom_call_target="tpu_custom_call" | custom-call | tf_op jit(solution)/shard_map/pallas_call | solution.py:278
  10.2 0.5 collective-permute-start.3
  10.8 1.3 %collective-permute-start = (bf16[2320,512]{1,0:T(8,128)(2,1)}, bf16[2320,512]{1,0:T(8,128)(2,1)S(1)}, u32[]{:S(2)}, u32[]{:S(2)}) collective-permute-start(bf16[2320,512]{1,0:T(8,128)(2,1)} %get-tuple-element.23), channel_id=1, source_target_pairs={{2,0},{4,2},{6,4},{3,1},{5,3},{7,5},{10,8},{12,10},{14,12},{11,9},... | collective-permute-start | bytes 7127048 | tf_op jit(solution)/shard_map/ppermute | solution.py:451
  12.0 2.6 %collective-permute-start.2 = (bf16[1184,512]{1,0:T(8,128)(2,1)S(1)}, bf16[1184,512]{1,0:T(8,128)(2,1)S(1)}, u32[]{:S(2)}, u32[]{:S(2)}) collective-permute-start(bf16[1184,512]{1,0:T(8,128)(2,1)S(1)} %get-tuple-element.26), channel_id=1, source_target_pairs={{0,1},{1,0},{2,3},{3,2},{4,5},{5,4},{6,7},{7,6},{8,9},{9,8},{10,11... | collective-permute-start | bytes 3637256 | tf_op jit(solution)/shard_map/ppermute | solution.py:448
  14.6 0.0 collective-permute-done.3.refs_0_
  14.6 2.0 %shard_map.70.refs_0_ = s16[4144,128]{1,0:T(8,128)(2,1)S(1)} custom-call(f32[1,1024,512]{2,1,0:T(8,128)S(1)} %get-tuple-element.27.kept_ref, s16[4112,128]{1,0:T(8,128)(2,1)S(1)} %collective-permute-done.3.refs_0_), custom_call_target="tpu_custom_call" | custom-call | tf_op jit(solution)/shard_map/pallas_call | solution.py:151
  16.6 1.6 %collective-permute-start.6 = (s16[4144,128]{1,0:T(8,128)(2,1)S(1)}, s16[4144,128]{1,0:T(8,128)(2,1)S(1)}, u32[]{:S(2)}, u32[]{:S(2)}) collective-permute-start(s16[4144,128]{1,0:T(8,128)(2,1)S(1)} %shard_map.70.refs_0_), channel_id=1, source_target_pairs={{0,16},{8,24},{16,0},{24,8},{1,17},{9,25},{17,1},{25,9},{2,18},{10... | collective-permute-start | bytes 3182600 | tf_op jit(solution)/shard_map/ppermute | solution.py:445
  18.2 8.0 %shard_map.71 = (s16[4112,128]{1,0:T(8,128)(2,1)S(1)}, s16[4112,128]{1,0:T(8,128)(2,1)S(1)}) custom-call(s32[3]{0:T(128)S(1)} %pad_add_fusion.1.where, s32[1]{0:T(128)S(6)} %copy.25.slot, s32[8]{0:T(128)S(1)} %copy-done.1, bf16[4,272,8192]{2,1,0:T(8,128)(2,1)} %bitcast.29, bf16[4,272,512]{2,1,0:T(8,128)(2,1)S(1)} %bitcast.23, ...), custom_call_target="tpu_custom_call" | custom-call | tf_op jit(solution)/shard_map/pallas_call | solution.py:278
  26.2 0.1 collective-permute-start.5
  26.2 0.5 collective-permute-start.4
  26.7 2.2 %collective-permute-done.5.refs_0_ = s16[4112,128]{1,0:T(8,128)(2,1)S(1)} collective-permute-done((s16[4112,128]{1,0:T(8,128)(2,1)S(1)}, s16[4112,128]{1,0:T(8,128)(2,1)S(1)}, u32[]{:S(2)}, u32[]{:S(2)}) %collective-permute-start.5) | collective-permute-done | bytes 1052704 | tf_op jit(solution)/shard_map/ppermute | solution.py:442
  28.9 5.3 %shard_map.72.refs_1_.refs_0_ = s16[4256,128]{1,0:T(8,128)(2,1)S(1)} custom-call(s32[3]{0:T(128)S(1)} %pad_add_fusion.1.where, s32[1]{0:T(128)S(6)} %copy.25.slot, s32[8]{0:T(128)S(1)} %copy-done.1, bf16[4,272,8192]{2,1,0:T(8,128)(2,1)} %bitcast.30, bf16[4,272,512]{2,1,0:T(8,128)(2,1)S(1)} %bitcast.24, s16[4112,128]{1,0:T(8,128)(2,1)S(1)} %collective-permute-done.5.refs_0_), custom_call_target="tpu_custom_call" | custom-call | tf_op jit(solution)/shard_map/pallas_call | solution.py:278
  34.2 0.0 collective-permute-done.4.refs_0_
  34.2 4.0 %shard_map.73.kept_ref = f32[1,1024,512]{2,1,0:T(8,128)S(1)} custom-call(s32[3]{0:T(128)S(1)} %pad_add_fusion.1.where, s32[1]{0:T(128)S(6)} %copy.25.slot, s32[8]{0:T(128)S(1)} %copy-done.1, bf16[4,272,8192]{2,1,0:T(8,128)(2,1)} %bitcast.31, bf16[4,272,512]{2,1,0:T(8,128)(2,1)S(1)} %bitcast.25, s16[4112,128]{1,0:T(8,128)(2,1)S(1)} %collective-permute-done.4.refs_0_, ...), custom_call_target="tpu_custom_call" | custom-call | tf_op jit(solution)/shard_map/pallas_call | solution.py:278
  38.2 4.0 %collective-permute-done.6.refs_0_ = s16[4144,128]{1,0:T(8,128)(2,1)S(1)} collective-permute-done((s16[4144,128]{1,0:T(8,128)(2,1)S(1)}, s16[4144,128]{1,0:T(8,128)(2,1)S(1)}, u32[]{:S(2)}, u32[]{:S(2)}) %collective-permute-start.6) | collective-permute-done | bytes 1060896 | tf_op jit(solution)/shard_map/ppermute | solution.py:445
  42.2 2.0 %shard_map.74.refs_0_.refs_1_ = s16[4368,128]{1,0:T(8,128)(2,1)S(1)} custom-call(f32[1,1024,512]{2,1,0:T(8,128)S(1)} %shard_map.73.kept_ref, s16[4144,128]{1,0:T(8,128)(2,1)S(1)} %collective-permute-done.6.refs_0_), custom_call_target="tpu_custom_call" | custom-call | tf_op jit(solution)/shard_map/pallas_call | solution.py:151
  44.2 1.3 %collective-permute-start.10 = (s16[4368,128]{1,0:T(8,128)(2,1)S(1)}, s16[4368,128]{1,0:T(8,128)(2,1)S(1)}, u32[]{:S(2)}, u32[]{:S(2)}) collective-permute-start(s16[4368,128]{1,0:T(8,128)(2,1)S(1)} %shard_map.74.refs_0_.refs_1_), channel_id=1, source_target_pairs={{0,1},{1,0},{2,3},{3,2},{4,5},{5,4},{6,7},{7,6},{8,9},{9,8},{10,11... | collective-permute-start | bytes 3354632 | tf_op jit(solution)/shard_map/ppermute | solution.py:448
  45.5 1.5 %collective-permute-start.9 = (s16[4256,128]{1,0:T(8,128)(2,1)S(1)}, s16[4256,128]{1,0:T(8,128)(2,1)S(1)}, u32[]{:S(2)}, u32[]{:S(2)}) collective-permute-start(s16[4256,128]{1,0:T(8,128)(2,1)S(1)} %shard_map.78), channel_id=1, source_target_pairs={{0,16},{8,24},{16,0},{24,8},{1,17},{9,25},{17,1},{25,9},{2,18},{10... | collective-permute-start | bytes 3268616 | tf_op jit(solution)/shard_map/ppermute | solution.py:445
  47.0 0.0 collective-permute-done.2.refs_1_.refs_0_
  47.0 4.9 %shard_map.75.refs_0_ = s16[4112,128]{1,0:T(8,128)(2,1)S(1)} custom-call(s32[3]{0:T(128)S(1)} %pad_add_fusion.1.where, s32[1]{0:T(128)S(6)} %copy.25.slot, s32[8]{0:T(128)S(1)} %copy-done.1, bf16[4,272,8192]{2,1,0:T(8,128)(2,1)} %bitcast.32, bf16[4,272,512]{2,1,0:T(8,128)(2,1)S(1)} %bitcast.26, s16[4368,128]{1,0:T(8,128)(2,1)S(1)} %shard_map.74.refs_0_.refs_1_, ...), custom_call_target="tpu_custom_call" | custom-call | tf_op jit(solution)/shard_map/pallas_call | solution.py:278
  51.9 0.1 collective-permute-start.8
  51.9 3.5 %shard_map.76.refs_1_.kept_ref = f32[1,1024,512]{2,1,0:T(8,128)S(1)} custom-call(s32[3]{0:T(128)S(1)} %pad_add_fusion.1.where, s32[1]{0:T(128)S(6)} %copy.25.slot, s32[8]{0:T(128)S(1)} %copy-done.1, bf16[4,272,8192]{2,1,0:T(8,128)(2,1)} %bitcast.33, bf16[4,272,512]{2,1,0:T(8,128)(2,1)S(1)} %bitcast.27, s16[4112,128]{1,0:T(8,128)(2,1)S(1)} %shard_map.75.refs_0_), custom_call_target="tpu_custom_call" | custom-call | tf_op jit(solution)/shard_map/pallas_call | solution.py:278
  55.4 1.5 %collective-permute-start.7 = (bf16[1184,512]{1,0:T(8,128)(2,1)S(1)}, bf16[1184,512]{1,0:T(8,128)(2,1)S(1)}, u32[]{:S(2)}, u32[]{:S(2)}) collective-permute-start(bf16[1184,512]{1,0:T(8,128)(2,1)S(1)} %shard_map.77), channel_id=1, source_target_pairs={{2,0},{4,2},{6,4},{3,1},{5,3},{7,5},{10,8},{12,10},{14,12},{11,9},... | collective-permute-start | bytes 3637256 | tf_op jit(solution)/shard_map/ppermute | solution.py:451
  56.9 11.0 %collective-permute-done.value_ref = bf16[2320,512]{1,0:T(8,128)(2,1)S(1)} collective-permute-done((bf16[2320,512]{1,0:T(8,128)(2,1)}, bf16[2320,512]{1,0:T(8,128)(2,1)S(1)}, u32[]{:S(2)}, u32[]{:S(2)}) %collective-permute-start) | collective-permute-done | bytes 2375712 | tf_op jit(solution)/shard_map/ppermute | solution.py:451
  67.9 2.2 %shard_map.69 = (bf16[1056,512]{1,0:T(8,128)(2,1)}, bf16[1056,512]{1,0:T(8,128)(2,1)}, bf16[1072,512]{1,0:T(8,128)(2,1)}, bf16[272,512]{1,0:T(8,128)(2,1)S(1)}) custom-call(bf16[2320,512]{1,0:T(8,128)(2,1)S(1)} %collective-permute-done.value_ref), custom_call_target="tpu_custom_call" | custom-call | tf_op jit(solution)/shard_map/pallas_call | solution.py:80
  70.1 0.1 collective-permute-start.12
  70.2 0.0 collective-permute-done.8.refs_0_
  70.2 1.9 %collective-permute-start.1 = (bf16[1072,512]{1,0:T(8,128)(2,1)}, bf16[1072,512]{1,0:T(8,128)(2,1)}, u32[]{:S(2)}, u32[]{:S(2)}) collective-permute-start(bf16[1072,512]{1,0:T(8,128)(2,1)} %get-tuple-element.25), channel_id=1, source_target_pairs={{0,1},{1,0},{2,3},{3,2},{4,5},{5,4},{6,7},{7,6},{8,9},{9,8},{10,11... | collective-permute-start | bytes 3293192 | tf_op jit(solution)/shard_map/ppermute | solution.py:448
  72.1 0.0 collective-permute-done.9.refs_1_
  72.1 0.2 collective-permute-start.13
  72.3 0.0 collective-permute-done.10.refs_2_
  72.3 3.8 %shard_map.79.refs_0_ = s16[4160,128]{1,0:T(8,128)(2,1)} custom-call(f32[1,1024,512]{2,1,0:T(8,128)S(1)} %shard_map.76.refs_1_.kept_ref, s16[4112,128]{1,0:T(8,128)(2,1)S(1)} %collective-permute-done.8.refs_0_, s16[4256,128]{1,0:T(8,128)(2,1)S(1)} %collective-permute-done.9.refs_1_, s16[4368,128]{1,0:T(8,128)(2,1)S(1)} %collective-permute-done.10.refs_2_, ...), custom_call_target="tpu_custom_call" | custom-call | tf_op jit(solution)/shard_map/pallas_call | solution.py:151
  76.1 0.4 collective-permute-start.11
  76.4 0.1 pad_add_fusion.2.place
  76.5 0.0 collective-permute-done.12.refs_1_
  76.5 1.5 %collective-permute-start.16 = (s16[4160,128]{1,0:T(8,128)(2,1)}, s16[4160,128]{1,0:T(8,128)(2,1)}, u32[]{:S(2)}, u32[]{:S(2)}) collective-permute-start(s16[4160,128]{1,0:T(8,128)(2,1)} %shard_map.79.refs_0_), channel_id=1, source_target_pairs={{0,16},{8,24},{16,0},{24,8},{1,17},{9,25},{17,1},{25,9},{2,18},{10... | collective-permute-start | bytes 3194888 | tf_op jit(solution)/shard_map/ppermute | solution.py:445
  78.0 0.1 pad_add_fusion.3.starts
  78.1 0.0 collective-permute-done.13.refs_3_
  78.1 4.9 %shard_map.80 = (bf16[272,8192]{1,0:T(8,128)(2,1)}, f32[8,128]{1,0:T(8,128)S(1)}) custom-call(s32[4]{0:T(128)S(1)} %pad_add_fusion.3.starts, bf16[272,512]{1,0:T(8,128)(2,1)S(1)} %get-tuple-element.24.refs_3_.current_ref, bf16[1056,512]{1,0:T(8,128)(2,1)} %get-tuple-element.31.refs_0_, bf16[1056,512]{1,0:T(8,128)(2,1)} %collective-permute-done.12.refs_1_, ...), custom_call_target="tpu_custom_call" | custom-call | tf_op jit(solution)/shard_map/pallas_call | solution.py:338
  83.0 0.0 collective-permute-done.11.refs_1_
  83.1 3.9 %shard_map.81 = (f32[4,1024,512]{2,1,0:T(8,128)}, f32[8,128]{1,0:T(8,128)S(1)}) custom-call(s32[2]{0:T(128)S(1)} %pad_add_fusion.2.place, s16[4160,128]{1,0:T(8,128)(2,1)} %shard_map.79.refs_0_, s16[4160,128]{1,0:T(8,128)(2,1)} %collective-permute-done.11.refs_1_, f32[8,128]{1,0:T(8,128)S(1)} %get-tuple-element.33.refs_2_), custom_call_target="tpu_custom_call" | custom-call | tf_op jit(solution)/shard_map/pallas_call | solution.py:408
  86.9 6.7 %collective-permute-done.7.refs_0_ = bf16[1184,512]{1,0:T(8,128)(2,1)S(1)} collective-permute-done((bf16[1184,512]{1,0:T(8,128)(2,1)S(1)}, bf16[1184,512]{1,0:T(8,128)(2,1)S(1)}, u32[]{:S(2)}, u32[]{:S(2)}) %collective-permute-start.7) | collective-permute-done | bytes 1212448 | tf_op jit(solution)/shard_map/ppermute | solution.py:451
  93.7 1.1 shard_map.83.refs_0_
  94.8 0.1 collective-permute-start.15
  94.9 2.5 %shard_map.84 = (bf16[272,8192]{1,0:T(8,128)(2,1)}, f32[8,128]{1,0:T(8,128)S(1)}) custom-call(s32[1]{0:T(128)} %bitcast.9.starts, bf16[272,512]{1,0:T(8,128)(2,1)S(1)} %get-tuple-element.24.refs_3_.current_ref, bf16[1024,512]{1,0:T(8,128)(2,1)} %shard_map.83.refs_0_, bf16[272,8192]{1,0:T(8,128)(2,1)} %get-tuple-element.35.refs_1_), custom_call_target="tpu_custom_call", output_to_operand_aliasing={{0}: (3, {})} | custom-call | tf_op jit(solution)/shard_map/pallas_call | solution.py:338
  97.4 0.0 collective-permute-done.1.refs_0_
  97.4 1.3 %shard_map.86.refs_0_ = bf16[1024,512]{1,0:T(8,128)(2,1)S(1)} custom-call(bf16[1072,512]{1,0:T(8,128)(2,1)} %shard_map.85.value_ref), custom_call_target="tpu_custom_call" | custom-call | tf_op jit(solution)/shard_map/pallas_call | solution.py:80
  98.7 0.6 collective-permute-start.14
  99.3 0.0 collective-permute-done.15.refs_0_
  99.3 1.3 %shard_map.87 = (bf16[272,8192]{1,0:T(8,128)(2,1)}, f32[8,128]{1,0:T(8,128)S(1)}) custom-call(s32[1]{0:T(128)} %bitcast.16.starts, bf16[272,512]{1,0:T(8,128)(2,1)S(1)} %get-tuple-element.24.refs_3_.current_ref, bf16[1024,512]{1,0:T(8,128)(2,1)S(1)} %collective-permute-done.15.refs_0_, ...), custom_call_target="tpu_custom_call", output_to_operand_aliasing={{0}: (3, {})} | custom-call | tf_op jit(solution)/shard_map/pallas_call | solution.py:338
  100.6 1.8 %collective-permute-done.16.refs_0_ = s16[4160,128]{1,0:T(8,128)(2,1)} collective-permute-done((s16[4160,128]{1,0:T(8,128)(2,1)}, s16[4160,128]{1,0:T(8,128)(2,1)}, u32[]{:S(2)}, u32[]{:S(2)}) %collective-permute-start.16) | collective-permute-done | bytes 1064992 | tf_op jit(solution)/shard_map/ppermute | solution.py:445
  102.4 0.0 collective-permute-done.14.refs_1_.refs_2_
  102.4 0.0 collective-permute-start.17
  102.4 0.1 pad_add_fusion.starts
  102.5 0.1 pad_add_fusion.4.place
  102.5 2.2 %shard_map.88 = (bf16[272,8192]{1,0:T(8,128)(2,1)}, f32[8,128]{1,0:T(8,128)S(1)}) custom-call(s32[2]{0:T(128)S(1)} %pad_add_fusion.starts, bf16[272,512]{1,0:T(8,128)(2,1)S(1)} %get-tuple-element.24.refs_3_.current_ref, bf16[1024,512]{1,0:T(8,128)(2,1)S(1)} %shard_map.86.refs_0_, ...), custom_call_target="tpu_custom_call", output_to_operand_aliasing={{0}: (4, {})} | custom-call | tf_op jit(solution)/shard_map/pallas_call | solution.py:338
  104.7 0.6 collective-permute-done.17.refs_1_
  105.3 4.5 %shard_map.90 = (f32[4,1024,512]{2,1,0:T(8,128)}, f32[8,128]{1,0:T(8,128)}) custom-call(s32[2]{0:T(128)S(1)} %pad_add_fusion.4.place, s16[4160,128]{1,0:T(8,128)(2,1)} %shard_map.89.refs_0_, s16[4160,128]{1,0:T(8,128)(2,1)S(1)} %collective-permute-done.17.refs_1_, f32[4,1024,512]{2,1,0:T(8,128)} %get-tuple-element.41.refs_2_, ...), custom_call_target="tpu_custom_call", output_to_operand_aliasing={{0}: (3, {})} | custom-call | tf_op jit(solution)/shard_map/pallas_call | solution.py:408
  (5 shorter events, 0.0 us)
Async XLA Ops:
  1.4 1.2 %copy-start = (bf16[1,1,4,272,512]{4,3,2,1,0:T(8,128)(2,1)S(1)}, bf16[1,1,4,272,512]{4,3,2,1,0:T(8,128)(2,1)}, u32[]{:S(2)}) copy-start(bf16[1,1,4,272,512]{4,3,2,1,0:T(8,128)(2,1)} %param.6) | copy-start | bytes 3342340
  2.6 0.7 copy-start.1
  10.2 4.4 %collective-permute-start.3 = (s16[4112,128]{1,0:T(8,128)(2,1)S(1)}, s16[4112,128]{1,0:T(8,128)(2,1)S(1)}, u32[]{:S(2)}, u32[]{:S(2)}) collective-permute-start(s16[4112,128]{1,0:T(8,128)(2,1)S(1)} %get-tuple-element.28), channel_id=1, source_target_pairs={{0,8},{8,0},{16,24},{24,16},{1,9},{9,1},{17,25},{25,17},{2,10},{10... | collective-permute-start | bytes 3158024 | tf_op jit(solution)/shard_map/ppermute | solution.py:442
  10.8 57.1 %collective-permute-start = (bf16[2320,512]{1,0:T(8,128)(2,1)}, bf16[2320,512]{1,0:T(8,128)(2,1)S(1)}, u32[]{:S(2)}, u32[]{:S(2)}) collective-permute-start(bf16[2320,512]{1,0:T(8,128)(2,1)} %get-tuple-element.23), channel_id=1, source_target_pairs={{2,0},{4,2},{6,4},{3,1},{5,3},{7,5},{10,8},{12,10},{14,12},{11,9},... | collective-permute-start | bytes 7127048 | tf_op jit(solution)/shard_map/ppermute | solution.py:451
  12.0 34.9 %collective-permute-start.2 = (bf16[1184,512]{1,0:T(8,128)(2,1)S(1)}, bf16[1184,512]{1,0:T(8,128)(2,1)S(1)}, u32[]{:S(2)}, u32[]{:S(2)}) collective-permute-start(bf16[1184,512]{1,0:T(8,128)(2,1)S(1)} %get-tuple-element.26), channel_id=1, source_target_pairs={{0,1},{1,0},{2,3},{3,2},{4,5},{5,4},{6,7},{7,6},{8,9},{9,8},{10,11... | collective-permute-start | bytes 3637256 | tf_op jit(solution)/shard_map/ppermute | solution.py:448
  16.6 25.6 %collective-permute-start.6 = (s16[4144,128]{1,0:T(8,128)(2,1)S(1)}, s16[4144,128]{1,0:T(8,128)(2,1)S(1)}, u32[]{:S(2)}, u32[]{:S(2)}) collective-permute-start(s16[4144,128]{1,0:T(8,128)(2,1)S(1)} %shard_map.70.refs_0_), channel_id=1, source_target_pairs={{0,16},{8,24},{16,0},{24,8},{1,17},{9,25},{17,1},{25,9},{2,18},{10... | collective-permute-start | bytes 3182600 | tf_op jit(solution)/shard_map/ppermute | solution.py:445
  26.2 2.7 %collective-permute-start.5 = (s16[4112,128]{1,0:T(8,128)(2,1)S(1)}, s16[4112,128]{1,0:T(8,128)(2,1)S(1)}, u32[]{:S(2)}, u32[]{:S(2)}) collective-permute-start(s16[4112,128]{1,0:T(8,128)(2,1)S(1)} %get-tuple-element.30), channel_id=1, source_target_pairs={{0,8},{8,0},{16,24},{24,16},{1,9},{9,1},{17,25},{25,17},{2,10},{10... | collective-permute-start | bytes 3158024 | tf_op jit(solution)/shard_map/ppermute | solution.py:442
  26.2 8.0 %collective-permute-start.4 = (s16[4112,128]{1,0:T(8,128)(2,1)S(1)}, s16[4112,128]{1,0:T(8,128)(2,1)S(1)}, u32[]{:S(2)}, u32[]{:S(2)}) collective-permute-start(s16[4112,128]{1,0:T(8,128)(2,1)S(1)} %get-tuple-element.29), channel_id=1, source_target_pairs={{0,8},{8,0},{16,24},{24,16},{1,9},{9,1},{17,25},{25,17},{2,10},{10... | collective-permute-start | bytes 3158024 | tf_op jit(solution)/shard_map/ppermute | solution.py:442
  44.2 28.1 %collective-permute-start.10 = (s16[4368,128]{1,0:T(8,128)(2,1)S(1)}, s16[4368,128]{1,0:T(8,128)(2,1)S(1)}, u32[]{:S(2)}, u32[]{:S(2)}) collective-permute-start(s16[4368,128]{1,0:T(8,128)(2,1)S(1)} %shard_map.74.refs_0_.refs_1_), channel_id=1, source_target_pairs={{0,1},{1,0},{2,3},{3,2},{4,5},{5,4},{6,7},{7,6},{8,9},{9,8},{10,11... | collective-permute-start | bytes 3354632 | tf_op jit(solution)/shard_map/ppermute | solution.py:448
  45.5 26.7 %collective-permute-start.9 = (s16[4256,128]{1,0:T(8,128)(2,1)S(1)}, s16[4256,128]{1,0:T(8,128)(2,1)S(1)}, u32[]{:S(2)}, u32[]{:S(2)}) collective-permute-start(s16[4256,128]{1,0:T(8,128)(2,1)S(1)} %shard_map.78), channel_id=1, source_target_pairs={{0,16},{8,24},{16,0},{24,8},{1,17},{9,25},{17,1},{25,9},{2,18},{10... | collective-permute-start | bytes 3268616 | tf_op jit(solution)/shard_map/ppermute | solution.py:445
  51.9 18.3 %collective-permute-start.8 = (s16[4112,128]{1,0:T(8,128)(2,1)S(1)}, s16[4112,128]{1,0:T(8,128)(2,1)S(1)}, u32[]{:S(2)}, u32[]{:S(2)}) collective-permute-start(s16[4112,128]{1,0:T(8,128)(2,1)S(1)} %shard_map.75.refs_0_), channel_id=1, source_target_pairs={{0,8},{8,0},{16,24},{24,16},{1,9},{9,1},{17,25},{25,17},{2,10},{10... | collective-permute-start | bytes 3158024 | tf_op jit(solution)/shard_map/ppermute | solution.py:442
  55.4 38.2 %collective-permute-start.7 = (bf16[1184,512]{1,0:T(8,128)(2,1)S(1)}, bf16[1184,512]{1,0:T(8,128)(2,1)S(1)}, u32[]{:S(2)}, u32[]{:S(2)}) collective-permute-start(bf16[1184,512]{1,0:T(8,128)(2,1)S(1)} %shard_map.77), channel_id=1, source_target_pairs={{2,0},{4,2},{6,4},{3,1},{5,3},{7,5},{10,8},{12,10},{14,12},{11,9},... | collective-permute-start | bytes 3637256 | tf_op jit(solution)/shard_map/ppermute | solution.py:451
  70.1 6.4 %collective-permute-start.12 = (bf16[1056,512]{1,0:T(8,128)(2,1)}, bf16[1056,512]{1,0:T(8,128)(2,1)}, u32[]{:S(2)}, u32[]{:S(2)}) collective-permute-start(bf16[1056,512]{1,0:T(8,128)(2,1)} %get-tuple-element.31.refs_0_), channel_id=1, source_target_pairs={{0,8},{8,0},{16,24},{24,16},{1,9},{9,1},{17,25},{25,17},{2,10},{10... | collective-permute-start | bytes 3244040 | tf_op jit(solution)/shard_map/ppermute | solution.py:442
  70.2 27.2 %collective-permute-start.1 = (bf16[1072,512]{1,0:T(8,128)(2,1)}, bf16[1072,512]{1,0:T(8,128)(2,1)}, u32[]{:S(2)}, u32[]{:S(2)}) collective-permute-start(bf16[1072,512]{1,0:T(8,128)(2,1)} %get-tuple-element.25), channel_id=1, source_target_pairs={{0,1},{1,0},{2,3},{3,2},{4,5},{5,4},{6,7},{7,6},{8,9},{9,8},{10,11... | collective-permute-start | bytes 3293192 | tf_op jit(solution)/shard_map/ppermute | solution.py:448
  72.1 6.0 %collective-permute-start.13 = (bf16[1056,512]{1,0:T(8,128)(2,1)}, bf16[1056,512]{1,0:T(8,128)(2,1)}, u32[]{:S(2)}, u32[]{:S(2)}) collective-permute-start(bf16[1056,512]{1,0:T(8,128)(2,1)} %get-tuple-element.32.refs_2_), channel_id=1, source_target_pairs={{0,8},{8,0},{16,24},{24,16},{1,9},{9,1},{17,25},{25,17},{2,10},{10... | collective-permute-start | bytes 3244040 | tf_op jit(solution)/shard_map/ppermute | solution.py:442
  76.1 7.0 %collective-permute-start.11 = (s16[4160,128]{1,0:T(8,128)(2,1)}, s16[4160,128]{1,0:T(8,128)(2,1)}, u32[]{:S(2)}, u32[]{:S(2)}) collective-permute-start(s16[4160,128]{1,0:T(8,128)(2,1)} %shard_map.79.refs_0_), channel_id=1, source_target_pairs={{0,8},{8,0},{16,24},{24,16},{1,9},{9,1},{17,25},{25,17},{2,10},{10... | collective-permute-start | bytes 3194888 | tf_op jit(solution)/shard_map/ppermute | solution.py:442
  76.5 25.9 %collective-permute-start.16 = (s16[4160,128]{1,0:T(8,128)(2,1)}, s16[4160,128]{1,0:T(8,128)(2,1)}, u32[]{:S(2)}, u32[]{:S(2)}) collective-permute-start(s16[4160,128]{1,0:T(8,128)(2,1)} %shard_map.79.refs_0_), channel_id=1, source_target_pairs={{0,16},{8,24},{16,0},{24,8},{1,17},{9,25},{17,1},{25,9},{2,18},{10... | collective-permute-start | bytes 3194888 | tf_op jit(solution)/shard_map/ppermute | solution.py:445
  94.8 4.5 %collective-permute-start.15 = (bf16[1024,512]{1,0:T(8,128)(2,1)}, bf16[1024,512]{1,0:T(8,128)(2,1)S(1)}, u32[]{:S(2)}, u32[]{:S(2)}) collective-permute-start(bf16[1024,512]{1,0:T(8,128)(2,1)} %shard_map.83.refs_0_), channel_id=1, source_target_pairs={{0,8},{8,0},{16,24},{24,16},{1,9},{9,1},{17,25},{25,17},{2,10},{10... | collective-permute-start | bytes 3145736 | tf_op jit(solution)/shard_map/ppermute | solution.py:442
  98.7 3.7 %collective-permute-start.14 = (bf16[1024,512]{1,0:T(8,128)(2,1)S(1)}, bf16[1024,512]{1,0:T(8,128)(2,1)S(1)}, u32[]{:S(2)}, u32[]{:S(2)}) collective-permute-start(bf16[1024,512]{1,0:T(8,128)(2,1)S(1)} %shard_map.86.refs_0_), channel_id=1, source_target_pairs={{0,8},{8,0},{16,24},{24,16},{1,9},{9,1},{17,25},{25,17},{2,10},{10... | collective-permute-start | bytes 3145736 | tf_op jit(solution)/shard_map/ppermute | solution.py:442
  102.4 2.9 %collective-permute-start.17 = (s16[4160,128]{1,0:T(8,128)(2,1)}, s16[4160,128]{1,0:T(8,128)(2,1)S(1)}, u32[]{:S(2)}, u32[]{:S(2)}) collective-permute-start(s16[4160,128]{1,0:T(8,128)(2,1)} %shard_map.89.refs_0_), channel_id=1, source_target_pairs={{0,8},{8,0},{16,24},{24,16},{1,9},{9,1},{17,25},{25,17},{2,10},{10... | collective-permute-start | bytes 3194888 | tf_op jit(solution)/shard_map/ppermute | solution.py:442

commit v6 on v5

--- a/solution.py
+++ b/solution.py
@@ -10,12 +10,12 @@
 
 LANES = 128
 TAIL = 16
-CHUNKS = 2
+CHUNKS = 4
 MORE = 32
 PAD = 160
 LATE_PAD = 48
 FAR_TAILS = 3
-SIDE_TAILS = 16
+SIDE_TAILS = 10
 DONE = jax.ShapeDtypeStruct((8, LANES), jnp.float32)
 INNER = 2
 TOP = 32767.0
@@ -522,18 +522,14 @@
     home_theirs = swap(home_sent[0])
     (home_kept,) = products(kept_by(home), False, [], home_sent[0])
     z_crossed = [to_previous(after(c, home_kept)) for c in crossed_most]
-    z_first, z_second, late, current = split(
-        z_all,
-        (0, half // 2 + MORE),
-        (half // 2, half - half // 2 + MORE),
-        (0, late_part + LATE_PAD),
-        (half, tokens),
-    )
-    z_pieces = [(z_first, half // 2), (z_second, half - half // 2)]
+    z_first, z_second, current = split(
+        z_all, (0, late_part + LATE_PAD), (late_part, half - late_part + MORE), (half, tokens)
+    )
+    z_pieces = [(z_first, late_part), (z_second, half - late_part)]
     codes = [home_theirs, *[got[0, ko] for ko in range(1, outer)], *crossed]
     own = combine(home_kept, codes, current, tails=4)
     others = {ko: to_outer(own, ko) for ko in range(1, outer)}
-    late = [to_ctx(late, kx) for kx in range(1, n_ctx)]
+    late = [to_ctx(z_first, kx) for kx in range(1, n_ctx)]
     pass_on(0, 0, z_pieces)
     result, result_done = decode(
         jnp.stack([me_o * INNER + me_i, me_o * INNER + (me_i + 1) % INNER]),
@@ -556,8 +552,8 @@
     for ko in range(1, outer):
         other = after(others[ko], crossed_done, *late_theirs)
         o = (me_o - ko) % outer
-        place = jnp.stack([o * INNER + me_i, o * INNER + (me_i + 1) % INNER])
-        result, _ = decode(place, [other, swap(other)], n_dp, rows, width, result, passed_done)
+        place = jnp.stack([o * INNER + (me_i + 1) % INNER, o * INNER + me_i])
+        result, _ = decode(place, [swap(other), other], n_dp, rows, width, result, passed_done)
     return passed[None, None], result.reshape(1, n_dp * rows, width)
 
 

time: 110 us -> 110 us (level)
  Pallas kernels: 64.1 us -> 62.9 us
where the time goes in v6:
time: 110 us; the launch traced here: 109 us
  Pallas kernels  62.9 us (57%)
  waiting for transfers between devices  26.8 us (24%)
  starting transfers between devices  15.4 us (14%)
  local copies, waits for them, and re-layouts  1.9 us (2%)
  between operations  1.7 us (2%)
    pallas_call x6, Pallas kernels, token_products(): pl.pallas_call(functools.partial(token_kernel, owners=owners, sizes=sizes...  32.5 us
    ppermute x2, waiting for transfers between devices, to_previous(): return lax.ppermute(value, 'pipe', [(d, d - 1) for d in range(1, n_pipe)])  18.4 us
    pallas_call x4, Pallas kernels, key_products(): pl.pallas_call(functools.partial(key_kernel, segments=[(skip, rows) for _...  10.9 us
    pallas_call x3, Pallas kernels, combine(): pl.pallas_call(functools.partial(combine_kernel, n_codes=len(codes), rows...  7.72 us
    pallas_call x2, Pallas kernels, decode(): pl.pallas_call(functools.partial(decode_kernel, count=count, rows=rows, w...  7.65 us
    ppermute x3, starting transfers between devices, to_ctx(): lax.ppermute(value, 'ctx', [(d, (d + by) % n_ctx) for d in range(n_ctx)])  5.66 us
    ppermute x3, waiting for transfers between devices, to_outer(): lax.ppermute(value, 'dp', [(d, (d + by * INNER) % n_dp) for d in range(n_...  5.64 us
    ppermute x3, starting transfers between devices, to_outer(): lax.ppermute(value, 'dp', [(d, (d + by * INNER) % n_dp) for d in range(n_...  4.67 us
  transfers between devices with their start and end apart: 18, of which 6 were waited for; matrix products, arithmetic and copies ran while one was open for 0% of the time, Pallas kernels for 48%

profile of v6, /device:TPU:0, one launch (start us, length us, event | category | flops | bytes accessed | tf_op | source)
XLA Modules:
  0.0 109.1 jit_solution(8463284211500880828)
XLA Ops:
  1.3 0.1 pad_add_fusion.1.where
  1.4 0.0 copy-start
  1.4 1.2 %copy-done = bf16[1,1,4,272,512]{4,3,2,1,0:T(8,128)(2,1)S(1)} copy-done((bf16[1,1,4,272,512]{4,3,2,1,0:T(8,128)(2,1)S(1)}, bf16[1,1,4,272,512]{4,3,2,1,0:T(8,128)(2,1)}, u32[]{:S(2)}) %copy-start) | copy-done | bytes 1114136
  2.6 0.0 copy-start.1
  2.6 0.7 copy-done.1
  3.3 7.0 %shard_map.68 = (s16[4112,128]{1,0:T(8,128)(2,1)S(1)}, f32[1,1024,512]{2,1,0:T(8,128)S(1)}, bf16[2320,512]{1,0:T(8,128)(2,1)}, bf16[1184,512]{1,0:T(8,128)(2,1)S(1)}) custom-call(s32[3]{0:T(128)S(1)} %pad_add_fusion.1.where, s32[1]{0:T(128)S(6)} %copy.25.slot, s32[8]{0:T(128)S(1)} %copy-done.1, bf16[4,272,8192]{2,1,0:T(8,128)(2,1)} %bitcast.28, ...), custom_call_target="tpu_custom_call" | custom-call | tf_op jit(solution)/shard_map/pallas_call | solution.py:278
  10.2 0.5 collective-permute-start.3
  10.8 1.3 %collective-permute-start = (bf16[2320,512]{1,0:T(8,128)(2,1)}, bf16[2320,512]{1,0:T(8,128)(2,1)S(1)}, u32[]{:S(2)}, u32[]{:S(2)}) collective-permute-start(bf16[2320,512]{1,0:T(8,128)(2,1)} %get-tuple-element.22), channel_id=1, source_target_pairs={{2,0},{4,2},{6,4},{3,1},{5,3},{7,5},{10,8},{12,10},{14,12},{11,9},... | collective-permute-start | bytes 7127048 | tf_op jit(solution)/shard_map/ppermute | solution.py:451
  12.0 2.6 %collective-permute-start.2 = (bf16[1184,512]{1,0:T(8,128)(2,1)S(1)}, bf16[1184,512]{1,0:T(8,128)(2,1)S(1)}, u32[]{:S(2)}, u32[]{:S(2)}) collective-permute-start(bf16[1184,512]{1,0:T(8,128)(2,1)S(1)} %get-tuple-element.25), channel_id=1, source_target_pairs={{0,1},{1,0},{2,3},{3,2},{4,5},{5,4},{6,7},{7,6},{8,9},{9,8},{10,11... | collective-permute-start | bytes 3637256 | tf_op jit(solution)/shard_map/ppermute | solution.py:448
  14.6 0.0 collective-permute-done.3.refs_0_
  14.6 2.0 %shard_map.70.refs_0_ = s16[4144,128]{1,0:T(8,128)(2,1)S(1)} custom-call(f32[1,1024,512]{2,1,0:T(8,128)S(1)} %get-tuple-element.26.kept_ref, s16[4112,128]{1,0:T(8,128)(2,1)S(1)} %collective-permute-done.3.refs_0_), custom_call_target="tpu_custom_call" | custom-call | tf_op jit(solution)/shard_map/pallas_call | solution.py:151
  16.6 1.6 %collective-permute-start.6 = (s16[4144,128]{1,0:T(8,128)(2,1)S(1)}, s16[4144,128]{1,0:T(8,128)(2,1)S(1)}, u32[]{:S(2)}, u32[]{:S(2)}) collective-permute-start(s16[4144,128]{1,0:T(8,128)(2,1)S(1)} %shard_map.70.refs_0_), channel_id=1, source_target_pairs={{0,16},{8,24},{16,0},{24,8},{1,17},{9,25},{17,1},{25,9},{2,18},{10... | collective-permute-start | bytes 3182600 | tf_op jit(solution)/shard_map/ppermute | solution.py:445
  18.2 8.0 %shard_map.71 = (s16[4112,128]{1,0:T(8,128)(2,1)S(1)}, s16[4112,128]{1,0:T(8,128)(2,1)S(1)}) custom-call(s32[3]{0:T(128)S(1)} %pad_add_fusion.1.where, s32[1]{0:T(128)S(6)} %copy.25.slot, s32[8]{0:T(128)S(1)} %copy-done.1, bf16[4,272,8192]{2,1,0:T(8,128)(2,1)} %bitcast.29, bf16[4,272,512]{2,1,0:T(8,128)(2,1)S(1)} %bitcast.23, ...), custom_call_target="tpu_custom_call" | custom-call | tf_op jit(solution)/shard_map/pallas_call | solution.py:278
  26.2 0.1 collective-permute-start.5
  26.2 0.5 collective-permute-start.4
  26.7 2.2 %collective-permute-done.5.refs_0_ = s16[4112,128]{1,0:T(8,128)(2,1)S(1)} collective-permute-done((s16[4112,128]{1,0:T(8,128)(2,1)S(1)}, s16[4112,128]{1,0:T(8,128)(2,1)S(1)}, u32[]{:S(2)}, u32[]{:S(2)}) %collective-permute-start.5) | collective-permute-done | bytes 1052704 | tf_op jit(solution)/shard_map/ppermute | solution.py:442
  28.9 5.3 %shard_map.72.refs_1_.refs_0_ = s16[4160,128]{1,0:T(8,128)(2,1)S(1)} custom-call(s32[3]{0:T(128)S(1)} %pad_add_fusion.1.where, s32[1]{0:T(128)S(6)} %copy.25.slot, s32[8]{0:T(128)S(1)} %copy-done.1, bf16[4,272,8192]{2,1,0:T(8,128)(2,1)} %bitcast.30, bf16[4,272,512]{2,1,0:T(8,128)(2,1)S(1)} %bitcast.24, s16[4112,128]{1,0:T(8,128)(2,1)S(1)} %collective-permute-done.5.refs_0_), custom_call_target="tpu_custom_call" | custom-call | tf_op jit(solution)/shard_map/pallas_call | solution.py:278
  34.2 0.0 collective-permute-done.4.refs_0_
  34.2 3.9 %shard_map.73.kept_ref = f32[1,1024,512]{2,1,0:T(8,128)S(1)} custom-call(s32[3]{0:T(128)S(1)} %pad_add_fusion.1.where, s32[1]{0:T(128)S(6)} %copy.25.slot, s32[8]{0:T(128)S(1)} %copy-done.1, bf16[4,272,8192]{2,1,0:T(8,128)(2,1)} %bitcast.31, bf16[4,272,512]{2,1,0:T(8,128)(2,1)S(1)} %bitcast.25, s16[4112,128]{1,0:T(8,128)(2,1)S(1)} %collective-permute-done.4.refs_0_, ...), custom_call_target="tpu_custom_call" | custom-call | tf_op jit(solution)/shard_map/pallas_call | solution.py:278
  38.1 4.1 %collective-permute-done.6.refs_0_ = s16[4144,128]{1,0:T(8,128)(2,1)S(1)} collective-permute-done((s16[4144,128]{1,0:T(8,128)(2,1)S(1)}, s16[4144,128]{1,0:T(8,128)(2,1)S(1)}, u32[]{:S(2)}, u32[]{:S(2)}) %collective-permute-start.6) | collective-permute-done | bytes 1060896 | tf_op jit(solution)/shard_map/ppermute | solution.py:445
  42.2 2.0 %shard_map.74.refs_0_.refs_1_ = s16[4272,128]{1,0:T(8,128)(2,1)S(1)} custom-call(f32[1,1024,512]{2,1,0:T(8,128)S(1)} %shard_map.73.kept_ref, s16[4144,128]{1,0:T(8,128)(2,1)S(1)} %collective-permute-done.6.refs_0_), custom_call_target="tpu_custom_call" | custom-call | tf_op jit(solution)/shard_map/pallas_call | solution.py:151
  44.2 1.6 %collective-permute-start.9 = (s16[4160,128]{1,0:T(8,128)(2,1)S(1)}, s16[4160,128]{1,0:T(8,128)(2,1)S(1)}, u32[]{:S(2)}, u32[]{:S(2)}) collective-permute-start(s16[4160,128]{1,0:T(8,128)(2,1)S(1)} %shard_map.78), channel_id=1, source_target_pairs={{0,16},{8,24},{16,0},{24,8},{1,17},{9,25},{17,1},{25,9},{2,18},{10... | collective-permute-start | bytes 3194888 | tf_op jit(solution)/shard_map/ppermute | solution.py:445
  45.8 1.2 %collective-permute-start.10 = (s16[4272,128]{1,0:T(8,128)(2,1)S(1)}, s16[4272,128]{1,0:T(8,128)(2,1)S(1)}, u32[]{:S(2)}, u32[]{:S(2)}) collective-permute-start(s16[4272,128]{1,0:T(8,128)(2,1)S(1)} %shard_map.74.refs_0_.refs_1_), channel_id=1, source_target_pairs={{0,1},{1,0},{2,3},{3,2},{4,5},{5,4},{6,7},{7,6},{8,9},{9,8},{10,11... | collective-permute-start | bytes 3280904 | tf_op jit(solution)/shard_map/ppermute | solution.py:448
  47.0 0.0 collective-permute-done.2.refs_1_.refs_0_
  47.0 4.9 %shard_map.75.refs_0_ = s16[4112,128]{1,0:T(8,128)(2,1)S(1)} custom-call(s32[3]{0:T(128)S(1)} %pad_add_fusion.1.where, s32[1]{0:T(128)S(6)} %copy.25.slot, s32[8]{0:T(128)S(1)} %copy-done.1, bf16[4,272,8192]{2,1,0:T(8,128)(2,1)} %bitcast.32, bf16[4,272,512]{2,1,0:T(8,128)(2,1)S(1)} %bitcast.26, s16[4272,128]{1,0:T(8,128)(2,1)S(1)} %shard_map.74.refs_0_.refs_1_, ...), custom_call_target="tpu_custom_call" | custom-call | tf_op jit(solution)/shard_map/pallas_call | solution.py:278
  51.9 0.1 collective-permute-start.8
  51.9 3.5 %shard_map.76.refs_1_.kept_ref = f32[1,1024,512]{2,1,0:T(8,128)S(1)} custom-call(s32[3]{0:T(128)S(1)} %pad_add_fusion.1.where, s32[1]{0:T(128)S(6)} %copy.25.slot, s32[8]{0:T(128)S(1)} %copy-done.1, bf16[4,272,8192]{2,1,0:T(8,128)(2,1)} %bitcast.33, bf16[4,272,512]{2,1,0:T(8,128)(2,1)S(1)} %bitcast.27, s16[4112,128]{1,0:T(8,128)(2,1)S(1)} %shard_map.75.refs_0_), custom_call_target="tpu_custom_call" | custom-call | tf_op jit(solution)/shard_map/pallas_call | solution.py:278
  55.4 1.5 %collective-permute-start.7 = (bf16[1184,512]{1,0:T(8,128)(2,1)S(1)}, bf16[1184,512]{1,0:T(8,128)(2,1)S(1)}, u32[]{:S(2)}, u32[]{:S(2)}) collective-permute-start(bf16[1184,512]{1,0:T(8,128)(2,1)S(1)} %shard_map.77), channel_id=1, source_target_pairs={{2,0},{4,2},{6,4},{3,1},{5,3},{7,5},{10,8},{12,10},{14,12},{11,9},... | collective-permute-start | bytes 3637256 | tf_op jit(solution)/shard_map/ppermute | solution.py:451
  56.9 11.0 %collective-permute-done.value_ref = bf16[2320,512]{1,0:T(8,128)(2,1)S(1)} collective-permute-done((bf16[2320,512]{1,0:T(8,128)(2,1)}, bf16[2320,512]{1,0:T(8,128)(2,1)S(1)}, u32[]{:S(2)}, u32[]{:S(2)}) %collective-permute-start) | collective-permute-done | bytes 2375712 | tf_op jit(solution)/shard_map/ppermute | solution.py:451
  67.9 1.7 %shard_map.69 = (bf16[1072,512]{1,0:T(8,128)(2,1)}, bf16[1056,512]{1,0:T(8,128)(2,1)}, bf16[272,512]{1,0:T(8,128)(2,1)S(1)}) custom-call(bf16[2320,512]{1,0:T(8,128)(2,1)S(1)} %collective-permute-done.value_ref), custom_call_target="tpu_custom_call" | custom-call | tf_op jit(solution)/shard_map/pallas_call | solution.py:80
  69.6 0.1 collective-permute-start.13
  69.7 0.0 collective-permute-done.8.refs_0_
  69.7 0.5 collective-permute-start.12
  70.2 0.0 collective-permute-done.9.refs_1_
  70.2 1.9 %collective-permute-start.1 = (bf16[1072,512]{1,0:T(8,128)(2,1)}, bf16[1072,512]{1,0:T(8,128)(2,1)}, u32[]{:S(2)}, u32[]{:S(2)}) collective-permute-start(bf16[1072,512]{1,0:T(8,128)(2,1)} %get-tuple-element.24.refs_0_), channel_id=1, source_target_pairs={{0,1},{1,0},{2,3},{3,2},{4,5},{5,4},{6,7},{7,6},{8,9},{9,8},{10,11... | collective-permute-start | bytes 3293192 | tf_op jit(solution)/shard_map/ppermute | solution.py:448
  72.0 0.0 collective-permute-done.10.refs_2_
  72.0 3.8 %shard_map.79.refs_0_ = s16[4160,128]{1,0:T(8,128)(2,1)} custom-call(f32[1,1024,512]{2,1,0:T(8,128)S(1)} %shard_map.76.refs_1_.kept_ref, s16[4112,128]{1,0:T(8,128)(2,1)S(1)} %collective-permute-done.8.refs_0_, s16[4160,128]{1,0:T(8,128)(2,1)S(1)} %collective-permute-done.9.refs_1_, s16[4272,128]{1,0:T(8,128)(2,1)S(1)} %collective-permute-done.10.refs_2_, ...), custom_call_target="tpu_custom_call" | custom-call | tf_op jit(solution)/shard_map/pallas_call | solution.py:151
  75.8 0.0 collective-permute-start.11
  75.8 0.1 pad_add_fusion.2.place
  75.9 0.0 collective-permute-done.13.refs_3_
  75.9 1.5 %collective-permute-start.16 = (s16[4160,128]{1,0:T(8,128)(2,1)}, s16[4160,128]{1,0:T(8,128)(2,1)}, u32[]{:S(2)}, u32[]{:S(2)}) collective-permute-start(s16[4160,128]{1,0:T(8,128)(2,1)} %shard_map.79.refs_0_), channel_id=1, source_target_pairs={{0,16},{8,24},{16,0},{24,8},{1,17},{9,25},{17,1},{25,9},{2,18},{10... | collective-permute-start | bytes 3194888 | tf_op jit(solution)/shard_map/ppermute | solution.py:445
  77.4 0.1 pad_add_fusion.3.starts
  77.5 0.0 collective-permute-done.12.refs_1_
  77.5 5.0 %shard_map.80 = (bf16[272,8192]{1,0:T(8,128)(2,1)}, f32[8,128]{1,0:T(8,128)S(1)}) custom-call(s32[4]{0:T(128)S(1)} %pad_add_fusion.3.starts, bf16[272,512]{1,0:T(8,128)(2,1)S(1)} %get-tuple-element.23.refs_3_.current_ref, bf16[1072,512]{1,0:T(8,128)(2,1)} %get-tuple-element.24.refs_0_, bf16[1072,512]{1,0:T(8,128)(2,1)} %collective-permute-done.12.refs_1_, ...), custom_call_target="tpu_custom_call" | custom-call | tf_op jit(solution)/shard_map/pallas_call | solution.py:338
  82.5 0.0 collective-permute-done.11.refs_1_
  82.5 3.8 %shard_map.81 = (f32[4,1024,512]{2,1,0:T(8,128)}, f32[8,128]{1,0:T(8,128)S(1)}) custom-call(s32[2]{0:T(128)S(1)} %pad_add_fusion.2.place, s16[4160,128]{1,0:T(8,128)(2,1)} %shard_map.79.refs_0_, s16[4160,128]{1,0:T(8,128)(2,1)} %collective-permute-done.11.refs_1_, f32[8,128]{1,0:T(8,128)S(1)} %get-tuple-element.31.refs_2_), custom_call_target="tpu_custom_call" | custom-call | tf_op jit(solution)/shard_map/pallas_call | solution.py:408
  86.2 7.4 %collective-permute-done.7.refs_0_ = bf16[1184,512]{1,0:T(8,128)(2,1)S(1)} collective-permute-done((bf16[1184,512]{1,0:T(8,128)(2,1)S(1)}, bf16[1184,512]{1,0:T(8,128)(2,1)S(1)}, u32[]{:S(2)}, u32[]{:S(2)}) %collective-permute-start.7) | collective-permute-done | bytes 1212448 | tf_op jit(solution)/shard_map/ppermute | solution.py:451
  93.7 1.1 shard_map.83.refs_0_
  94.8 0.1 collective-permute-start.15
  94.9 2.5 %shard_map.84 = (bf16[272,8192]{1,0:T(8,128)(2,1)}, f32[8,128]{1,0:T(8,128)S(1)}) custom-call(s32[1]{0:T(128)} %bitcast.9.starts, bf16[272,512]{1,0:T(8,128)(2,1)S(1)} %get-tuple-element.23.refs_3_.current_ref, bf16[1024,512]{1,0:T(8,128)(2,1)} %shard_map.83.refs_0_, bf16[272,8192]{1,0:T(8,128)(2,1)} %get-tuple-element.33.refs_1_), custom_call_target="tpu_custom_call", output_to_operand_aliasing={{0}: (3, {})} | custom-call | tf_op jit(solution)/shard_map/pallas_call | solution.py:338
  97.4 0.0 collective-permute-done.1.refs_0_
  97.4 1.3 %shard_map.86.refs_0_ = bf16[1024,512]{1,0:T(8,128)(2,1)S(1)} custom-call(bf16[1072,512]{1,0:T(8,128)(2,1)} %shard_map.85.value_ref), custom_call_target="tpu_custom_call" | custom-call | tf_op jit(solution)/shard_map/pallas_call | solution.py:80
  98.7 0.6 collective-permute-start.14
  99.3 0.0 collective-permute-done.15.refs_0_
  99.3 1.3 %shard_map.87 = (bf16[272,8192]{1,0:T(8,128)(2,1)}, f32[8,128]{1,0:T(8,128)S(1)}) custom-call(s32[1]{0:T(128)} %bitcast.16.starts, bf16[272,512]{1,0:T(8,128)(2,1)S(1)} %get-tuple-element.23.refs_3_.current_ref, bf16[1024,512]{1,0:T(8,128)(2,1)S(1)} %collective-permute-done.15.refs_0_, ...), custom_call_target="tpu_custom_call", output_to_operand_aliasing={{0}: (3, {})} | custom-call | tf_op jit(solution)/shard_map/pallas_call | solution.py:338
  100.6 1.5 %collective-permute-done.16.refs_0_ = s16[4160,128]{1,0:T(8,128)(2,1)} collective-permute-done((s16[4160,128]{1,0:T(8,128)(2,1)}, s16[4160,128]{1,0:T(8,128)(2,1)}, u32[]{:S(2)}, u32[]{:S(2)}) %collective-permute-start.16) | collective-permute-done | bytes 1064992 | tf_op jit(solution)/shard_map/ppermute | solution.py:445
  102.1 0.0 collective-permute-done.14.refs_1_.refs_2_
  102.2 0.0 collective-permute-start.17
  102.2 0.1 pad_add_fusion.starts
  102.2 0.1 pad_add_fusion.4.place
  102.3 2.2 %shard_map.88 = (bf16[272,8192]{1,0:T(8,128)(2,1)}, f32[8,128]{1,0:T(8,128)S(1)}) custom-call(s32[2]{0:T(128)S(1)} %pad_add_fusion.starts, bf16[272,512]{1,0:T(8,128)(2,1)S(1)} %get-tuple-element.23.refs_3_.current_ref, bf16[1024,512]{1,0:T(8,128)(2,1)S(1)} %shard_map.86.refs_0_, ...), custom_call_target="tpu_custom_call", output_to_operand_aliasing={{0}: (4, {})} | custom-call | tf_op jit(solution)/shard_map/pallas_call | solution.py:338
  104.5 0.6 collective-permute-done.17.refs_0_
  105.0 3.9 %shard_map.90 = (f32[4,1024,512]{2,1,0:T(8,128)}, f32[8,128]{1,0:T(8,128)}) custom-call(s32[2]{0:T(128)S(1)} %pad_add_fusion.4.place, s16[4160,128]{1,0:T(8,128)(2,1)S(1)} %collective-permute-done.17.refs_0_, s16[4160,128]{1,0:T(8,128)(2,1)} %shard_map.89.refs_1_, f32[4,1024,512]{2,1,0:T(8,128)} %get-tuple-element.39.refs_2_, ...), custom_call_target="tpu_custom_call", output_to_operand_aliasing={{0}: (3, {})} | custom-call | tf_op jit(solution)/shard_map/pallas_call | solution.py:408
  (5 shorter events, 0.0 us)
Async XLA Ops:
  1.4 1.2 %copy-start = (bf16[1,1,4,272,512]{4,3,2,1,0:T(8,128)(2,1)S(1)}, bf16[1,1,4,272,512]{4,3,2,1,0:T(8,128)(2,1)}, u32[]{:S(2)}) copy-start(bf16[1,1,4,272,512]{4,3,2,1,0:T(8,128)(2,1)} %param.6) | copy-start | bytes 3342340
  2.6 0.7 copy-start.1
  10.2 4.4 %collective-permute-start.3 = (s16[4112,128]{1,0:T(8,128)(2,1)S(1)}, s16[4112,128]{1,0:T(8,128)(2,1)S(1)}, u32[]{:S(2)}, u32[]{:S(2)}) collective-permute-start(s16[4112,128]{1,0:T(8,128)(2,1)S(1)} %get-tuple-element.27), channel_id=1, source_target_pairs={{0,8},{8,0},{16,24},{24,16},{1,9},{9,1},{17,25},{25,17},{2,10},{10... | collective-permute-start | bytes 3158024 | tf_op jit(solution)/shard_map/ppermute | solution.py:442
  10.8 57.1 %collective-permute-start = (bf16[2320,512]{1,0:T(8,128)(2,1)}, bf16[2320,512]{1,0:T(8,128)(2,1)S(1)}, u32[]{:S(2)}, u32[]{:S(2)}) collective-permute-start(bf16[2320,512]{1,0:T(8,128)(2,1)} %get-tuple-element.22), channel_id=1, source_target_pairs={{2,0},{4,2},{6,4},{3,1},{5,3},{7,5},{10,8},{12,10},{14,12},{11,9},... | collective-permute-start | bytes 7127048 | tf_op jit(solution)/shard_map/ppermute | solution.py:451
  12.0 34.9 %collective-permute-start.2 = (bf16[1184,512]{1,0:T(8,128)(2,1)S(1)}, bf16[1184,512]{1,0:T(8,128)(2,1)S(1)}, u32[]{:S(2)}, u32[]{:S(2)}) collective-permute-start(bf16[1184,512]{1,0:T(8,128)(2,1)S(1)} %get-tuple-element.25), channel_id=1, source_target_pairs={{0,1},{1,0},{2,3},{3,2},{4,5},{5,4},{6,7},{7,6},{8,9},{9,8},{10,11... | collective-permute-start | bytes 3637256 | tf_op jit(solution)/shard_map/ppermute | solution.py:448
  16.6 25.6 %collective-permute-start.6 = (s16[4144,128]{1,0:T(8,128)(2,1)S(1)}, s16[4144,128]{1,0:T(8,128)(2,1)S(1)}, u32[]{:S(2)}, u32[]{:S(2)}) collective-permute-start(s16[4144,128]{1,0:T(8,128)(2,1)S(1)} %shard_map.70.refs_0_), channel_id=1, source_target_pairs={{0,16},{8,24},{16,0},{24,8},{1,17},{9,25},{17,1},{25,9},{2,18},{10... | collective-permute-start | bytes 3182600 | tf_op jit(solution)/shard_map/ppermute | solution.py:445
  26.2 2.7 %collective-permute-start.5 = (s16[4112,128]{1,0:T(8,128)(2,1)S(1)}, s16[4112,128]{1,0:T(8,128)(2,1)S(1)}, u32[]{:S(2)}, u32[]{:S(2)}) collective-permute-start(s16[4112,128]{1,0:T(8,128)(2,1)S(1)} %get-tuple-element.29), channel_id=1, source_target_pairs={{0,8},{8,0},{16,24},{24,16},{1,9},{9,1},{17,25},{25,17},{2,10},{10... | collective-permute-start | bytes 3158024 | tf_op jit(solution)/shard_map/ppermute | solution.py:442
  26.2 7.9 %collective-permute-start.4 = (s16[4112,128]{1,0:T(8,128)(2,1)S(1)}, s16[4112,128]{1,0:T(8,128)(2,1)S(1)}, u32[]{:S(2)}, u32[]{:S(2)}) collective-permute-start(s16[4112,128]{1,0:T(8,128)(2,1)S(1)} %get-tuple-element.28), channel_id=1, source_target_pairs={{0,8},{8,0},{16,24},{24,16},{1,9},{9,1},{17,25},{25,17},{2,10},{10... | collective-permute-start | bytes 3158024 | tf_op jit(solution)/shard_map/ppermute | solution.py:442
  44.2 26.0 %collective-permute-start.9 = (s16[4160,128]{1,0:T(8,128)(2,1)S(1)}, s16[4160,128]{1,0:T(8,128)(2,1)S(1)}, u32[]{:S(2)}, u32[]{:S(2)}) collective-permute-start(s16[4160,128]{1,0:T(8,128)(2,1)S(1)} %shard_map.78), channel_id=1, source_target_pairs={{0,16},{8,24},{16,0},{24,8},{1,17},{9,25},{17,1},{25,9},{2,18},{10... | collective-permute-start | bytes 3194888 | tf_op jit(solution)/shard_map/ppermute | solution.py:445
  45.8 26.3 %collective-permute-start.10 = (s16[4272,128]{1,0:T(8,128)(2,1)S(1)}, s16[4272,128]{1,0:T(8,128)(2,1)S(1)}, u32[]{:S(2)}, u32[]{:S(2)}) collective-permute-start(s16[4272,128]{1,0:T(8,128)(2,1)S(1)} %shard_map.74.refs_0_.refs_1_), channel_id=1, source_target_pairs={{0,1},{1,0},{2,3},{3,2},{4,5},{5,4},{6,7},{7,6},{8,9},{9,8},{10,11... | collective-permute-start | bytes 3280904 | tf_op jit(solution)/shard_map/ppermute | solution.py:448
  51.9 17.8 %collective-permute-start.8 = (s16[4112,128]{1,0:T(8,128)(2,1)S(1)}, s16[4112,128]{1,0:T(8,128)(2,1)S(1)}, u32[]{:S(2)}, u32[]{:S(2)}) collective-permute-start(s16[4112,128]{1,0:T(8,128)(2,1)S(1)} %shard_map.75.refs_0_), channel_id=1, source_target_pairs={{0,8},{8,0},{16,24},{24,16},{1,9},{9,1},{17,25},{25,17},{2,10},{10... | collective-permute-start | bytes 3158024 | tf_op jit(solution)/shard_map/ppermute | solution.py:442
  55.4 38.2 %collective-permute-start.7 = (bf16[1184,512]{1,0:T(8,128)(2,1)S(1)}, bf16[1184,512]{1,0:T(8,128)(2,1)S(1)}, u32[]{:S(2)}, u32[]{:S(2)}) collective-permute-start(bf16[1184,512]{1,0:T(8,128)(2,1)S(1)} %shard_map.77), channel_id=1, source_target_pairs={{2,0},{4,2},{6,4},{3,1},{5,3},{7,5},{10,8},{12,10},{14,12},{11,9},... | collective-permute-start | bytes 3637256 | tf_op jit(solution)/shard_map/ppermute | solution.py:451
  69.6 6.3 %collective-permute-start.13 = (bf16[1056,512]{1,0:T(8,128)(2,1)}, bf16[1056,512]{1,0:T(8,128)(2,1)}, u32[]{:S(2)}, u32[]{:S(2)}) collective-permute-start(bf16[1056,512]{1,0:T(8,128)(2,1)} %get-tuple-element.30.refs_2_), channel_id=1, source_target_pairs={{0,8},{8,0},{16,24},{24,16},{1,9},{9,1},{17,25},{25,17},{2,10},{10... | collective-permute-start | bytes 3244040 | tf_op jit(solution)/shard_map/ppermute | solution.py:442
  69.7 7.8 %collective-permute-start.12 = (bf16[1072,512]{1,0:T(8,128)(2,1)}, bf16[1072,512]{1,0:T(8,128)(2,1)}, u32[]{:S(2)}, u32[]{:S(2)}) collective-permute-start(bf16[1072,512]{1,0:T(8,128)(2,1)} %get-tuple-element.24.refs_0_), channel_id=1, source_target_pairs={{0,8},{8,0},{16,24},{24,16},{1,9},{9,1},{17,25},{25,17},{2,10},{10... | collective-permute-start | bytes 3293192 | tf_op jit(solution)/shard_map/ppermute | solution.py:442
  70.2 27.2 %collective-permute-start.1 = (bf16[1072,512]{1,0:T(8,128)(2,1)}, bf16[1072,512]{1,0:T(8,128)(2,1)}, u32[]{:S(2)}, u32[]{:S(2)}) collective-permute-start(bf16[1072,512]{1,0:T(8,128)(2,1)} %get-tuple-element.24.refs_0_), channel_id=1, source_target_pairs={{0,1},{1,0},{2,3},{3,2},{4,5},{5,4},{6,7},{7,6},{8,9},{9,8},{10,11... | collective-permute-start | bytes 3293192 | tf_op jit(solution)/shard_map/ppermute | solution.py:448
  75.8 6.6 %collective-permute-start.11 = (s16[4160,128]{1,0:T(8,128)(2,1)}, s16[4160,128]{1,0:T(8,128)(2,1)}, u32[]{:S(2)}, u32[]{:S(2)}) collective-permute-start(s16[4160,128]{1,0:T(8,128)(2,1)} %shard_map.79.refs_0_), channel_id=1, source_target_pairs={{0,8},{8,0},{16,24},{24,16},{1,9},{9,1},{17,25},{25,17},{2,10},{10... | collective-permute-start | bytes 3194888 | tf_op jit(solution)/shard_map/ppermute | solution.py:442
  75.9 26.2 %collective-permute-start.16 = (s16[4160,128]{1,0:T(8,128)(2,1)}, s16[4160,128]{1,0:T(8,128)(2,1)}, u32[]{:S(2)}, u32[]{:S(2)}) collective-permute-start(s16[4160,128]{1,0:T(8,128)(2,1)} %shard_map.79.refs_0_), channel_id=1, source_target_pairs={{0,16},{8,24},{16,0},{24,8},{1,17},{9,25},{17,1},{25,9},{2,18},{10... | collective-permute-start | bytes 3194888 | tf_op jit(solution)/shard_map/ppermute | solution.py:445
  94.8 4.5 %collective-permute-start.15 = (bf16[1024,512]{1,0:T(8,128)(2,1)}, bf16[1024,512]{1,0:T(8,128)(2,1)S(1)}, u32[]{:S(2)}, u32[]{:S(2)}) collective-permute-start(bf16[1024,512]{1,0:T(8,128)(2,1)} %shard_map.83.refs_0_), channel_id=1, source_target_pairs={{0,8},{8,0},{16,24},{24,16},{1,9},{9,1},{17,25},{25,17},{2,10},{10... | collective-permute-start | bytes 3145736 | tf_op jit(solution)/shard_map/ppermute | solution.py:442
  98.7 3.4 %collective-permute-start.14 = (bf16[1024,512]{1,0:T(8,128)(2,1)S(1)}, bf16[1024,512]{1,0:T(8,128)(2,1)S(1)}, u32[]{:S(2)}, u32[]{:S(2)}) collective-permute-start(bf16[1024,512]{1,0:T(8,128)(2,1)S(1)} %shard_map.86.refs_0_), channel_id=1, source_target_pairs={{0,8},{8,0},{16,24},{24,16},{1,9},{9,1},{17,25},{25,17},{2,10},{10... | collective-permute-start | bytes 3145736 | tf_op jit(solution)/shard_map/ppermute | solution.py:442
  102.2 2.9 %collective-permute-start.17 = (s16[4160,128]{1,0:T(8,128)(2,1)}, s16[4160,128]{1,0:T(8,128)(2,1)S(1)}, u32[]{:S(2)}, u32[]{:S(2)}) collective-permute-start(s16[4160,128]{1,0:T(8,128)(2,1)} %shard_map.89.refs_1_), channel_id=1, source_target_pairs={{0,8},{8,0},{16,24},{24,16},{1,9},{9,1},{17,25},{25,17},{2,10},{10... | collective-permute-start | bytes 3194888 | tf_op jit(solution)/shard_map/ppermute | solution.py:442

commit v7 on v6

--- a/solution.py
+++ b/solution.py
@@ -12,14 +12,14 @@
 TAIL = 16
 CHUNKS = 4
 MORE = 32
-PAD = 160
+PAD = 144
 LATE_PAD = 48
 FAR_TAILS = 3
 SIDE_TAILS = 10
 DONE = jax.ShapeDtypeStruct((8, LANES), jnp.float32)
 INNER = 2
 TOP = 32767.0
-VMEM_LIMIT = 26 << 20
+VMEM_LIMIT = 18 << 20
 TOKEN_VMEM_LIMIT = 47 << 20
 FIRST_VMEM_LIMIT = 47 << 20
 
@@ -527,7 +527,7 @@
     )
     z_pieces = [(z_first, late_part), (z_second, half - late_part)]
     codes = [home_theirs, *[got[0, ko] for ko in range(1, outer)], *crossed]
-    own = combine(home_kept, codes, current, tails=4)
+    own = combine(home_kept, codes, current, tails=3)
     others = {ko: to_outer(own, ko) for ko in range(1, outer)}
     late = [to_ctx(z_first, kx) for kx in range(1, n_ctx)]
     pass_on(0, 0, z_pieces)

time: 110 us -> 109 us (level)
  no operation moved by 1% of the time
where the time goes in v7:
time: 109 us
  Pallas kernels  62.8 us (58%)
  waiting for transfers between devices  26.7 us (24%)
  starting transfers between devices  15.4 us (14%)
  local copies, waits for them, and re-layouts  1.9 us (2%)
  between operations  1.7 us (2%)
    pallas_call x6, Pallas kernels, token_products(): pl.pallas_call(functools.partial(token_kernel, owners=owners, sizes=sizes...  32.4 us
    ppermute x2, waiting for transfers between devices, to_previous(): return lax.ppermute(value, 'pipe', [(d, d - 1) for d in range(1, n_pipe)])  18.1 us
    pallas_call x4, Pallas kernels, key_products(): pl.pallas_call(functools.partial(key_kernel, segments=[(skip, rows) for _...  10.9 us
    pallas_call x3, Pallas kernels, combine(): pl.pallas_call(functools.partial(combine_kernel, n_codes=len(codes), rows...  7.72 us
    pallas_call x2, Pallas kernels, decode(): pl.pallas_call(functools.partial(decode_kernel, count=count, rows=rows, w...  7.65 us
    ppermute x3, waiting for transfers between devices, to_outer(): lax.ppermute(value, 'dp', [(d, (d + by * INNER) % n_dp) for d in range(n_...  5.9 us
    ppermute x3, starting transfers between devices, to_ctx(): lax.ppermute(value, 'ctx', [(d, (d + by) % n_ctx) for d in range(n_ctx)])  5.66 us
    ppermute x3, starting transfers between devices, to_outer(): lax.ppermute(value, 'dp', [(d, (d + by * INNER) % n_dp) for d in range(n_...  4.67 us
  transfers between devices with their start and end apart: 18, of which 6 were waited for; matrix products, arithmetic and copies ran while one was open for 0% of the time, Pallas kernels for 48%

profile of v7, /device:TPU:0, one launch (start us, length us, event | category | flops | bytes accessed | tf_op | source)
XLA Modules:
  0.0 109.0 jit_solution(18401139897957101836)
XLA Ops:
  1.3 0.1 pad_add_fusion.1.where
  1.4 0.0 copy-start
  1.4 1.2 %copy-done = bf16[1,1,4,272,512]{4,3,2,1,0:T(8,128)(2,1)S(1)} copy-done((bf16[1,1,4,272,512]{4,3,2,1,0:T(8,128)(2,1)S(1)}, bf16[1,1,4,272,512]{4,3,2,1,0:T(8,128)(2,1)}, u32[]{:S(2)}) %copy-start) | copy-done | bytes 1114136
  2.6 0.0 copy-start.1
  2.6 0.7 copy-done.1
  3.3 6.9 %shard_map.68 = (s16[4112,128]{1,0:T(8,128)(2,1)S(1)}, f32[1,1024,512]{2,1,0:T(8,128)S(1)}, bf16[2320,512]{1,0:T(8,128)(2,1)}, bf16[1168,512]{1,0:T(8,128)(2,1)S(1)}) custom-call(s32[3]{0:T(128)S(1)} %pad_add_fusion.1.where, s32[1]{0:T(128)S(6)} %copy.25.slot, s32[8]{0:T(128)S(1)} %copy-done.1, bf16[4,272,8192]{2,1,0:T(8,128)(2,1)} %bitcast.28, ...), custom_call_target="tpu_custom_call" | custom-call | tf_op jit(solution)/shard_map/pallas_call | solution.py:278
  10.2 0.5 collective-permute-start.3
  10.7 1.3 %collective-permute-start = (bf16[2320,512]{1,0:T(8,128)(2,1)}, bf16[2320,512]{1,0:T(8,128)(2,1)S(1)}, u32[]{:S(2)}, u32[]{:S(2)}) collective-permute-start(bf16[2320,512]{1,0:T(8,128)(2,1)} %get-tuple-element.22), channel_id=1, source_target_pairs={{2,0},{4,2},{6,4},{3,1},{5,3},{7,5},{10,8},{12,10},{14,12},{11,9},... | collective-permute-start | bytes 7127048 | tf_op jit(solution)/shard_map/ppermute | solution.py:451
  12.0 2.6 %collective-permute-start.2 = (bf16[1168,512]{1,0:T(8,128)(2,1)S(1)}, bf16[1168,512]{1,0:T(8,128)(2,1)S(1)}, u32[]{:S(2)}, u32[]{:S(2)}) collective-permute-start(bf16[1168,512]{1,0:T(8,128)(2,1)S(1)} %get-tuple-element.25), channel_id=1, source_target_pairs={{0,1},{1,0},{2,3},{3,2},{4,5},{5,4},{6,7},{7,6},{8,9},{9,8},{10,11... | collective-permute-start | bytes 3588104 | tf_op jit(solution)/shard_map/ppermute | solution.py:448
  14.6 0.0 collective-permute-done.3.refs_0_
  14.6 2.0 %shard_map.70.refs_0_ = s16[4144,128]{1,0:T(8,128)(2,1)S(1)} custom-call(f32[1,1024,512]{2,1,0:T(8,128)S(1)} %get-tuple-element.26.kept_ref, s16[4112,128]{1,0:T(8,128)(2,1)S(1)} %collective-permute-done.3.refs_0_), custom_call_target="tpu_custom_call" | custom-call | tf_op jit(solution)/shard_map/pallas_call | solution.py:151
  16.6 1.6 %collective-permute-start.6 = (s16[4144,128]{1,0:T(8,128)(2,1)S(1)}, s16[4144,128]{1,0:T(8,128)(2,1)S(1)}, u32[]{:S(2)}, u32[]{:S(2)}) collective-permute-start(s16[4144,128]{1,0:T(8,128)(2,1)S(1)} %shard_map.70.refs_0_), channel_id=1, source_target_pairs={{0,16},{8,24},{16,0},{24,8},{1,17},{9,25},{17,1},{25,9},{2,18},{10... | collective-permute-start | bytes 3182600 | tf_op jit(solution)/shard_map/ppermute | solution.py:445
  18.2 8.0 %shard_map.71 = (s16[4112,128]{1,0:T(8,128)(2,1)S(1)}, s16[4112,128]{1,0:T(8,128)(2,1)S(1)}) custom-call(s32[3]{0:T(128)S(1)} %pad_add_fusion.1.where, s32[1]{0:T(128)S(6)} %copy.25.slot, s32[8]{0:T(128)S(1)} %copy-done.1, bf16[4,272,8192]{2,1,0:T(8,128)(2,1)} %bitcast.29, bf16[4,272,512]{2,1,0:T(8,128)(2,1)S(1)} %bitcast.23, ...), custom_call_target="tpu_custom_call" | custom-call | tf_op jit(solution)/shard_map/pallas_call | solution.py:278
  26.1 0.1 collective-permute-start.5
  26.2 0.5 collective-permute-start.4
  26.7 2.2 %collective-permute-done.5.refs_0_ = s16[4112,128]{1,0:T(8,128)(2,1)S(1)} collective-permute-done((s16[4112,128]{1,0:T(8,128)(2,1)S(1)}, s16[4112,128]{1,0:T(8,128)(2,1)S(1)}, u32[]{:S(2)}, u32[]{:S(2)}) %collective-permute-start.5) | collective-permute-done | bytes 1052704 | tf_op jit(solution)/shard_map/ppermute | solution.py:442
  28.9 5.3 %shard_map.72.refs_1_.refs_0_ = s16[4160,128]{1,0:T(8,128)(2,1)S(1)} custom-call(s32[3]{0:T(128)S(1)} %pad_add_fusion.1.where, s32[1]{0:T(128)S(6)} %copy.25.slot, s32[8]{0:T(128)S(1)} %copy-done.1, bf16[4,272,8192]{2,1,0:T(8,128)(2,1)} %bitcast.30, bf16[4,272,512]{2,1,0:T(8,128)(2,1)S(1)} %bitcast.24, s16[4112,128]{1,0:T(8,128)(2,1)S(1)} %collective-permute-done.5.refs_0_), custom_call_target="tpu_custom_call" | custom-call | tf_op jit(solution)/shard_map/pallas_call | solution.py:278
  34.1 0.0 collective-permute-done.4.refs_0_
  34.2 3.9 %shard_map.73.kept_ref = f32[1,1024,512]{2,1,0:T(8,128)S(1)} custom-call(s32[3]{0:T(128)S(1)} %pad_add_fusion.1.where, s32[1]{0:T(128)S(6)} %copy.25.slot, s32[8]{0:T(128)S(1)} %copy-done.1, bf16[4,272,8192]{2,1,0:T(8,128)(2,1)} %bitcast.31, bf16[4,272,512]{2,1,0:T(8,128)(2,1)S(1)} %bitcast.25, s16[4112,128]{1,0:T(8,128)(2,1)S(1)} %collective-permute-done.4.refs_0_, ...), custom_call_target="tpu_custom_call" | custom-call | tf_op jit(solution)/shard_map/pallas_call | solution.py:278
  38.1 4.1 %collective-permute-done.6.refs_0_ = s16[4144,128]{1,0:T(8,128)(2,1)S(1)} collective-permute-done((s16[4144,128]{1,0:T(8,128)(2,1)S(1)}, s16[4144,128]{1,0:T(8,128)(2,1)S(1)}, u32[]{:S(2)}, u32[]{:S(2)}) %collective-permute-start.6) | collective-permute-done | bytes 1060896 | tf_op jit(solution)/shard_map/ppermute | solution.py:445
  42.2 2.0 %shard_map.74.refs_0_.refs_1_ = s16[4272,128]{1,0:T(8,128)(2,1)S(1)} custom-call(f32[1,1024,512]{2,1,0:T(8,128)S(1)} %shard_map.73.kept_ref, s16[4144,128]{1,0:T(8,128)(2,1)S(1)} %collective-permute-done.6.refs_0_), custom_call_target="tpu_custom_call" | custom-call | tf_op jit(solution)/shard_map/pallas_call | solution.py:151
  44.2 1.6 %collective-permute-start.9 = (s16[4160,128]{1,0:T(8,128)(2,1)S(1)}, s16[4160,128]{1,0:T(8,128)(2,1)S(1)}, u32[]{:S(2)}, u32[]{:S(2)}) collective-permute-start(s16[4160,128]{1,0:T(8,128)(2,1)S(1)} %shard_map.78), channel_id=1, source_target_pairs={{0,16},{8,24},{16,0},{24,8},{1,17},{9,25},{17,1},{25,9},{2,18},{10... | collective-permute-start | bytes 3194888 | tf_op jit(solution)/shard_map/ppermute | solution.py:445
  45.7 1.2 %collective-permute-start.10 = (s16[4272,128]{1,0:T(8,128)(2,1)S(1)}, s16[4272,128]{1,0:T(8,128)(2,1)S(1)}, u32[]{:S(2)}, u32[]{:S(2)}) collective-permute-start(s16[4272,128]{1,0:T(8,128)(2,1)S(1)} %shard_map.74.refs_0_.refs_1_), channel_id=1, source_target_pairs={{0,1},{1,0},{2,3},{3,2},{4,5},{5,4},{6,7},{7,6},{8,9},{9,8},{10,11... | collective-permute-start | bytes 3280904 | tf_op jit(solution)/shard_map/ppermute | solution.py:448
  47.0 0.0 collective-permute-done.2.refs_1_.refs_0_
  47.0 4.9 %shard_map.75.refs_0_ = s16[4112,128]{1,0:T(8,128)(2,1)S(1)} custom-call(s32[3]{0:T(128)S(1)} %pad_add_fusion.1.where, s32[1]{0:T(128)S(6)} %copy.25.slot, s32[8]{0:T(128)S(1)} %copy-done.1, bf16[4,272,8192]{2,1,0:T(8,128)(2,1)} %bitcast.32, bf16[4,272,512]{2,1,0:T(8,128)(2,1)S(1)} %bitcast.26, s16[4272,128]{1,0:T(8,128)(2,1)S(1)} %shard_map.74.refs_0_.refs_1_, ...), custom_call_target="tpu_custom_call" | custom-call | tf_op jit(solution)/shard_map/pallas_call | solution.py:278
  51.8 0.1 collective-permute-start.8
  51.9 3.5 %shard_map.76.refs_1_.kept_ref = f32[1,1024,512]{2,1,0:T(8,128)S(1)} custom-call(s32[3]{0:T(128)S(1)} %pad_add_fusion.1.where, s32[1]{0:T(128)S(6)} %copy.25.slot, s32[8]{0:T(128)S(1)} %copy-done.1, bf16[4,272,8192]{2,1,0:T(8,128)(2,1)} %bitcast.33, bf16[4,272,512]{2,1,0:T(8,128)(2,1)S(1)} %bitcast.27, s16[4112,128]{1,0:T(8,128)(2,1)S(1)} %shard_map.75.refs_0_), custom_call_target="tpu_custom_call" | custom-call | tf_op jit(solution)/shard_map/pallas_call | solution.py:278
  55.4 1.5 %collective-permute-start.7 = (bf16[1168,512]{1,0:T(8,128)(2,1)S(1)}, bf16[1168,512]{1,0:T(8,128)(2,1)S(1)}, u32[]{:S(2)}, u32[]{:S(2)}) collective-permute-start(bf16[1168,512]{1,0:T(8,128)(2,1)S(1)} %shard_map.77), channel_id=1, source_target_pairs={{2,0},{4,2},{6,4},{3,1},{5,3},{7,5},{10,8},{12,10},{14,12},{11,9},... | collective-permute-start | bytes 3588104 | tf_op jit(solution)/shard_map/ppermute | solution.py:451
  56.9 11.0 %collective-permute-done.value_ref = bf16[2320,512]{1,0:T(8,128)(2,1)S(1)} collective-permute-done((bf16[2320,512]{1,0:T(8,128)(2,1)}, bf16[2320,512]{1,0:T(8,128)(2,1)S(1)}, u32[]{:S(2)}, u32[]{:S(2)}) %collective-permute-start) | collective-permute-done | bytes 2375712 | tf_op jit(solution)/shard_map/ppermute | solution.py:451
  67.9 1.7 %shard_map.69 = (bf16[1072,512]{1,0:T(8,128)(2,1)}, bf16[1056,512]{1,0:T(8,128)(2,1)}, bf16[272,512]{1,0:T(8,128)(2,1)S(1)}) custom-call(bf16[2320,512]{1,0:T(8,128)(2,1)S(1)} %collective-permute-done.value_ref), custom_call_target="tpu_custom_call" | custom-call | tf_op jit(solution)/shard_map/pallas_call | solution.py:80
  69.6 0.1 collective-permute-start.13
  69.6 0.0 collective-permute-done.8.refs_0_
  69.7 0.5 collective-permute-start.12
  70.1 0.0 collective-permute-done.9.refs_1_
  70.1 1.9 %collective-permute-start.1 = (bf16[1072,512]{1,0:T(8,128)(2,1)}, bf16[1072,512]{1,0:T(8,128)(2,1)}, u32[]{:S(2)}, u32[]{:S(2)}) collective-permute-start(bf16[1072,512]{1,0:T(8,128)(2,1)} %get-tuple-element.24.refs_0_), channel_id=1, source_target_pairs={{0,1},{1,0},{2,3},{3,2},{4,5},{5,4},{6,7},{7,6},{8,9},{9,8},{10,11... | collective-permute-start | bytes 3293192 | tf_op jit(solution)/shard_map/ppermute | solution.py:448
  72.0 0.0 collective-permute-done.10.refs_2_
  72.0 3.8 %shard_map.79.refs_0_ = s16[4144,128]{1,0:T(8,128)(2,1)} custom-call(f32[1,1024,512]{2,1,0:T(8,128)S(1)} %shard_map.76.refs_1_.kept_ref, s16[4112,128]{1,0:T(8,128)(2,1)S(1)} %collective-permute-done.8.refs_0_, s16[4160,128]{1,0:T(8,128)(2,1)S(1)} %collective-permute-done.9.refs_1_, s16[4272,128]{1,0:T(8,128)(2,1)S(1)} %collective-permute-done.10.refs_2_, ...), custom_call_target="tpu_custom_call" | custom-call | tf_op jit(solution)/shard_map/pallas_call | solution.py:151
  75.8 0.0 collective-permute-start.11
  75.8 0.1 pad_add_fusion.2.place
  75.9 0.0 collective-permute-done.13.refs_3_
  75.9 1.5 %collective-permute-start.16 = (s16[4144,128]{1,0:T(8,128)(2,1)}, s16[4144,128]{1,0:T(8,128)(2,1)}, u32[]{:S(2)}, u32[]{:S(2)}) collective-permute-start(s16[4144,128]{1,0:T(8,128)(2,1)} %shard_map.79.refs_0_), channel_id=1, source_target_pairs={{0,16},{8,24},{16,0},{24,8},{1,17},{9,25},{17,1},{25,9},{2,18},{10... | collective-permute-start | bytes 3182600 | tf_op jit(solution)/shard_map/ppermute | solution.py:445
  77.4 0.1 pad_add_fusion.3.starts
  77.5 0.0 collective-permute-done.12.refs_1_
  77.5 5.0 %shard_map.80 = (bf16[272,8192]{1,0:T(8,128)(2,1)}, f32[8,128]{1,0:T(8,128)S(1)}) custom-call(s32[4]{0:T(128)S(1)} %pad_add_fusion.3.starts, bf16[272,512]{1,0:T(8,128)(2,1)S(1)} %get-tuple-element.23.refs_3_.current_ref, bf16[1072,512]{1,0:T(8,128)(2,1)} %get-tuple-element.24.refs_0_, bf16[1072,512]{1,0:T(8,128)(2,1)} %collective-permute-done.12.refs_1_, ...), custom_call_target="tpu_custom_call" | custom-call | tf_op jit(solution)/shard_map/pallas_call | solution.py:338
  82.4 0.0 collective-permute-done.11.refs_1_
  82.5 3.8 %shard_map.81 = (f32[4,1024,512]{2,1,0:T(8,128)}, f32[8,128]{1,0:T(8,128)S(1)}) custom-call(s32[2]{0:T(128)S(1)} %pad_add_fusion.2.place, s16[4144,128]{1,0:T(8,128)(2,1)} %shard_map.79.refs_0_, s16[4144,128]{1,0:T(8,128)(2,1)} %collective-permute-done.11.refs_1_, f32[8,128]{1,0:T(8,128)S(1)} %get-tuple-element.31.refs_2_), custom_call_target="tpu_custom_call" | custom-call | tf_op jit(solution)/shard_map/pallas_call | solution.py:408
  86.2 7.1 %collective-permute-done.7.refs_0_ = bf16[1168,512]{1,0:T(8,128)(2,1)S(1)} collective-permute-done((bf16[1168,512]{1,0:T(8,128)(2,1)S(1)}, bf16[1168,512]{1,0:T(8,128)(2,1)S(1)}, u32[]{:S(2)}, u32[]{:S(2)}) %collective-permute-start.7) | collective-permute-done | bytes 1196064 | tf_op jit(solution)/shard_map/ppermute | solution.py:451
  93.3 1.1 shard_map.83.refs_0_
  94.4 0.1 collective-permute-start.15
  94.5 2.5 %shard_map.84 = (bf16[272,8192]{1,0:T(8,128)(2,1)}, f32[8,128]{1,0:T(8,128)S(1)}) custom-call(s32[1]{0:T(128)} %bitcast.9.starts, bf16[272,512]{1,0:T(8,128)(2,1)S(1)} %get-tuple-element.23.refs_3_.current_ref, bf16[1024,512]{1,0:T(8,128)(2,1)} %shard_map.83.refs_0_, bf16[272,8192]{1,0:T(8,128)(2,1)} %get-tuple-element.33.refs_1_), custom_call_target="tpu_custom_call", output_to_operand_aliasing={{0}: (3, {})} | custom-call | tf_op jit(solution)/shard_map/pallas_call | solution.py:338
  97.0 0.0 collective-permute-done.1.refs_0_
  97.0 1.3 %shard_map.86.refs_0_ = bf16[1024,512]{1,0:T(8,128)(2,1)S(1)} custom-call(bf16[1072,512]{1,0:T(8,128)(2,1)} %shard_map.85.value_ref), custom_call_target="tpu_custom_call" | custom-call | tf_op jit(solution)/shard_map/pallas_call | solution.py:80
  98.4 0.6 collective-permute-start.14
  98.9 0.0 collective-permute-done.15.refs_0_
  98.9 1.3 %shard_map.87 = (bf16[272,8192]{1,0:T(8,128)(2,1)}, f32[8,128]{1,0:T(8,128)S(1)}) custom-call(s32[1]{0:T(128)} %bitcast.16.starts, bf16[272,512]{1,0:T(8,128)(2,1)S(1)} %get-tuple-element.23.refs_3_.current_ref, bf16[1024,512]{1,0:T(8,128)(2,1)S(1)} %collective-permute-done.15.refs_0_, ...), custom_call_target="tpu_custom_call", output_to_operand_aliasing={{0}: (3, {})} | custom-call | tf_op jit(solution)/shard_map/pallas_call | solution.py:338
  100.2 1.8 %collective-permute-done.16.refs_0_ = s16[4144,128]{1,0:T(8,128)(2,1)} collective-permute-done((s16[4144,128]{1,0:T(8,128)(2,1)}, s16[4144,128]{1,0:T(8,128)(2,1)}, u32[]{:S(2)}, u32[]{:S(2)}) %collective-permute-start.16) | collective-permute-done | bytes 1060896 | tf_op jit(solution)/shard_map/ppermute | solution.py:445
  102.0 0.0 collective-permute-done.14.refs_1_.refs_2_
  102.0 0.0 collective-permute-start.17
  102.0 0.1 pad_add_fusion.starts
  102.1 0.1 pad_add_fusion.4.place
  102.2 2.2 %shard_map.88 = (bf16[272,8192]{1,0:T(8,128)(2,1)}, f32[8,128]{1,0:T(8,128)S(1)}) custom-call(s32[2]{0:T(128)S(1)} %pad_add_fusion.starts, bf16[272,512]{1,0:T(8,128)(2,1)S(1)} %get-tuple-element.23.refs_3_.current_ref, bf16[1024,512]{1,0:T(8,128)(2,1)S(1)} %shard_map.86.refs_0_, ...), custom_call_target="tpu_custom_call", output_to_operand_aliasing={{0}: (4, {})} | custom-call | tf_op jit(solution)/shard_map/pallas_call | solution.py:338
  104.4 0.6 collective-permute-done.17.refs_0_
  104.9 3.9 %shard_map.90 = (f32[4,1024,512]{2,1,0:T(8,128)}, f32[8,128]{1,0:T(8,128)}) custom-call(s32[2]{0:T(128)S(1)} %pad_add_fusion.4.place, s16[4144,128]{1,0:T(8,128)(2,1)S(1)} %collective-permute-done.17.refs_0_, s16[4144,128]{1,0:T(8,128)(2,1)} %shard_map.89.refs_1_, f32[4,1024,512]{2,1,0:T(8,128)} %get-tuple-element.39.refs_2_, ...), custom_call_target="tpu_custom_call", output_to_operand_aliasing={{0}: (3, {})} | custom-call | tf_op jit(solution)/shard_map/pallas_call | solution.py:408
  (5 shorter events, 0.0 us)
Async XLA Ops:
  1.4 1.2 %copy-start = (bf16[1,1,4,272,512]{4,3,2,1,0:T(8,128)(2,1)S(1)}, bf16[1,1,4,272,512]{4,3,2,1,0:T(8,128)(2,1)}, u32[]{:S(2)}) copy-start(bf16[1,1,4,272,512]{4,3,2,1,0:T(8,128)(2,1)} %param.6) | copy-start | bytes 3342340
  2.6 0.7 copy-start.1
  10.2 4.4 %collective-permute-start.3 = (s16[4112,128]{1,0:T(8,128)(2,1)S(1)}, s16[4112,128]{1,0:T(8,128)(2,1)S(1)}, u32[]{:S(2)}, u32[]{:S(2)}) collective-permute-start(s16[4112,128]{1,0:T(8,128)(2,1)S(1)} %get-tuple-element.27), channel_id=1, source_target_pairs={{0,8},{8,0},{16,24},{24,16},{1,9},{9,1},{17,25},{25,17},{2,10},{10... | collective-permute-start | bytes 3158024 | tf_op jit(solution)/shard_map/ppermute | solution.py:442
  10.7 57.1 %collective-permute-start = (bf16[2320,512]{1,0:T(8,128)(2,1)}, bf16[2320,512]{1,0:T(8,128)(2,1)S(1)}, u32[]{:S(2)}, u32[]{:S(2)}) collective-permute-start(bf16[2320,512]{1,0:T(8,128)(2,1)} %get-tuple-element.22), channel_id=1, source_target_pairs={{2,0},{4,2},{6,4},{3,1},{5,3},{7,5},{10,8},{12,10},{14,12},{11,9},... | collective-permute-start | bytes 7127048 | tf_op jit(solution)/shard_map/ppermute | solution.py:451
  12.0 34.9 %collective-permute-start.2 = (bf16[1168,512]{1,0:T(8,128)(2,1)S(1)}, bf16[1168,512]{1,0:T(8,128)(2,1)S(1)}, u32[]{:S(2)}, u32[]{:S(2)}) collective-permute-start(bf16[1168,512]{1,0:T(8,128)(2,1)S(1)} %get-tuple-element.25), channel_id=1, source_target_pairs={{0,1},{1,0},{2,3},{3,2},{4,5},{5,4},{6,7},{7,6},{8,9},{9,8},{10,11... | collective-permute-start | bytes 3588104 | tf_op jit(solution)/shard_map/ppermute | solution.py:448
  16.6 25.6 %collective-permute-start.6 = (s16[4144,128]{1,0:T(8,128)(2,1)S(1)}, s16[4144,128]{1,0:T(8,128)(2,1)S(1)}, u32[]{:S(2)}, u32[]{:S(2)}) collective-permute-start(s16[4144,128]{1,0:T(8,128)(2,1)S(1)} %shard_map.70.refs_0_), channel_id=1, source_target_pairs={{0,16},{8,24},{16,0},{24,8},{1,17},{9,25},{17,1},{25,9},{2,18},{10... | collective-permute-start | bytes 3182600 | tf_op jit(solution)/shard_map/ppermute | solution.py:445
  26.1 2.7 %collective-permute-start.5 = (s16[4112,128]{1,0:T(8,128)(2,1)S(1)}, s16[4112,128]{1,0:T(8,128)(2,1)S(1)}, u32[]{:S(2)}, u32[]{:S(2)}) collective-permute-start(s16[4112,128]{1,0:T(8,128)(2,1)S(1)} %get-tuple-element.29), channel_id=1, source_target_pairs={{0,8},{8,0},{16,24},{24,16},{1,9},{9,1},{17,25},{25,17},{2,10},{10... | collective-permute-start | bytes 3158024 | tf_op jit(solution)/shard_map/ppermute | solution.py:442
  26.2 7.9 %collective-permute-start.4 = (s16[4112,128]{1,0:T(8,128)(2,1)S(1)}, s16[4112,128]{1,0:T(8,128)(2,1)S(1)}, u32[]{:S(2)}, u32[]{:S(2)}) collective-permute-start(s16[4112,128]{1,0:T(8,128)(2,1)S(1)} %get-tuple-element.28), channel_id=1, source_target_pairs={{0,8},{8,0},{16,24},{24,16},{1,9},{9,1},{17,25},{25,17},{2,10},{10... | collective-permute-start | bytes 3158024 | tf_op jit(solution)/shard_map/ppermute | solution.py:442
  44.2 26.0 %collective-permute-start.9 = (s16[4160,128]{1,0:T(8,128)(2,1)S(1)}, s16[4160,128]{1,0:T(8,128)(2,1)S(1)}, u32[]{:S(2)}, u32[]{:S(2)}) collective-permute-start(s16[4160,128]{1,0:T(8,128)(2,1)S(1)} %shard_map.78), channel_id=1, source_target_pairs={{0,16},{8,24},{16,0},{24,8},{1,17},{9,25},{17,1},{25,9},{2,18},{10... | collective-permute-start | bytes 3194888 | tf_op jit(solution)/shard_map/ppermute | solution.py:445
  45.7 26.3 %collective-permute-start.10 = (s16[4272,128]{1,0:T(8,128)(2,1)S(1)}, s16[4272,128]{1,0:T(8,128)(2,1)S(1)}, u32[]{:S(2)}, u32[]{:S(2)}) collective-permute-start(s16[4272,128]{1,0:T(8,128)(2,1)S(1)} %shard_map.74.refs_0_.refs_1_), channel_id=1, source_target_pairs={{0,1},{1,0},{2,3},{3,2},{4,5},{5,4},{6,7},{7,6},{8,9},{9,8},{10,11... | collective-permute-start | bytes 3280904 | tf_op jit(solution)/shard_map/ppermute | solution.py:448
  51.8 17.8 %collective-permute-start.8 = (s16[4112,128]{1,0:T(8,128)(2,1)S(1)}, s16[4112,128]{1,0:T(8,128)(2,1)S(1)}, u32[]{:S(2)}, u32[]{:S(2)}) collective-permute-start(s16[4112,128]{1,0:T(8,128)(2,1)S(1)} %shard_map.75.refs_0_), channel_id=1, source_target_pairs={{0,8},{8,0},{16,24},{24,16},{1,9},{9,1},{17,25},{25,17},{2,10},{10... | collective-permute-start | bytes 3158024 | tf_op jit(solution)/shard_map/ppermute | solution.py:442
  55.4 37.9 %collective-permute-start.7 = (bf16[1168,512]{1,0:T(8,128)(2,1)S(1)}, bf16[1168,512]{1,0:T(8,128)(2,1)S(1)}, u32[]{:S(2)}, u32[]{:S(2)}) collective-permute-start(bf16[1168,512]{1,0:T(8,128)(2,1)S(1)} %shard_map.77), channel_id=1, source_target_pairs={{2,0},{4,2},{6,4},{3,1},{5,3},{7,5},{10,8},{12,10},{14,12},{11,9},... | collective-permute-start | bytes 3588104 | tf_op jit(solution)/shard_map/ppermute | solution.py:451
  69.6 6.3 %collective-permute-start.13 = (bf16[1056,512]{1,0:T(8,128)(2,1)}, bf16[1056,512]{1,0:T(8,128)(2,1)}, u32[]{:S(2)}, u32[]{:S(2)}) collective-permute-start(bf16[1056,512]{1,0:T(8,128)(2,1)} %get-tuple-element.30.refs_2_), channel_id=1, source_target_pairs={{0,8},{8,0},{16,24},{24,16},{1,9},{9,1},{17,25},{25,17},{2,10},{10... | collective-permute-start | bytes 3244040 | tf_op jit(solution)/shard_map/ppermute | solution.py:442
  69.7 7.8 %collective-permute-start.12 = (bf16[1072,512]{1,0:T(8,128)(2,1)}, bf16[1072,512]{1,0:T(8,128)(2,1)}, u32[]{:S(2)}, u32[]{:S(2)}) collective-permute-start(bf16[1072,512]{1,0:T(8,128)(2,1)} %get-tuple-element.24.refs_0_), channel_id=1, source_target_pairs={{0,8},{8,0},{16,24},{24,16},{1,9},{9,1},{17,25},{25,17},{2,10},{10... | collective-permute-start | bytes 3293192 | tf_op jit(solution)/shard_map/ppermute | solution.py:442
  70.1 26.9 %collective-permute-start.1 = (bf16[1072,512]{1,0:T(8,128)(2,1)}, bf16[1072,512]{1,0:T(8,128)(2,1)}, u32[]{:S(2)}, u32[]{:S(2)}) collective-permute-start(bf16[1072,512]{1,0:T(8,128)(2,1)} %get-tuple-element.24.refs_0_), channel_id=1, source_target_pairs={{0,1},{1,0},{2,3},{3,2},{4,5},{5,4},{6,7},{7,6},{8,9},{9,8},{10,11... | collective-permute-start | bytes 3293192 | tf_op jit(solution)/shard_map/ppermute | solution.py:448
  75.8 6.6 %collective-permute-start.11 = (s16[4144,128]{1,0:T(8,128)(2,1)}, s16[4144,128]{1,0:T(8,128)(2,1)}, u32[]{:S(2)}, u32[]{:S(2)}) collective-permute-start(s16[4144,128]{1,0:T(8,128)(2,1)} %shard_map.79.refs_0_), channel_id=1, source_target_pairs={{0,8},{8,0},{16,24},{24,16},{1,9},{9,1},{17,25},{25,17},{2,10},{10... | collective-permute-start | bytes 3182600 | tf_op jit(solution)/shard_map/ppermute | solution.py:442
  75.9 26.2 %collective-permute-start.16 = (s16[4144,128]{1,0:T(8,128)(2,1)}, s16[4144,128]{1,0:T(8,128)(2,1)}, u32[]{:S(2)}, u32[]{:S(2)}) collective-permute-start(s16[4144,128]{1,0:T(8,128)(2,1)} %shard_map.79.refs_0_), channel_id=1, source_target_pairs={{0,16},{8,24},{16,0},{24,8},{1,17},{9,25},{17,1},{25,9},{2,18},{10... | collective-permute-start | bytes 3182600 | tf_op jit(solution)/shard_map/ppermute | solution.py:445
  94.4 4.5 %collective-permute-start.15 = (bf16[1024,512]{1,0:T(8,128)(2,1)}, bf16[1024,512]{1,0:T(8,128)(2,1)S(1)}, u32[]{:S(2)}, u32[]{:S(2)}) collective-permute-start(bf16[1024,512]{1,0:T(8,128)(2,1)} %shard_map.83.refs_0_), channel_id=1, source_target_pairs={{0,8},{8,0},{16,24},{24,16},{1,9},{9,1},{17,25},{25,17},{2,10},{10... | collective-permute-start | bytes 3145736 | tf_op jit(solution)/shard_map/ppermute | solution.py:442
  98.4 3.7 %collective-permute-start.14 = (bf16[1024,512]{1,0:T(8,128)(2,1)S(1)}, bf16[1024,512]{1,0:T(8,128)(2,1)S(1)}, u32[]{:S(2)}, u32[]{:S(2)}) collective-permute-start(bf16[1024,512]{1,0:T(8,128)(2,1)S(1)} %shard_map.86.refs_0_), channel_id=1, source_target_pairs={{0,8},{8,0},{16,24},{24,16},{1,9},{9,1},{17,25},{25,17},{2,10},{10... | collective-permute-start | bytes 3145736 | tf_op jit(solution)/shard_map/ppermute | solution.py:442
  102.0 2.9 %collective-permute-start.17 = (s16[4144,128]{1,0:T(8,128)(2,1)}, s16[4144,128]{1,0:T(8,128)(2,1)S(1)}, u32[]{:S(2)}, u32[]{:S(2)}) collective-permute-start(s16[4144,128]{1,0:T(8,128)(2,1)} %shard_map.89.refs_1_), channel_id=1, source_target_pairs={{0,8},{8,0},{16,24},{24,16},{1,9},{9,1},{17,25},{25,17},{2,10},{10... | collective-permute-start | bytes 3182600 | tf_op jit(solution)/shard_map/ppermute | solution.py:442
